TPU v7x, 512 devices: a whole 4x4x16 slice. The times are simulated.
512 devices in a mesh: queue: 32 (over z_hi, x, core), sp: 16 (over z_lo, y).
Axes of the slice: x: 4, y: 4, z: 16 (z_hi: 4, z_lo: 4; z = z_hi * 4 + z_lo), core: 2. Of those that a mesh axis runs over, the one named last changes fastest.
Arguments:
- spatial_qkv: bfloat16 [64, 3, 2048, 1152], P('queue', None, 'sp'), may hold values from -8 to 8
- temporal_query: bfloat16 [64, 2048, 1152], P('queue', 'sp'), may hold values from -8 to 8
- temporal_kv: bfloat16 [64, 2, 2048, 1152], P('queue', None, 'sp'), may hold values from -8 to 8
- timestep: int32 [64], P('queue'), may hold values from 0 to 29
- noise_level: int32 [64], P('queue'), may hold values from 0 to 63
- spatial_gate: float32 [30, 1152], replicated, may hold values from 1 to 10
- temporal_gate: float32 [30, 1152], replicated, may hold values from 0.1 to 1
- step_table: float32 [64], replicated, may hold values from 0.5 to 2
Outputs:
- advanced: bfloat16 [64, 2048, 1152], P('queue', 'sp')
All inputs are finite; a program needn't handle non-finite values.
Results may differ from a plain program's by a relative error of at most 0.0055.
Values may be sent and summed in bfloat16 or wider, within the bound.
No kernel may reach another device: no remote copies, remote signals or barrier semaphores. Data moves between devices by JAX's collectives and lax.ppermute only.
A program may use at most 64 MiB of HBM per device.

v0:
```python
import math

import jax
import jax.numpy as jnp
from jax import lax
from jax.sharding import PartitionSpec as P

HEAD_DIM = 72
PLEN = 16
NSTEPS = 30
LEVELS = 64


def from_behind(block, axis, distance):
    devices = range(lax.axis_size(axis))
    route = [((i - distance) % len(devices), i) for i in devices]
    return lax.ppermute(block, axis, route)


def spatial_core(packed, head_dim):
    item_total, _, length, width_all = packed.shape
    head_count = width_all // head_dim
    queries = packed[:, 0].reshape(item_total, length, head_count, head_dim)
    key_rows = packed[:, 1].reshape(item_total, length, head_count, head_dim)
    values = packed[:, 2].reshape(item_total, length, head_count, head_dim)
    block_rows = min(512, length)
    score_scale = 1.0 / math.sqrt(head_dim)

    def one_block(block_index):
        query_rows = lax.dynamic_slice_in_dim(queries, block_index * block_rows, block_rows, 1)
        scores = (
            jnp.einsum("nqhe,nkhe->nhqk", query_rows, key_rows, preferred_element_type=jnp.float32)
            * score_scale
        )
        row_max = jnp.max(scores, axis=-1, keepdims=True)
        weights = jnp.exp(scores - row_max)
        row_sum = jnp.sum(weights, axis=-1)
        weighted = jnp.einsum(
            "nhqk,nkhe->nqhe",
            weights.astype(jnp.bfloat16),
            values,
            preferred_element_type=jnp.float32,
        )
        return (weighted / jnp.swapaxes(row_sum, 1, 2)[..., None]).astype(jnp.bfloat16)

    outputs = lax.map(one_block, jnp.arange(length // block_rows, dtype=jnp.int32))
    return jnp.moveaxis(outputs, 0, 1).reshape(item_total, length, width_all)


def temporal_core(query_all, kv_all, head_dim):
    frame_total, _, length, width_all = kv_all.shape
    head_count = width_all // head_dim
    part_count = frame_total // PLEN
    score_scale = 1.0 / math.sqrt(head_dim)
    query_heads = query_all[:, 0].reshape(part_count, PLEN, length, head_count, head_dim)
    key_heads = kv_all[:, 0].reshape(part_count, PLEN, length, head_count, head_dim)
    value_heads = kv_all[:, 1].reshape(part_count, PLEN, length, head_count, head_dim)
    scores = (
        jnp.einsum("pflhe,pglhe->plhfg", query_heads, key_heads, preferred_element_type=jnp.float32)
        * score_scale
    )
    row_max = jnp.max(scores, axis=-1, keepdims=True)
    weights = jnp.exp(scores - row_max)
    row_sum = jnp.sum(weights, axis=-1)
    weighted = jnp.einsum(
        "plhfg,pglhe->pflhe",
        weights.astype(jnp.bfloat16),
        value_heads,
        preferred_element_type=jnp.float32,
    )
    divided = weighted / jnp.transpose(row_sum, (0, 3, 1, 2))[..., None]
    return divided.astype(jnp.bfloat16).reshape(frame_total, length, width_all)


def temporal_queue(query_in, kv_in, head_dim):
    query_all, kv_all = (
        lax.all_to_all(query_in, "queue", split_axis=2, concat_axis=0, tiled=True),
        lax.all_to_all(kv_in, "queue", split_axis=2, concat_axis=0, tiled=True),
    )
    result = temporal_core(query_all, kv_all, head_dim)
    return lax.all_to_all(result, "queue", split_axis=0, concat_axis=1, tiled=True)


def combine(space_out, timely, gate_s, gate_t, step_sizes):
    space_wide = lax.optimization_barrier(space_out).astype(jnp.float32)
    timely_wide = lax.optimization_barrier(timely).astype(jnp.float32)
    mixed_sum = gate_s[:, None, :] * space_wide + gate_t[:, None, :] * timely_wide
    return (step_sizes[:, None, None] * mixed_sum).astype(jnp.bfloat16)


def to_tokens(head_layout):
    return lax.all_to_all(head_layout, "sp", split_axis=1, concat_axis=2, tiled=True)


def spatial_tokens(packed):
    return to_tokens(spatial_core(packed, HEAD_DIM))


def move_queue(first_frame):
    return from_behind(first_frame, "queue", -1)


def per_device(
    spatial_qkv,
    temporal_query,
    temporal_kv,
    timestep,
    noise_level,
    spatial_gate,
    temporal_gate,
    step_table,
):
    step_hot = (timestep[:, None] == jnp.arange(NSTEPS, dtype=jnp.int32)[None, :]).astype(
        jnp.float32
    )
    gate_space = jnp.dot(step_hot, spatial_gate, precision=lax.Precision.HIGHEST)
    gate_time = jnp.dot(step_hot, temporal_gate, precision=lax.Precision.HIGHEST)
    level_hot = noise_level[:, None] == jnp.arange(LEVELS, dtype=jnp.int32)[None, :]
    step_size = jnp.sum(jnp.where(level_hot, step_table[None, :], 0.0), axis=1)
    timely = temporal_queue(temporal_query[:, None], temporal_kv, HEAD_DIM)
    space_out = spatial_tokens(
        lax.all_to_all(spatial_qkv, "sp", split_axis=3, concat_axis=2, tiled=True)
    )
    updated = combine(space_out, timely, gate_space, gate_time, step_size)
    return jnp.concatenate([updated[1:], move_queue(updated[:1])], axis=0)


def solution(mesh):
    return jax.shard_map(
        per_device,
        mesh=mesh,
        in_specs=(
            P("queue", None, "sp", None),
            P("queue", "sp", None),
            P("queue", None, "sp", None),
            P("queue"),
            P("queue"),
            P(),
            P(),
            P(),
        ),
        out_specs=P("queue", "sp", None),
        check_vma=False,
    )
```

profile of v0, /device:TPU:23, one launch (start us, length us, event | category | flops | bytes accessed | tf_op | source)
XLA Modules:
  0.0 262.2 jit_solution(1115291674917914005)
XLA Ops:
  0.0 2.6 copy.136
  2.6 18.5 %all-to-all-start.2 = ((bf16[2,1,128,1152]{3,0,1,2:T(2,128)(2,1)}), bf16[2,1,128,1152]{3,0,1,2:T(2,128)(2,1)S(1)}, u32[]{:S(2)}, u32[]{:S(2)}) async-start(bf16[2,1,128,1152]{3,0,1,2:T(2,128)(2,1)} %bitcast.77), calls=%async_computation.2 | async-start | bytes 1179648 | tf_op jit(solution)/shard_map/all_to_all | solution.py:77
  21.1 2.2 copy.96
  23.4 27.4 %all-to-all-done.2 = bf16[2,1,128,1152]{3,0,1,2:T(2,128)(2,1)S(1)} async-done(((bf16[2,1,128,1152]{3,0,1,2:T(2,128)(2,1)}), bf16[2,1,128,1152]{3,0,1,2:T(2,128)(2,1)S(1)}, u32[]{:S(2)}, u32[]{:S(2)}) %all-to-all-start.2) | async-done | bytes 589856 | tf_op jit(solution)/shard_map/all_to_all | solution.py:77
  50.7 11.4 %all-to-all-start.3 = ((bf16[2,2,128,1152]{3,1,0,2:T(2,128)(2,1)}), bf16[2,2,128,1152]{3,1,0,2:T(2,128)(2,1)S(1)}, u32[]{:S(2)}, u32[]{:S(2)}) async-start(bf16[2,2,128,1152]{3,1,0,2:T(2,128)(2,1)} %copy.96), calls=%async_computation.3 | async-start | bytes 2359296 | tf_op jit(solution)/shard_map/all_to_all | solution.py:78
  62.1 6.5 %copy.87 = bf16[2,3,128,1152]{2,0,1,3:T(2,128)(2,1)} copy(bf16[2,3,128,1152]{3,2,1,0:T(8,128)(2,1)} %param.10) | data formatting | bytes 3538944 | tf_op args[0]
  68.7 48.1 %all-to-all-done.3 = bf16[2,2,128,1152]{3,1,0,2:T(2,128)(2,1)S(1)} async-done(((bf16[2,2,128,1152]{3,1,0,2:T(2,128)(2,1)}), bf16[2,2,128,1152]{3,1,0,2:T(2,128)(2,1)S(1)}, u32[]{:S(2)}, u32[]{:S(2)}) %all-to-all-start.3) | async-done | bytes 1179680 | tf_op jit(solution)/shard_map/all_to_all | solution.py:78
  116.8 10.6 %all-to-all-start = ((bf16[2,3,128,1152]{2,0,1,3:T(2,128)(2,1)}), bf16[2,3,128,1152]{2,0,1,3:T(2,128)(2,1)S(1)}, u32[]{:S(2)}, u32[]{:S(2)}) async-start(bf16[2,3,128,1152]{2,0,1,3:T(2,128)(2,1)} %copy.87), calls=%async_computation | async-start | bytes 3538944 | tf_op jit(solution)/shard_map/all_to_all | solution.py:122
  127.4 2.1 copy.135
  129.5 3.8 %reshape_squeeze.21 = bf16[4,16,4,16,72]{4,3,2,1,0:T(8,128)(2,1)} reshape(bf16[32,2,1,4,1152]{4,3,1,0,2:T(4,128)(2,1)} %bitcast.96) | data formatting | bytes 1179648 | tf_op jit(solution)/shard_map/reshape;squeeze | solution.py:55
  133.3 0.5 copy.97
  133.7 1.2 fusion.42
  135.0 3.8 %reshape.46 = bf16[4,16,4,16,72]{4,3,2,1,0:T(8,128)(2,1)} reshape(bf16[64,1,4,1152]{3,2,1,0:T(4,128)(2,1)} %get-tuple-element.56) | data formatting | bytes 1179648 | tf_op jit(solution)/shard_map/reshape;squeeze | solution.py:56
  138.8 2.9 %reshape.47 = bf16[4,16,4,16,72]{4,3,2,1,0:T(8,128)(2,1)} reshape(bf16[64,1,4,1152]{3,2,1,0:T(4,128)(2,1)S(1)} %get-tuple-element.55) | data formatting | bytes 1179648 | tf_op jit(solution)/shard_map/reshape;squeeze | solution.py:57
  141.7 2.8 %multiply_reduce_fusion.1 = (f32[4,4,16,16]{3,2,1,0:T(8,128)S(1)}, f32[4,4,16,16,16]{3,4,2,1,0:T(8,128)S(1)}) fusion(bf16[4,16,4,16,72]{4,3,2,1,0:T(8,128)(2,1)} %reshape.46, bf16[4,16,4,16,72]{4,3,2,1,0:T(8,128)(2,1)S(1)} %copy-done.1), kind=kOutput, calls=%fused_computation.20 | convolution fusion | flops 9564160 | bytes 1458176 | tf_op jit(solution)/shard_map/pflhe,pglhe->plhfg/dot_general | solution.py:59
  144.5 0.8 fusion.27
  145.8 1.4 fusion.26
  147.5 2.5 reshape.48
  150.0 13.8 %all-to-all-done = bf16[2,3,128,1152]{2,0,1,3:T(2,128)(2,1)S(1)} async-done(((bf16[2,3,128,1152]{2,0,1,3:T(2,128)(2,1)}), bf16[2,3,128,1152]{2,0,1,3:T(2,128)(2,1)S(1)}, u32[]{:S(2)}, u32[]{:S(2)}) %all-to-all-start) | async-done | bytes 1769504 | tf_op jit(solution)/shard_map/all_to_all | solution.py:122
  163.8 8.1 %all-to-all-start.4 = ((bf16[64,4,1152]{2,1,0:T(4,128)(2,1)}), bf16[64,4,1152]{2,1,0:T(4,128)(2,1)S(1)}, u32[]{:S(2)}, u32[]{:S(2)}) async-start(bf16[64,4,1152]{2,1,0:T(4,128)(2,1)} %reshape.48), calls=%async_computation.4 | async-start | bytes 1179648 | tf_op jit(solution)/shard_map/all_to_all | solution.py:81
  172.1 0.5 copy.134
  172.7 0.9 copy-done.5
  173.7 24.0 %while.10 = (s32[]{:T(128)}, bf16[4,2,512,1,72]{2,4,1,3,0:T(8,128)(2,1)S(1)}, s32[4]{0:T(128)S(1)}, bf16[2,2048,1,72]{1,3,0,2:T(8,128)(2,1)S(1)}, bf16[2,2048,1,...) while((s32[]{:T(128)}, ...), condition=%wide.region_4.5_spmd, body=%wide.region_1.4_spmd.sunk | while | flops 620902400 | bytes 26661032 | solution.py:46
  173.7 0.6 dynamic_slice.16
  174.9 1.4 multiply_reduce_fusion.3
  176.3 1.6 fusion.52
  177.9 1.7 fusion.53
  179.7 0.6 dynamic_slice.16
  180.9 1.4 multiply_reduce_fusion.3
  182.3 1.6 fusion.52
  184.0 1.7 fusion.53
  185.7 0.6 dynamic_slice.16
  186.9 1.4 multiply_reduce_fusion.3
  188.3 1.6 fusion.52
  190.0 1.7 fusion.53
  191.7 0.6 dynamic_slice.16
  192.9 1.4 multiply_reduce_fusion.3
  194.3 1.6 fusion.52
  196.0 1.7 fusion.53
  197.7 2.0 copy.110
  199.7 13.2 %all-to-all-start.1 = ((bf16[2,2048,72]{2,0,1:T(2,128)(2,1)}), bf16[2,2048,72]{2,0,1:T(2,128)(2,1)S(1)}, u32[]{:S(2)}, u32[]{:S(2)}) async-start(bf16[2,2048,72]{2,0,1:T(2,128)(2,1)} %bitcast.14), calls=%async_computation.1 | async-start | bytes 2097152 | tf_op jit(solution)/shard_map/all_to_all | solution.py:92
  214.0 0.7 copy.107
  214.7 21.1 %all-to-all-done.1 = bf16[2,2048,72]{2,0,1:T(2,128)(2,1)S(1)} async-done(((bf16[2,2048,72]{2,0,1:T(2,128)(2,1)}), bf16[2,2048,72]{2,0,1:T(2,128)(2,1)S(1)}, u32[]{:S(2)}, u32[]{:S(2)}) %all-to-all-start.1) | async-done | bytes 589856 | tf_op jit(solution)/shard_map/all_to_all | solution.py:92
  235.8 0.8 copy.112
  236.6 0.8 multiply_convert_fusion
  237.4 4.2 %collective-permute-start = (bf16[1,128,1152]{1,2,0:T(8,128)(2,1)S(1)}, bf16[1,128,1152]{1,2,0:T(8,128)(2,1)S(1)}, u32[]{:S(2)}, u32[]{:S(2)}) collective-permute-start(bf16[1,128,1152]{1,2,0:T(8,128)(2,1)S(1)} %get-tuple-element.58), channel_id=1, source_target_pairs={{16,0},{32,16},{48,32},{64,48},{80,64},{96,80},{112,96},{128,112},... | collective-permute-start | bytes 884744 | tf_op jit(solution)/shard_map/ppermute | solution.py:17
  241.6 19.4 %collective-permute-done = bf16[1,128,1152]{1,2,0:T(8,128)(2,1)S(1)} collective-permute-done((bf16[1,128,1152]{1,2,0:T(8,128)(2,1)S(1)}, bf16[1,128,1152]{1,2,0:T(8,128)(2,1)S(1)}, u32[]{:S(2)}, u32[]{:S(2)}) %collective-permute-start) | collective-permute-done | bytes 294944 | tf_op jit(solution)/shard_map/ppermute | solution.py:17
  261.1 1.1 copy.108
  (31 shorter events, 2.3 us)
Async XLA Ops:
  0.0 213.1 %copy-start = (f32[30,1152]{1,0:T(8,128)S(1)}, f32[30,1152]{1,0:T(8,128)}, u32[]{:S(2)}) copy-start(f32[30,1152]{1,0:T(8,128)} %param.16) | copy-start | bytes 414724
  0.0 21.1 %copy-start.3 = (bf16[2,2,128,1152]{3,2,1,0:T(8,128)(2,1)S(1)}, bf16[2,2,128,1152]{3,2,1,0:T(8,128)(2,1)}, u32[]{:S(2)}) copy-start(bf16[2,2,128,1152]{3,2,1,0:T(8,128)(2,1)} %param.12) | copy-start | bytes 3538948
  2.6 48.1 %all-to-all-start.2 = ((bf16[2,1,128,1152]{3,0,1,2:T(2,128)(2,1)}), bf16[2,1,128,1152]{3,0,1,2:T(2,128)(2,1)S(1)}, u32[]{:S(2)}, u32[]{:S(2)}) async-start(bf16[2,1,128,1152]{3,0,1,2:T(2,128)(2,1)} %bitcast.77), calls=%async_computation.2 | async-start | bytes 1179648 | tf_op jit(solution)/shard_map/all_to_all | solution.py:77
  50.7 66.1 %copy-start.2 = (bf16[2,1,128,1152]{3,0,1,2:T(2,128)(2,1)}, bf16[2,1,128,1152]{3,0,1,2:T(2,128)(2,1)S(1)}, u32[]{:S(2)}) copy-start(bf16[2,1,128,1152]{3,0,1,2:T(2,128)(2,1)S(1)} %all-to-all-done.2) | copy-start | bytes 1769476
  50.7 66.1 %all-to-all-start.3 = ((bf16[2,2,128,1152]{3,1,0,2:T(2,128)(2,1)}), bf16[2,2,128,1152]{3,1,0,2:T(2,128)(2,1)S(1)}, u32[]{:S(2)}, u32[]{:S(2)}) async-start(bf16[2,2,128,1152]{3,1,0,2:T(2,128)(2,1)} %copy.96), calls=%async_computation.3 | async-start | bytes 2359296 | tf_op jit(solution)/shard_map/all_to_all | solution.py:78
  116.8 47.0 %all-to-all-start = ((bf16[2,3,128,1152]{2,0,1,3:T(2,128)(2,1)}), bf16[2,3,128,1152]{2,0,1,3:T(2,128)(2,1)S(1)}, u32[]{:S(2)}, u32[]{:S(2)}) async-start(bf16[2,3,128,1152]{2,0,1,3:T(2,128)(2,1)} %copy.87), calls=%async_computation | async-start | bytes 3538944 | tf_op jit(solution)/shard_map/all_to_all | solution.py:122
  135.0 6.8 %copy-start.1 = (bf16[4,16,4,16,72]{4,3,2,1,0:T(8,128)(2,1)S(1)}, bf16[4,16,4,16,72]{4,3,2,1,0:T(8,128)(2,1)}, u32[]{:S(2)}) copy-start(bf16[4,16,4,16,72]{4,3,2,1,0:T(8,128)(2,1)} %reshape_squeeze.21) | copy-start | bytes 1769476
  144.5 1.2 copy-start.4
  163.8 35.9 %all-to-all-start.4 = ((bf16[64,4,1152]{2,1,0:T(4,128)(2,1)}), bf16[64,4,1152]{2,1,0:T(4,128)(2,1)S(1)}, u32[]{:S(2)}, u32[]{:S(2)}) async-start(bf16[64,4,1152]{2,1,0:T(4,128)(2,1)} %reshape.48), calls=%async_computation.4 | async-start | bytes 1179648 | tf_op jit(solution)/shard_map/all_to_all | solution.py:81
  172.6 1.1 copy-start.5
  197.7 15.2 %copy-start.8 = (f32[64]{0:T(128)S(1)}, f32[64]{0:T(128)}, u32[]{:S(2)}) copy-start(f32[64]{0:T(128)} %param.17) | copy-start | bytes 772
  197.7 15.2 %copy-start.9 = (s32[2]{0:T(128)S(1)}, s32[2]{0:T(128)}, u32[]{:S(2)}) copy-start(s32[2]{0:T(128)} %param.14) | copy-start | bytes 28
  197.7 15.4 %copy-start.7 = (s32[2]{0:T(128)S(1)}, s32[2]{0:T(128)}, u32[]{:S(2)}) copy-start(s32[2]{0:T(128)} %param.13) | copy-start | bytes 28
  197.7 15.6 %copy-start.6 = (f32[30,1152]{1,0:T(8,128)S(1)}, f32[30,1152]{1,0:T(8,128)}, u32[]{:S(2)}) copy-start(f32[30,1152]{1,0:T(8,128)} %param.15) | copy-start | bytes 414724
  199.7 36.1 %all-to-all-start.1 = ((bf16[2,2048,72]{2,0,1:T(2,128)(2,1)}), bf16[2,2048,72]{2,0,1:T(2,128)(2,1)S(1)}, u32[]{:S(2)}, u32[]{:S(2)}) async-start(bf16[2,2048,72]{2,0,1:T(2,128)(2,1)} %bitcast.14), calls=%async_computation.1 | async-start | bytes 2097152 | tf_op jit(solution)/shard_map/all_to_all | solution.py:92
  237.4 23.6 %collective-permute-start = (bf16[1,128,1152]{1,2,0:T(8,128)(2,1)S(1)}, bf16[1,128,1152]{1,2,0:T(8,128)(2,1)S(1)}, u32[]{:S(2)}, u32[]{:S(2)}) collective-permute-start(bf16[1,128,1152]{1,2,0:T(8,128)(2,1)S(1)} %get-tuple-element.58), channel_id=1, source_target_pairs={{16,0},{32,16},{48,32},{64,48},{80,64},{96,80},{112,96},{128,112},... | collective-permute-start | bytes 884744 | tf_op jit(solution)/shard_map/ppermute | solution.py:17
where the time goes:
time: 263 us; the launch traced here: 262 us
  waiting for transfers between devices  130 us (49%)
  starting transfers between devices  65.9 us (25%)
  local copies, waits for them, and re-layouts  38.2 us (15%)
  matrix products  17 us (6%)
  other arithmetic  8.35 us (3%)
  loops' own time  2.65 us (1%)
    all_to_all x1, waiting for transfers between devices, temporal_queue(): lax.all_to_all(kv_in, 'queue', split_axis=2, concat_axis=0, tiled=True)  48.1 us
    all_to_all x1, waiting for transfers between devices, temporal_queue(): lax.all_to_all(query_in, 'queue', split_axis=2, concat_axis=0, tiled=True)  27.4 us
    all_to_all x1, waiting for transfers between devices, to_tokens(): lax.all_to_all(head_layout, 'sp', split_axis=1, concat_axis=2, tiled=True)  21.1 us
    ppermute x1, waiting for transfers between devices, from_behind(): return lax.ppermute(block, axis, route)  19.4 us
    all_to_all x1, starting transfers between devices, temporal_queue(): lax.all_to_all(query_in, 'queue', split_axis=2, concat_axis=0, tiled=True)  18.5 us
    all_to_all x1, waiting for transfers between devices, per_device(): lax.all_to_all(spatial_qkv, 'sp', split_axis=3, concat_axis=2, tiled=True)  13.8 us
    all_to_all x1, starting transfers between devices, to_tokens(): lax.all_to_all(head_layout, 'sp', split_axis=1, concat_axis=2, tiled=True)  13.2 us
    unnamed x23, local copies, waits for them, and re-layouts  12.8 us
  transfers between devices with their start and end apart: 6, of which 5 were waited for; matrix products, arithmetic and copies ran while one was open for 22% of the time, Pallas kernels for 0%

commit v1 on v0

v1 whole, which is shorter than its diff:
```python
import math

import jax
import jax.numpy as jnp
from jax import lax
from jax.experimental import pallas as pl
from jax.experimental.pallas import tpu as pltpu
from jax.sharding import Mesh
from jax.sharding import PartitionSpec as P

D = 1152
HEADS = 16
HEAD_DIM = 72
PLEN = 16
GROUPS = 16
TOK = 128
QBLOCK = 256
SHARE = 16
SCALE = math.log2(math.e) / math.sqrt(HEAD_DIM)

F32 = jnp.float32
BF16 = jnp.bfloat16
VMEM = pl.BlockSpec(memory_space=pltpu.VMEM)
SMEM = pl.BlockSpec(memory_space=pltpu.SMEM)
PARAMS = pltpu.CompilerParams(vmem_limit_bytes=56 << 20)


def matmul(a, b, a_dim, b_dim):
    return lax.dot_general(
        a, b, (((a_dim,), (b_dim,)), ((), ())), preferred_element_type=F32
    )


def pack_kernel(x_ref, o_ref):
    for part in range(3):
        turned = x_ref[0, part].T
        for head in range(HEADS):
            o_ref[head, part] = turned[head * HEAD_DIM : (head + 1) * HEAD_DIM]


def pack_frame(spatial_qkv, frame):
    return pl.pallas_call(
        pack_kernel,
        grid=(1,),
        in_specs=[pl.BlockSpec((1, 3, TOK, D), lambda i: (frame, 0, 0, 0))],
        out_specs=pl.BlockSpec((HEADS, 3, HEAD_DIM, TOK), lambda i: (0, 0, 0, 0)),
        out_shape=jax.ShapeDtypeStruct((HEADS, 3, HEAD_DIM, TOK), BF16),
        compiler_params=PARAMS,
        name="pack",
    )(spatial_qkv)


def spatial_kernel(x_ref, o_ref, query, value):
    for group in range(GROUPS):
        query[group * TOK : (group + 1) * TOK, :] = x_ref[group, 0].T
        value[0:HEAD_DIM, group * TOK : (group + 1) * TOK] = x_ref[group, 2]
    value[HEAD_DIM:, :] = jnp.ones((8, GROUPS * TOK), BF16)
    keys = jnp.concatenate([x_ref[group, 1] for group in range(GROUPS)], axis=1)
    values = value[...]
    for block in range(GROUPS * TOK // QBLOCK):
        scores = matmul(query[block * QBLOCK : (block + 1) * QBLOCK, :], keys, 1, 0)
        row_max = jnp.max(scores, axis=1, keepdims=True)
        weights = jnp.exp2(scores * SCALE - row_max * SCALE).astype(BF16)
        summed = matmul(weights, values, 1, 1).T
        result = (summed[:HEAD_DIM] / summed[HEAD_DIM : HEAD_DIM + 1]).astype(BF16)
        for j in range(QBLOCK // TOK):
            o_ref[block * (QBLOCK // TOK) + j] = result[:, j * TOK : (j + 1) * TOK]


def spatial_frame(packed):
    return pl.pallas_call(
        spatial_kernel,
        in_specs=[VMEM],
        out_specs=VMEM,
        out_shape=jax.ShapeDtypeStruct((GROUPS, HEAD_DIM, TOK), BF16),
        scratch_shapes=[
            pltpu.VMEM((GROUPS * TOK, HEAD_DIM), BF16),
            pltpu.VMEM((HEAD_DIM + 8, GROUPS * TOK), BF16),
        ],
        compiler_params=PARAMS,
        name="spatial",
    )(packed)


def temporal_kernel(q_ref, kv_ref, o_ref):
    rows = PLEN * SHARE
    token_of_row = lax.broadcasted_iota(jnp.int32, (rows, rows), 0) % SHARE
    token_of_column = lax.broadcasted_iota(jnp.int32, (rows, rows), 1) % SHARE
    same_token = token_of_row == token_of_column
    queries = q_ref[...].reshape(rows, D)
    keys = kv_ref[:, 0].reshape(rows, D)
    values = kv_ref[:, 1].reshape(rows, D)
    tiles = [jnp.zeros((rows, 128), F32) for _ in range(D // 128)]
    for head in range(HEADS):
        first, last = head * HEAD_DIM // 128, ((head + 1) * HEAD_DIM - 1) // 128
        low, high = first * 128, (last + 1) * 128
        lane = lax.broadcasted_iota(jnp.int32, (rows, high - low), 1) + low
        mine = (lane >= head * HEAD_DIM) & (lane < (head + 1) * HEAD_DIM)
        q = jnp.where(mine, queries[:, low:high], 0).astype(BF16)
        v = jnp.where(mine, values[:, low:high], 0).astype(BF16)
        scores = matmul(q, keys[:, low:high], 1, 1)
        scores = jnp.where(same_token, scores * SCALE, -1e30)
        weights = jnp.exp2(scores - jnp.max(scores, axis=1, keepdims=True))
        row_sum = jnp.sum(weights, axis=1, keepdims=True)
        summed = matmul(weights.astype(BF16), v, 1, 0) / row_sum
        for tile in range(first, last + 1):
            tiles[tile] += summed[:, tile * 128 - low : tile * 128 - low + 128]
    for tile in range(D // 128):
        o_ref[:, :, tile * 128 : (tile + 1) * 128] = (
            tiles[tile].astype(BF16).reshape(PLEN, SHARE, 128)
        )


def temporal_share(query, kv):
    return pl.pallas_call(
        temporal_kernel,
        in_specs=[VMEM, VMEM],
        out_specs=VMEM,
        out_shape=jax.ShapeDtypeStruct((PLEN, SHARE, D), BF16),
        compiler_params=PARAMS,
        name="temporal",
    )(query, kv)


def combine_kernel(near_ref, far_ref, time_ref, step_ref, level_ref, gs_ref, gt_ref, table_ref, o_ref):
    for slot, space_ref in enumerate((near_ref, far_ref)):
        space = space_ref[...].astype(F32).reshape(D, TOK).T
        timely = time_ref[:, slot].astype(F32).reshape(TOK, D)
        row = step_ref[slot]
        gate_space = gs_ref[pl.ds(row, 1), :]
        gate_time = gt_ref[pl.ds(row, 1), :]
        size = table_ref[level_ref[slot]]
        o_ref[slot] = (size * (gate_space * space + gate_time * timely)).astype(BF16)


def combine(near, far, timely, steps, levels, spatial_gate, temporal_gate, step_table):
    return pl.pallas_call(
        combine_kernel,
        in_specs=[VMEM, VMEM, VMEM, SMEM, SMEM, VMEM, VMEM, SMEM],
        out_specs=VMEM,
        out_shape=jax.ShapeDtypeStruct((2, TOK, D), BF16),
        compiler_params=PARAMS,
        name="combine",
    )(near, far, timely, steps, levels, spatial_gate, temporal_gate, step_table)


def one_back(block, axes):
    size = lax.axis_size(axes)
    return lax.ppermute(block, axes, [(i, (i - 1) % size) for i in range(size)])


def exchange(block, axes):
    return lax.all_to_all(block, axes, 0, 0)


def per_device(
    spatial_qkv,
    temporal_query,
    temporal_kv,
    timestep,
    noise_level,
    spatial_gate,
    temporal_gate,
    step_table,
):
    queue = ("part", "member")
    near_in = exchange(pack_frame(spatial_qkv, 0), "sp")
    far_in = exchange(pack_frame(spatial_qkv, 1), "sp")
    ahead = one_back(jnp.stack([timestep[0], noise_level[0]]), queue)
    steps = jnp.stack([timestep[1], ahead[0]])
    levels = jnp.stack([noise_level[1], ahead[1]])
    query = temporal_query.reshape(2, 8, SHARE, D).transpose(1, 0, 2, 3)
    kv = temporal_kv.reshape(2, 2, 8, SHARE, D).transpose(2, 0, 1, 3, 4)
    query = exchange(query, "member").reshape(PLEN, SHARE, D)
    kv = exchange(kv, "member").reshape(PLEN, 2, SHARE, D)
    timely = temporal_share(query, kv)
    next_part = one_back(timely[:1], "part")
    timely = jnp.concatenate([timely[1:], next_part]).reshape(8, 2, SHARE, D)
    timely = exchange(timely, "member")
    first = exchange(spatial_frame(near_in), "sp")
    first = one_back(first, queue)
    second = exchange(spatial_frame(far_in), "sp")
    return combine(
        second, first, timely, steps, levels, spatial_gate, temporal_gate, step_table
    )


def solution(mesh):
    members = 8
    inner = Mesh(
        mesh.devices.reshape(mesh.shape["queue"] // members, members, mesh.shape["sp"]),
        ("part", "member", "sp"),
    )
    queue = ("part", "member")
    return jax.shard_map(
        per_device,
        mesh=inner,
        in_specs=(
            P(queue, None, "sp", None),
            P(queue, "sp", None),
            P(queue, None, "sp", None),
            P(queue),
            P(queue),
            P(),
            P(),
            P(),
        ),
        out_specs=P(queue, "sp", None),
        check_vma=False,
    )
```

time: 263 us -> 178 us (0.68)
  the two profiles are of different devices: /device:TPU:23 before, /device:TPU:39 now
where the time goes in v1:
time: 178 us; the launch traced here: 177 us
  waiting for transfers between devices  64.2 us (36%)
  starting transfers between devices  53.8 us (30%)
  Pallas kernels  27.3 us (15%)
  blocking collectives  20.6 us (12%)
  other arithmetic  6.03 us (3%)
  local copies, waits for them, and re-layouts  4.98 us (3%)
    all_to_all x6, waiting for transfers between devices, exchange(): return lax.all_to_all(block, axes, 0, 0)  46.6 us
    all_to_all x6, starting transfers between devices, exchange(): return lax.all_to_all(block, axes, 0, 0)  35.6 us
    all_to_all x1, blocking collectives, exchange(): return lax.all_to_all(block, axes, 0, 0)  20.6 us
    ppermute x3, starting transfers between devices, one_back(): return lax.ppermute(block, axes, [(i, (i - 1) % size) for i in range(size)])  18.2 us
    ppermute x3, waiting for transfers between devices, one_back(): return lax.ppermute(block, axes, [(i, (i - 1) % size) for i in range(size)])  17.6 us
    pallas_call x2, Pallas kernels, spatial_frame(): pl.pallas_call(spatial_kernel, in_specs=[VMEM], out_specs=VMEM, out_shape...  15.6 us
    pallas_call x2, Pallas kernels, pack_frame(): pl.pallas_call(pack_kernel, grid=(1,), in_specs=[pl.BlockSpec((1, 3, TOK,...  4.81 us
    pallas_call x1, Pallas kernels, temporal_share(): pl.pallas_call(temporal_kernel, in_specs=[VMEM, VMEM], out_specs=VMEM, ou...  4.45 us
  transfers between devices with their start and end apart: 9, of which 7 were waited for; matrix products, arithmetic and copies ran while one was open for 4% of the time, Pallas kernels for 12%

profile of v1, /device:TPU:39, one launch (start us, length us, event | category | flops | bytes accessed | tf_op | source)
XLA Modules:
  0.0 177.1 jit_solution(10155498456616312592)
XLA Ops:
  0.0 0.0 copy-start.4
  0.0 2.0 %copy.14 = bf16[2,8,16,1152]{3,2,0,1:T(8,128)(2,1)} copy(bf16[2,8,16,1152]{3,2,1,0:T(8,128)(2,1)} %bitcast.15) | data formatting | bytes 1179648 | tf_op jit(solution)/shard_map/reshape | solution.py:172
  2.0 5.1 %all-to-all-start.4 = ((bf16[8,2,16,1152]{3,2,1,0:T(8,128)(2,1)}), bf16[8,2,16,1152]{3,2,1,0:T(8,128)(2,1)S(1)}, u32[]{:S(2)}, u32[]{:S(2)}) async-start(bf16[8,2,16,1152]{3,2,1,0:T(8,128)(2,1)} %bitcast.10), calls=%async_computation.4 | async-start | bytes 1179648 | tf_op jit(solution)/shard_map/all_to_all | solution.py:153
  7.1 0.0 copy-done.4
  7.1 0.1 copy.13
  7.2 8.4 %all-to-all-done.4 = bf16[8,2,16,1152]{3,2,1,0:T(8,128)(2,1)S(1)} async-done(((bf16[8,2,16,1152]{3,2,1,0:T(8,128)(2,1)}), bf16[8,2,16,1152]{3,2,1,0:T(8,128)(2,1)S(1)}, u32[]{:S(2)}, u32[]{:S(2)}) %all-to-all-start.4) | async-done | bytes 589856 | tf_op jit(solution)/shard_map/all_to_all | solution.py:153
  15.6 0.0 copy-start.3
  15.6 20.6 %all_to_all.35 = bf16[8,2,2,16,1152]{4,3,2,1,0:T(8,128)(2,1)} all-to-all(bf16[8,2,2,16,1152]{4,3,2,1,0:T(8,128)(2,1)S(1)} %bitcast.11), channel_id=1, replica_groups=mesh['part'=4,'member'=8,'sp'=16] {'member'}, dimensions={0} | all-to-all | bytes 2359296 | tf_op jit(solution)/shard_map/all_to_all | solution.py:153
  36.2 0.0 copy-done.3
  36.2 4.4 %temporal.1 = bf16[16,16,1152]{2,1,0:T(8,128)(2,1)} custom-call(bf16[16,16,1152]{2,1,0:T(8,128)(2,1)} %bitcast.13, bf16[16,2,16,1152]{3,2,1,0:T(8,128)(2,1)} %bitcast.12), custom_call_target="tpu_custom_call" | custom-call | tf_op jit(solution)/shard_map/temporal/pallas_call | solution.py:115
  40.7 0.0 slice-start
  40.7 0.8 slice.33
  41.5 11.5 %collective-permute-start.1 = (bf16[1,16,1152]{2,1,0:T(8,128)(2,1)S(1)}, bf16[1,16,1152]{2,1,0:T(8,128)(2,1)S(1)}, u32[]{:S(2)}, u32[]{:S(2)}) collective-permute-start(bf16[1,16,1152]{2,1,0:T(8,128)(2,1)S(1)} %slice.33), channel_id=1, source_target_pairs={{0,384},{128,0},{256,128},{384,256},{1,385},{129,1},{257,129},{385... | collective-permute-start | bytes 110600 | tf_op jit(solution)/shard_map/ppermute | solution.py:149
  53.0 1.0 collective-permute-done.1
  54.1 0.0 slice-done
  54.1 0.9 pad_maximum_fusion
  55.0 7.4 %all-to-all-start.6 = ((bf16[8,2,16,1152]{3,2,1,0:T(8,128)(2,1)}), bf16[8,2,16,1152]{3,2,1,0:T(8,128)(2,1)S(1)}, u32[]{:S(2)}, u32[]{:S(2)}) async-start(bf16[8,2,16,1152]{3,2,1,0:T(8,128)(2,1)} %bitcast.6), calls=%async_computation.6 | async-start | bytes 1179648 | tf_op jit(solution)/shard_map/all_to_all | solution.py:153
  62.4 2.4 %pack.3 = bf16[16,3,72,128]{3,2,1,0:T(8,128)(2,1)} custom-call(bf16[2,3,128,1152]{3,2,1,0:T(8,128)(2,1)} %x_ref.3), custom_call_target="tpu_custom_call" | custom-call | tf_op jit(solution)/shard_map/pack/pallas_call | solution.py:42
  64.8 6.0 %all-to-all-done.6.time_ref = bf16[8,2,16,1152]{3,2,1,0:T(8,128)(2,1)S(1)} async-done(((bf16[8,2,16,1152]{3,2,1,0:T(8,128)(2,1)}), bf16[8,2,16,1152]{3,2,1,0:T(8,128)(2,1)S(1)}, u32[]{:S(2)}, u32[]{:S(2)}) %all-to-all-start.6) | async-done | bytes 589856 | tf_op jit(solution)/shard_map/all_to_all | solution.py:153
  70.8 0.0 copy-start.2
  70.8 5.9 %all-to-all-start.2 = ((bf16[16,3,72,128]{3,2,1,0:T(8,128)(2,1)}), bf16[16,3,72,128]{3,2,1,0:T(8,128)(2,1)S(1)}, u32[]{:S(2)}, u32[]{:S(2)}) async-start(bf16[16,3,72,128]{3,2,1,0:T(8,128)(2,1)} %pack.3), calls=%async_computation.2 | async-start | bytes 1769472 | tf_op jit(solution)/shard_map/all_to_all | solution.py:153
  76.7 2.4 %pack.2 = bf16[16,3,72,128]{3,2,1,0:T(8,128)(2,1)} custom-call(bf16[2,3,128,1152]{3,2,1,0:T(8,128)(2,1)} %x_ref.3), custom_call_target="tpu_custom_call" | custom-call | tf_op jit(solution)/shard_map/pack/pallas_call | solution.py:42
  79.1 0.0 copy-done.2
  79.1 18.8 %all-to-all-done.2.x_ref = bf16[16,3,72,128]{3,2,1,0:T(8,128)(2,1)S(1)} async-done(((bf16[16,3,72,128]{3,2,1,0:T(8,128)(2,1)}), bf16[16,3,72,128]{3,2,1,0:T(8,128)(2,1)S(1)}, u32[]{:S(2)}, u32[]{:S(2)}) %all-to-all-start.2) | async-done | bytes 884768 | tf_op jit(solution)/shard_map/all_to_all | solution.py:153
  97.9 5.1 %all-to-all-start = ((bf16[16,3,72,128]{3,2,1,0:T(8,128)(2,1)}), bf16[16,3,72,128]{3,2,1,0:T(8,128)(2,1)S(1)}, u32[]{:S(2)}, u32[]{:S(2)}) async-start(bf16[16,3,72,128]{3,2,1,0:T(8,128)(2,1)} %pack.2), calls=%async_computation | async-start | bytes 1769472 | tf_op jit(solution)/shard_map/all_to_all | solution.py:153
  103.0 0.0 copy-done.1
  103.1 7.8 %spatial.3 = bf16[16,72,128]{2,1,0:T(8,128)(2,1)} custom-call(bf16[16,3,72,128]{3,2,1,0:T(8,128)(2,1)} %copy-done.1), custom_call_target="tpu_custom_call" | custom-call | tf_op jit(solution)/shard_map/spatial/pallas_call | solution.py:71
  110.9 13.4 %all-to-all-done.x_ref = bf16[16,3,72,128]{3,2,1,0:T(8,128)(2,1)S(1)} async-done(((bf16[16,3,72,128]{3,2,1,0:T(8,128)(2,1)}), bf16[16,3,72,128]{3,2,1,0:T(8,128)(2,1)S(1)}, u32[]{:S(2)}, u32[]{:S(2)}) %all-to-all-start) | async-done | bytes 884768 | tf_op jit(solution)/shard_map/all_to_all | solution.py:153
  124.2 5.1 %all-to-all-start.3 = ((bf16[16,72,128]{2,1,0:T(8,128)(2,1)}), bf16[16,72,128]{2,1,0:T(8,128)(2,1)S(1)}, u32[]{:S(2)}, u32[]{:S(2)}) async-start(bf16[16,72,128]{2,1,0:T(8,128)(2,1)} %spatial.3), calls=%async_computation.3 | async-start | bytes 589824 | tf_op jit(solution)/shard_map/all_to_all | solution.py:153
  129.4 0.0 copy-done
  129.4 7.8 %spatial.2 = bf16[16,72,128]{2,1,0:T(8,128)(2,1)} custom-call(bf16[16,3,72,128]{3,2,1,0:T(8,128)(2,1)} %copy-done), custom_call_target="tpu_custom_call" | custom-call | tf_op jit(solution)/shard_map/spatial/pallas_call | solution.py:71
  137.2 0.0 all-to-all-done.3
  137.2 7.0 %all-to-all-start.1 = ((bf16[16,72,128]{2,1,0:T(8,128)(2,1)}), bf16[16,72,128]{2,1,0:T(8,128)(2,1)S(1)}, u32[]{:S(2)}, u32[]{:S(2)}) async-start(bf16[16,72,128]{2,1,0:T(8,128)(2,1)} %spatial.2), calls=%async_computation.1 | async-start | bytes 589824 | tf_op jit(solution)/shard_map/all_to_all | solution.py:153
  144.1 0.0 copy-done.7
  144.1 0.0 copy-done.8
  144.2 0.7 fusion
  144.8 1.3 pad_add_fusion
  146.1 4.8 %collective-permute-start.2 = (s32[2]{0:T(128)S(1)}, s32[2]{0:T(128)S(1)}, u32[]{:S(2)}, u32[]{:S(2)}) collective-permute-start(s32[2]{0:T(128)S(1)} %pad_add_fusion), channel_id=1, source_target_pairs={{0,496},{16,0},{32,16},{48,32},{64,48},{80,64},{96,80},{112,96},{1... | collective-permute-start | bytes 32 | tf_op jit(solution)/shard_map/ppermute | solution.py:149
  150.9 1.9 %collective-permute-start = (bf16[16,72,128]{2,1,0:T(8,128)(2,1)S(1)}, bf16[16,72,128]{2,1,0:T(8,128)(2,1)S(1)}, u32[]{:S(2)}, u32[]{:S(2)}) collective-permute-start(bf16[16,72,128]{2,1,0:T(8,128)(2,1)S(1)} %all-to-all-done.3), channel_id=1, source_target_pairs={{0,496},{16,0},{32,16},{48,32},{64,48},{80,64},{96,80},{112,96},{1... | collective-permute-start | bytes 884744 | tf_op jit(solution)/shard_map/ppermute | solution.py:149
  152.8 5.6 %collective-permute-done.2 = s32[2]{0:T(128)S(1)} collective-permute-done((s32[2]{0:T(128)S(1)}, s32[2]{0:T(128)S(1)}, u32[]{:S(2)}, u32[]{:S(2)}) %collective-permute-start.2) | collective-permute-done | bytes 40 | tf_op jit(solution)/shard_map/ppermute | solution.py:149
  158.4 0.6 fusion.1
  159.0 2.0 %pad_add_fusion.1.step_ref = s32[2]{0:T(128)} fusion(s32[1]{0:T(128)} %get-tuple-element.8, s32[1]{0:T(128)} %get-tuple-element.12), kind=kLoop, calls=%fused_computation.4 | loop fusion | flops 2 | bytes 16 | tf_op jit(solution)/shard_map/stack | solution.py:170
  161.0 1.9 %pad_add_fusion.2.level_ref = s32[2]{0:T(128)} fusion(s32[1]{0:T(128)} %get-tuple-element.7, s32[1]{0:T(128)} %get-tuple-element.5), kind=kLoop, calls=%fused_computation.5 | loop fusion | flops 2 | bytes 16 | tf_op jit(solution)/shard_map/stack | solution.py:171
  162.9 0.0 all-to-all-done.1.near_ref
  162.9 11.0 %collective-permute-done.far_ref = bf16[16,72,128]{2,1,0:T(8,128)(2,1)S(1)} collective-permute-done((bf16[16,72,128]{2,1,0:T(8,128)(2,1)S(1)}, bf16[16,72,128]{2,1,0:T(8,128)(2,1)S(1)}, u32[]{:S(2)}, u32[]{:S(2)}) %collective-permute-start) | collective-permute-done | bytes 294944 | tf_op jit(solution)/shard_map/ppermute | solution.py:149
  173.9 0.0 copy-done.5
  173.9 0.7 copy-done.6
  174.6 2.5 %combine.1 = bf16[2,128,1152]{2,1,0:T(8,128)(2,1)} custom-call(bf16[16,72,128]{2,1,0:T(8,128)(2,1)} %copy-done.5, bf16[16,72,128]{2,1,0:T(8,128)(2,1)} %copy-done.6, bf16[8,2,16,1152]{3,2,1,0:T(8,128)(2,1)} %copy-done.2, s32[2]{0:T(128)} %pad_add_fusion.1.step_ref, s32[2]{0:T(128)} %pad_add_fusion.2.level_ref, f32[30,1152]{1,0:T(8,128)} %gs_ref.1, ...), custom_call_target="tpu_custom_call" | custom-call | tf_op jit(solution)/shard_map/combine/pallas_call | solution.py:137
  (6 shorter events, 0.0 us)
Async XLA Ops:
  0.0 7.1 %copy-start.4 = (bf16[2,2,128,1152]{3,2,1,0:T(8,128)(2,1)S(1)}, bf16[2,2,128,1152]{3,2,1,0:T(8,128)(2,1)}, u32[]{:S(2)}) copy-start(bf16[2,2,128,1152]{3,2,1,0:T(8,128)(2,1)} %param.10) | copy-start | bytes 3538948
  2.0 13.6 %all-to-all-start.4 = ((bf16[8,2,16,1152]{3,2,1,0:T(8,128)(2,1)}), bf16[8,2,16,1152]{3,2,1,0:T(8,128)(2,1)S(1)}, u32[]{:S(2)}, u32[]{:S(2)}) async-start(bf16[8,2,16,1152]{3,2,1,0:T(8,128)(2,1)} %bitcast.10), calls=%async_computation.4 | async-start | bytes 1179648 | tf_op jit(solution)/shard_map/all_to_all | solution.py:153
  15.6 20.6 %copy-start.3 = (bf16[8,2,16,1152]{3,2,1,0:T(8,128)(2,1)}, bf16[8,2,16,1152]{3,2,1,0:T(8,128)(2,1)S(1)}, u32[]{:S(2)}) copy-start(bf16[8,2,16,1152]{3,2,1,0:T(8,128)(2,1)S(1)} %all-to-all-done.4) | copy-start | bytes 1769476
  40.7 13.4 %slice-start = ((bf16[16,16,1152]{2,1,0:T(8,128)(2,1)}), bf16[15,16,1152]{2,1,0:T(8,128)(2,1)S(1)}, s32[]{:S(2)}) async-start(bf16[16,16,1152]{2,1,0:T(8,128)(2,1)} %temporal.1), calls=%async_computation.7 | async-start | bytes 1105920 | tf_op jit(solution)/shard_map/slice | solution.py:178
  41.5 12.6 %collective-permute-start.1 = (bf16[1,16,1152]{2,1,0:T(8,128)(2,1)S(1)}, bf16[1,16,1152]{2,1,0:T(8,128)(2,1)S(1)}, u32[]{:S(2)}, u32[]{:S(2)}) collective-permute-start(bf16[1,16,1152]{2,1,0:T(8,128)(2,1)S(1)} %slice.33), channel_id=1, source_target_pairs={{0,384},{128,0},{256,128},{384,256},{1,385},{129,1},{257,129},{385... | collective-permute-start | bytes 110600 | tf_op jit(solution)/shard_map/ppermute | solution.py:149
  55.0 15.9 %all-to-all-start.6 = ((bf16[8,2,16,1152]{3,2,1,0:T(8,128)(2,1)}), bf16[8,2,16,1152]{3,2,1,0:T(8,128)(2,1)S(1)}, u32[]{:S(2)}, u32[]{:S(2)}) async-start(bf16[8,2,16,1152]{3,2,1,0:T(8,128)(2,1)} %bitcast.6), calls=%async_computation.6 | async-start | bytes 1179648 | tf_op jit(solution)/shard_map/all_to_all | solution.py:153
  70.8 8.3 %copy-start.2 = (bf16[8,2,16,1152]{3,2,1,0:T(8,128)(2,1)}, bf16[8,2,16,1152]{3,2,1,0:T(8,128)(2,1)S(1)}, u32[]{:S(2)}) copy-start(bf16[8,2,16,1152]{3,2,1,0:T(8,128)(2,1)S(1)} %all-to-all-done.6.time_ref) | copy-start | bytes 1769476
  70.8 27.1 %all-to-all-start.2 = ((bf16[16,3,72,128]{3,2,1,0:T(8,128)(2,1)}), bf16[16,3,72,128]{3,2,1,0:T(8,128)(2,1)S(1)}, u32[]{:S(2)}, u32[]{:S(2)}) async-start(bf16[16,3,72,128]{3,2,1,0:T(8,128)(2,1)} %pack.3), calls=%async_computation.2 | async-start | bytes 1769472 | tf_op jit(solution)/shard_map/all_to_all | solution.py:153
  97.9 5.1 %copy-start.1 = (bf16[16,3,72,128]{3,2,1,0:T(8,128)(2,1)}, bf16[16,3,72,128]{3,2,1,0:T(8,128)(2,1)S(1)}, u32[]{:S(2)}) copy-start(bf16[16,3,72,128]{3,2,1,0:T(8,128)(2,1)S(1)} %all-to-all-done.2.x_ref) | copy-start | bytes 2654212
  97.9 26.3 %all-to-all-start = ((bf16[16,3,72,128]{3,2,1,0:T(8,128)(2,1)}), bf16[16,3,72,128]{3,2,1,0:T(8,128)(2,1)S(1)}, u32[]{:S(2)}, u32[]{:S(2)}) async-start(bf16[16,3,72,128]{3,2,1,0:T(8,128)(2,1)} %pack.2), calls=%async_computation | async-start | bytes 1769472 | tf_op jit(solution)/shard_map/all_to_all | solution.py:153
  110.8 33.3 %copy-start.7 = (s32[2]{0:T(128)S(1)}, s32[2]{0:T(128)}, u32[]{:S(2)}) copy-start(s32[2]{0:T(128)} %param.12) | copy-start | bytes 28
  110.9 33.3 %copy-start.8 = (s32[2]{0:T(128)S(1)}, s32[2]{0:T(128)}, u32[]{:S(2)}) copy-start(s32[2]{0:T(128)} %param.11) | copy-start | bytes 28
  124.2 5.1 %copy-start = (bf16[16,3,72,128]{3,2,1,0:T(8,128)(2,1)}, bf16[16,3,72,128]{3,2,1,0:T(8,128)(2,1)S(1)}, u32[]{:S(2)}) copy-start(bf16[16,3,72,128]{3,2,1,0:T(8,128)(2,1)S(1)} %all-to-all-done.x_ref) | copy-start | bytes 2654212
  124.2 12.9 %all-to-all-start.3 = ((bf16[16,72,128]{2,1,0:T(8,128)(2,1)}), bf16[16,72,128]{2,1,0:T(8,128)(2,1)S(1)}, u32[]{:S(2)}, u32[]{:S(2)}) async-start(bf16[16,72,128]{2,1,0:T(8,128)(2,1)} %spatial.3), calls=%async_computation.3 | async-start | bytes 589824 | tf_op jit(solution)/shard_map/all_to_all | solution.py:153
  137.2 25.7 %all-to-all-start.1 = ((bf16[16,72,128]{2,1,0:T(8,128)(2,1)}), bf16[16,72,128]{2,1,0:T(8,128)(2,1)S(1)}, u32[]{:S(2)}, u32[]{:S(2)}) async-start(bf16[16,72,128]{2,1,0:T(8,128)(2,1)} %spatial.2), calls=%async_computation.1 | async-start | bytes 589824 | tf_op jit(solution)/shard_map/all_to_all | solution.py:153
  146.1 12.3 %collective-permute-start.2 = (s32[2]{0:T(128)S(1)}, s32[2]{0:T(128)S(1)}, u32[]{:S(2)}, u32[]{:S(2)}) collective-permute-start(s32[2]{0:T(128)S(1)} %pad_add_fusion), channel_id=1, source_target_pairs={{0,496},{16,0},{32,16},{48,32},{64,48},{80,64},{96,80},{112,96},{1... | collective-permute-start | bytes 32 | tf_op jit(solution)/shard_map/ppermute | solution.py:149
  150.9 23.0 %collective-permute-start = (bf16[16,72,128]{2,1,0:T(8,128)(2,1)S(1)}, bf16[16,72,128]{2,1,0:T(8,128)(2,1)S(1)}, u32[]{:S(2)}, u32[]{:S(2)}) collective-permute-start(bf16[16,72,128]{2,1,0:T(8,128)(2,1)S(1)} %all-to-all-done.3), channel_id=1, source_target_pairs={{0,496},{16,0},{32,16},{48,32},{64,48},{80,64},{96,80},{112,96},{1... | collective-permute-start | bytes 884744 | tf_op jit(solution)/shard_map/ppermute | solution.py:149
  162.9 11.0 %copy-start.5 = (bf16[16,72,128]{2,1,0:T(8,128)(2,1)}, bf16[16,72,128]{2,1,0:T(8,128)(2,1)S(1)}, u32[]{:S(2)}) copy-start(bf16[16,72,128]{2,1,0:T(8,128)(2,1)S(1)} %all-to-all-done.1.near_ref) | copy-start | bytes 884740
  173.9 0.7 copy-start.6

commit v2 on v1

v2 whole, which is shorter than its diff:
```python
import functools
import math

import jax
import jax.numpy as jnp
from jax import lax
from jax.experimental import pallas as pl
from jax.experimental.pallas import tpu as pltpu
from jax.sharding import Mesh
from jax.sharding import PartitionSpec as P

D = 1152
HEADS = 16
HEAD_DIM = 72
PLEN = 16
GROUPS = 16
TOK = 128
QBLOCK = 256
CHIPS = 4
WIDE = 32
SHARE = 16
SCALE = math.log2(math.e) / math.sqrt(HEAD_DIM)

QUEUE = ("part", "x", "core")
F32 = jnp.float32
BF16 = jnp.bfloat16
VMEM = pl.BlockSpec(memory_space=pltpu.VMEM)
ANY = pl.BlockSpec(memory_space=pl.ANY)
SMEM = pl.BlockSpec(memory_space=pltpu.SMEM)
PARAMS = pltpu.CompilerParams(vmem_limit_bytes=56 << 20)


def matmul(a, b, a_dim, b_dim):
    return lax.dot_general(
        a, b, (((a_dim,), (b_dim,)), ((), ())), preferred_element_type=F32
    )


def resident(array):
    return pltpu.with_memory_space_constraint(array, pltpu.VMEM)


def turn(rows, write):
    turned = rows.T
    for head in range(HEADS):
        write(head, turned[head * HEAD_DIM : (head + 1) * HEAD_DIM])


def pack_kernel(parts, x_ref, time_ref, level_ref, *refs):
    o_ref, index_ref = refs[-2:]
    index_ref[0] = time_ref[0]
    index_ref[1] = level_ref[0]
    for place, (frame, part) in enumerate(parts):

        def write(head, rows, place=place):
            o_ref[head, place] = rows

        turn(x_ref[frame, part], write)


def pack(parts, spatial_qkv, timestep, noise_level, after):
    return pl.pallas_call(
        functools.partial(pack_kernel, parts),
        in_specs=[VMEM, SMEM, SMEM] + [ANY] * len(after),
        out_specs=[VMEM, SMEM],
        out_shape=[
            jax.ShapeDtypeStruct((HEADS, len(parts), HEAD_DIM, TOK), BF16),
            jax.ShapeDtypeStruct((2,), jnp.int32),
        ],
        compiler_params=PARAMS,
        name="pack",
    )(spatial_qkv, timestep, noise_level, *after)


def attend(find, query, value, write):
    for group in range(GROUPS):
        query[group * TOK : (group + 1) * TOK, :] = find(group, 0).T
        value[0:HEAD_DIM, group * TOK : (group + 1) * TOK] = find(group, 2)
    value[HEAD_DIM:, :] = jnp.ones((8, GROUPS * TOK), BF16)
    keys = jnp.concatenate([find(group, 1) for group in range(GROUPS)], axis=1)
    values = value[...]
    for block in range(GROUPS * TOK // QBLOCK):
        scores = matmul(query[block * QBLOCK : (block + 1) * QBLOCK, :], keys, 1, 0)
        row_max = jnp.max(scores, axis=1, keepdims=True)
        weights = jnp.exp2(scores * SCALE - row_max * SCALE).astype(BF16)
        summed = matmul(weights, values, 1, 1).T
        result = (summed[:HEAD_DIM] / summed[HEAD_DIM : HEAD_DIM + 1]).astype(BF16)
        for j in range(QBLOCK // TOK):
            write(block * (QBLOCK // TOK) + j, result[:, j * TOK : (j + 1) * TOK])


def first_kernel(x_ref, o_ref, query, value):
    def write(group, result):
        o_ref[group] = result

    attend(lambda group, part: x_ref[group, part], query, value, write)


def second_kernel(q_ref, kv_ref, far_ref, *refs):
    o_ref, query, value = refs[-3:]

    def find(group, part):
        return kv_ref[group, part - 1] if part else q_ref[group, 3]

    def write(group, result):
        o_ref[group, 0] = result
        o_ref[group, 1] = far_ref[group]

    attend(find, query, value, write)


SPATIAL_SCRATCH = [
    pltpu.VMEM((GROUPS * TOK, HEAD_DIM), BF16),
    pltpu.VMEM((HEAD_DIM + 8, GROUPS * TOK), BF16),
]


def first_frame(packed):
    return pl.pallas_call(
        first_kernel,
        in_specs=[VMEM],
        out_specs=VMEM,
        out_shape=jax.ShapeDtypeStruct((GROUPS, HEAD_DIM, TOK), BF16),
        scratch_shapes=SPATIAL_SCRATCH,
        compiler_params=PARAMS,
        name="first_frame",
    )(resident(packed))


def second_frame(queries, packed, far, after):
    return pl.pallas_call(
        second_kernel,
        in_specs=[VMEM, VMEM, VMEM] + [ANY] * len(after),
        out_specs=VMEM,
        out_shape=jax.ShapeDtypeStruct((GROUPS, 2, HEAD_DIM, TOK), BF16),
        scratch_shapes=SPATIAL_SCRATCH,
        compiler_params=PARAMS,
        name="second_frame",
    )(resident(queries), resident(packed), resident(far), *after)


def spread_kernel(x_ref, q_ref, kv_ref, after_ref, *o_refs):
    del after_ref
    for step, o_ref in enumerate(o_refs):
        column = lax.rem(x_ref[0] + step, CHIPS) * WIDE
        rows = pl.ds(pl.multiple_of(column, WIDE), WIDE)
        for frame in range(2):
            o_ref[frame] = q_ref[frame, rows]
            for part in range(2):
                o_ref[2 + 2 * frame + part] = kv_ref[frame, part, rows]


def spread(x, query, kv, after):
    return pl.pallas_call(
        spread_kernel,
        in_specs=[SMEM, VMEM, VMEM, ANY],
        out_specs=[VMEM] * CHIPS,
        out_shape=[jax.ShapeDtypeStruct((6, WIDE, D), BF16)] * CHIPS,
        compiler_params=PARAMS,
        name="spread",
    )(x, query, kv, after)


def swap_kernel(core_ref, *refs):
    blocks, o_ref = refs[:CHIPS], refs[CHIPS]
    half = pl.ds(pl.multiple_of((1 - core_ref[0]) * SHARE, SHARE), SHARE)
    for step in range(CHIPS):
        for row in range(6):
            o_ref[step, row] = blocks[step][row, half]


def swap_half(core, blocks):
    return pl.pallas_call(
        swap_kernel,
        in_specs=[SMEM] + [VMEM] * CHIPS,
        out_specs=VMEM,
        out_shape=jax.ShapeDtypeStruct((CHIPS, 6, SHARE, D), BF16),
        compiler_params=PARAMS,
        name="swap_half",
    )(core, *[resident(block) for block in blocks])


def temporal_kernel(core_ref, x_ref, *refs):
    blocks, other_ref = refs[:CHIPS], refs[CHIPS]
    o_ref, crossing_ref, query, key, value = refs[CHIPS + 1 :]
    half = pl.ds(pl.multiple_of(core_ref[0] * SHARE, SHARE), SHARE)
    rows = PLEN * SHARE
    token_of_row = lax.broadcasted_iota(jnp.int32, (rows, rows), 0) % SHARE
    token_of_column = lax.broadcasted_iota(jnp.int32, (rows, rows), 1) % SHARE
    same_token = token_of_row == token_of_column

    for step in range(CHIPS):
        for side in range(2):
            for frame in range(2):
                start = ((step * 2 + side) * 2 + frame) * SHARE
                place = slice(start, start + SHARE)
                for to, row in ((query, frame), (key, 2 + 2 * frame), (value, 3 + 2 * frame)):
                    to[place] = other_ref[step, row] if side else blocks[step][row, half]

    tiles = [jnp.zeros((rows, 128), F32) for _ in range(D // 128)]
    for head in range(HEADS):
        first, last = head * HEAD_DIM // 128, ((head + 1) * HEAD_DIM - 1) // 128
        low, high = first * 128, (last + 1) * 128
        lane = lax.broadcasted_iota(jnp.int32, (rows, high - low), 1) + low
        mine = (lane >= head * HEAD_DIM) & (lane < (head + 1) * HEAD_DIM)
        q = jnp.where(mine, query[:, low:high], 0).astype(BF16)
        v = jnp.where(mine, value[:, low:high], 0).astype(BF16)
        scores = matmul(q, key[:, low:high], 1, 1) * SCALE
        scores = jnp.where(same_token, scores, -1e30)
        weights = jnp.exp2(scores - jnp.max(scores, axis=1, keepdims=True))
        row_sum = jnp.sum(weights, axis=1, keepdims=True)
        summed = matmul(weights.astype(BF16), v, 1, 0) / row_sum
        for tile in range(first, last + 1):
            tiles[tile] += summed[:, tile * 128 - low : tile * 128 - low + 128]
    for step in range(CHIPS):
        for side in range(2):
            core = core_ref[0] if side == 0 else 1 - core_ref[0]
            ahead = (step + 1) % CHIPS
            even = jnp.where(core == 1, 4 * step + 1, 4 * ahead + 3)
            odd = 4 * step + 2 * core
            for frame, slot in enumerate((even, odd)):
                row = ((step * 2 + side) * 2 + frame) * SHARE
                for tile in range(D // 128):
                    o_ref[slot, :, tile * 128 : (tile + 1) * 128] = tiles[tile][
                        row : row + SHARE
                    ].astype(BF16)


    crossing_ref[...] = o_ref[crossing_slot(x_ref[0])]


def crossing_slot(x):
    return 4 * lax.rem(x + 1, CHIPS) + 3


def temporal_share(core, x, blocks, other):
    return pl.pallas_call(
        temporal_kernel,
        in_specs=[SMEM, SMEM] + [VMEM] * (CHIPS + 1),
        out_specs=[VMEM, VMEM],
        out_shape=[
            jax.ShapeDtypeStruct((PLEN, SHARE, D), BF16),
            jax.ShapeDtypeStruct((SHARE, D), BF16),
        ],
        scratch_shapes=[pltpu.VMEM((PLEN * SHARE, D), BF16)] * 3,
        compiler_params=PARAMS,
        name="temporal",
    )(core, x, *[resident(block) for block in blocks], resident(other))


def back_kernel(x_ref, timely_ref, passed_ref, *o_refs):
    slot = crossing_slot(x_ref[0])
    for step, o_ref in enumerate(o_refs):
        o_ref[...] = timely_ref[4 * step : 4 * step + 4]

        @pl.when(slot == 4 * step + 3)
        def _():
            o_ref[3] = passed_ref[...]


def to_send_back(x, timely, passed):
    return pl.pallas_call(
        back_kernel,
        in_specs=[SMEM, VMEM, VMEM],
        out_specs=[VMEM] * CHIPS,
        out_shape=[jax.ShapeDtypeStruct((4, SHARE, D), BF16)] * CHIPS,
        compiler_params=PARAMS,
        name="to_send_back",
    )(x, timely, resident(passed))


def return_kernel(core_ref, *refs):
    start = 2 * (1 - core_ref[0])
    for step in range(CHIPS):
        for slot in range(2):
            refs[CHIPS][step, slot] = refs[step][start + slot]


def return_half(core, back):
    return pl.pallas_call(
        return_kernel,
        in_specs=[SMEM] + [VMEM] * CHIPS,
        out_specs=VMEM,
        out_shape=jax.ShapeDtypeStruct((CHIPS, 2, SHARE, D), BF16),
        compiler_params=PARAMS,
        name="return_half",
    )(core, *[resident(block) for block in back])


def combine_kernel(core_ref, x_ref, space_ref, *refs):
    back, (theirs_ref, time_ref, level_ref, index_ref) = refs[:CHIPS], refs[CHIPS : CHIPS + 4]
    gs_ref, gt_ref, table_ref, o_ref, times = refs[CHIPS + 4 :]
    core = core_ref[0]
    for step in range(CHIPS):
        column = lax.rem(x_ref[0] + step, CHIPS) * WIDE
        here = pl.ds(pl.multiple_of(column + core * SHARE, SHARE), SHARE)
        there = pl.ds(pl.multiple_of(column + (1 - core) * SHARE, SHARE), SHARE)
        for slot in range(2):
            times[slot, here] = back[step][2 * core + slot]
            times[slot, there] = theirs_ref[step, slot]
    rows = time_ref[1], index_ref[0]
    levels = level_ref[1], index_ref[1]
    for slot in range(2):
        space = space_ref[:, slot].astype(F32).reshape(D, TOK).T
        timely = times[slot].astype(F32)
        gate_space = gs_ref[pl.ds(rows[slot], 1), :]
        gate_time = gt_ref[pl.ds(rows[slot], 1), :]
        size = table_ref[levels[slot]]
        o_ref[slot] = (size * (gate_space * space + gate_time * timely)).astype(BF16)


def combine(core, x, space, back, theirs, timestep, noise_level, indices, spatial_gate, temporal_gate, step_table):
    return pl.pallas_call(
        combine_kernel,
        in_specs=[SMEM, SMEM] + [VMEM] * (CHIPS + 2) + [SMEM] * 3 + [VMEM, VMEM, SMEM],
        out_specs=VMEM,
        out_shape=jax.ShapeDtypeStruct((2, TOK, D), BF16),
        scratch_shapes=[pltpu.VMEM((2, TOK, D), BF16)],
        compiler_params=PARAMS,
        name="combine",
    )(
        core, x, resident(space), *[resident(block) for block in back], resident(theirs),
        timestep, noise_level, indices, spatial_gate, temporal_gate, step_table,
    )


def shift(block, axes, distance):
    size = lax.axis_size(axes)
    return lax.ppermute(block, axes, [(i, (i + distance) % size) for i in range(size)])


def exchange(block, axes):
    return lax.all_to_all(block, axes, 0, 0)


def per_device(
    spatial_qkv,
    temporal_query,
    temporal_kv,
    timestep,
    noise_level,
    spatial_gate,
    temporal_gate,
    step_table,
):
    x, core = lax.axis_index("x"), lax.axis_index("core")
    x_arg, core_arg = x[None].astype(jnp.int32), core[None].astype(jnp.int32)
    packed, indices = pack(
        ((0, 0), (0, 1), (0, 2), (1, 0)), spatial_qkv, timestep, noise_level, ()
    )
    early = exchange(packed, "sp")
    indices = shift(indices, QUEUE, -1)
    blocks = spread(x_arg, temporal_query, temporal_kv, packed)
    blocks = [blocks[0]] + [shift(blocks[k], "x", k) for k in range(1, CHIPS)]
    packed, _ = pack(
        ((1, 1), (1, 2)), spatial_qkv, timestep, noise_level, (indices, *blocks[1:])
    )
    late = exchange(packed, "sp")
    other = shift(swap_half(core_arg, blocks), "core", 1)
    timely, passed = temporal_share(core_arg, x_arg, blocks, other)
    passed = shift(passed, "part", -1)
    back = to_send_back(x_arg, timely, passed)
    far = shift(first_frame(early), QUEUE, -1)
    space = exchange(second_frame(early, late, far, (back[0],)), "sp")
    back = [back[0]] + [shift(back[k], "x", -k) for k in range(1, CHIPS)]
    theirs = shift(return_half(core_arg, back), "core", 1)
    return combine(
        core_arg, x_arg, space, back, theirs, timestep, noise_level, indices,
        spatial_gate, temporal_gate, step_table,
    )


def solution(mesh):
    inner = Mesh(
        mesh.devices.reshape(
            mesh.shape["queue"] // (2 * CHIPS), CHIPS, 2, mesh.shape["sp"]
        ),
        QUEUE + ("sp",),
    )
    return jax.shard_map(
        per_device,
        mesh=inner,
        in_specs=(
            P(QUEUE, None, "sp", None),
            P(QUEUE, "sp", None),
            P(QUEUE, None, "sp", None),
            P(QUEUE),
            P(QUEUE),
            P(),
            P(),
            P(),
        ),
        out_specs=P(QUEUE, "sp", None),
        check_vma=False,
    )
```

time: 178 us -> 130 us (0.73)
  the two profiles are of different devices: /device:TPU:39 before, /device:TPU:1 now
where the time goes in v2:
time: 130 us
  starting transfers between devices  71.2 us (55%)
  Pallas kernels  30.7 us (24%)
  waiting for transfers between devices  24.8 us (19%)
  local copies, waits for them, and re-layouts  2.7 us (2%)
    ppermute x11, starting transfers between devices, shift(): lax.ppermute(block, axes, [(i, (i + distance) % size) for i in range(size)])  47.5 us
    ppermute x11, waiting for transfers between devices, shift(): lax.ppermute(block, axes, [(i, (i + distance) % size) for i in range(size)])  24.8 us
    all_to_all x3, starting transfers between devices, exchange(): return lax.all_to_all(block, axes, 0, 0)  23.7 us
    pallas_call x1, Pallas kernels, second_frame(): pl.pallas_call(second_kernel, in_specs=[VMEM, VMEM, VMEM] + [ANY] * len(a...  6.75 us
    pallas_call x1, Pallas kernels, first_frame(): pl.pallas_call(first_kernel, in_specs=[VMEM], out_specs=VMEM, out_shape=j...  6.66 us
    pallas_call x2, Pallas kernels, pack(): pl.pallas_call(functools.partial(pack_kernel, parts), in_specs=[VMEM, SME...  5.46 us
    pallas_call x1, Pallas kernels, temporal_share(): pl.pallas_call(temporal_kernel, in_specs=[SMEM, SMEM] + [VMEM] * (CHIPS +...  2.99 us
    pallas_call x1, Pallas kernels, spread(): pl.pallas_call(spread_kernel, in_specs=[SMEM, VMEM, VMEM, ANY], out_specs...  2.79 us
  transfers between devices with their start and end apart: 14, of which 5 were waited for; matrix products, arithmetic and copies ran while one was open for 0% of the time, Pallas kernels for 15%

profile of v2, /device:TPU:1, one launch (start us, length us, event | category | flops | bytes accessed | tf_op | source)
XLA Modules:
  0.0 129.6 jit_solution(10116754872570231293)
XLA Ops:
  0.0 2.9 %pack.2 = (bf16[16,4,72,128]{3,2,1,0:T(8,128)(2,1)}, s32[2]{0:T(128)}) custom-call(bf16[2,3,128,1152]{3,2,1,0:T(8,128)(2,1)} %x_ref.3, s32[2]{0:T(128)} %refs_5_.1, s32[2]{0:T(128)} %refs_6_.1), custom_call_target="tpu_custom_call" | custom-call | tf_op jit(solution)/shard_map/pack/pallas_call | solution.py:62
  2.9 9.2 %all-to-all-start = ((bf16[16,4,72,128]{3,2,1,0:T(8,128)(2,1)}), bf16[16,4,72,128]{3,2,1,0:T(8,128)(2,1)S(1)}, u32[]{:S(2)}, u32[]{:S(2)}) async-start(bf16[16,4,72,128]{3,2,1,0:T(8,128)(2,1)} %get-tuple-element.18.after_ref), calls=%async_computation | async-start | bytes 2359296 | tf_op jit(solution)/shard_map/all_to_all | solution.py:333
  12.1 0.0 copy-start.12
  12.1 2.8 %spread.1 = (bf16[6,32,1152]{2,1,0:T(8,128)(2,1)}, bf16[6,32,1152]{2,1,0:T(8,128)(2,1)}, bf16[6,32,1152]{2,1,0:T(8,128)(2,1)}, bf16[6,32,1152]{2,1,0:T(8,128)(2,1)}) custom-call(s32[1]{0:T(128)} %bitcast.1.x_ref, bf16[2,128,1152]{2,1,0:T(8,128)(2,1)} %q_ref.1, bf16[2,2,128,1152]{3,2,1,0:T(8,128)(2,1)} %kv_ref.1, ...), custom_call_target="tpu_custom_call" | custom-call | tf_op jit(solution)/shard_map/spread/pallas_call | solution.py:154
  14.9 3.1 %collective-permute-start.1 = (bf16[6,32,1152]{2,1,0:T(8,128)(2,1)}, bf16[6,32,1152]{2,1,0:T(8,128)(2,1)S(1)}, u32[]{:S(2)}, u32[]{:S(2)}) collective-permute-start(bf16[6,32,1152]{2,1,0:T(8,128)(2,1)} %get-tuple-element.20), channel_id=1, source_target_pairs={{0,32},{32,64},{64,96},{96,0},{1,33},{33,65},{65,97},{97,1},{2,34}... | collective-permute-start | bytes 1327112 | tf_op jit(solution)/shard_map/ppermute | solution.py:329
  18.0 4.4 %collective-permute-start.2 = (bf16[6,32,1152]{2,1,0:T(8,128)(2,1)}, bf16[6,32,1152]{2,1,0:T(8,128)(2,1)S(1)}, u32[]{:S(2)}, u32[]{:S(2)}) collective-permute-start(bf16[6,32,1152]{2,1,0:T(8,128)(2,1)} %get-tuple-element.21), channel_id=1, source_target_pairs={{0,64},{32,96},{64,0},{96,32},{1,65},{33,97},{65,1},{97,33},{2,66}... | collective-permute-start | bytes 1327112 | tf_op jit(solution)/shard_map/ppermute | solution.py:329
  22.4 3.1 %collective-permute-start.3 = (bf16[6,32,1152]{2,1,0:T(8,128)(2,1)}, bf16[6,32,1152]{2,1,0:T(8,128)(2,1)S(1)}, u32[]{:S(2)}, u32[]{:S(2)}) collective-permute-start(bf16[6,32,1152]{2,1,0:T(8,128)(2,1)} %get-tuple-element.22), channel_id=1, source_target_pairs={{0,96},{32,0},{64,32},{96,64},{1,97},{33,1},{65,33},{97,65},{2,98}... | collective-permute-start | bytes 1327112 | tf_op jit(solution)/shard_map/ppermute | solution.py:329
  25.5 0.0 copy-done.12
  25.5 3.7 %collective-permute-start = (s32[2]{0:T(128)S(1)}, s32[2]{0:T(128)S(1)}, u32[]{:S(2)}, u32[]{:S(2)}) collective-permute-start(s32[2]{0:T(128)S(1)} %copy-done.12), channel_id=1, source_target_pairs={{0,496},{16,0},{32,16},{48,32},{64,48},{80,64},{96,80},{112,96},{1... | collective-permute-start | bytes 32 | tf_op jit(solution)/shard_map/ppermute | solution.py:329
  29.2 13.2 %collective-permute-done.refs_0_.refs_7_ = s32[2]{0:T(128)S(1)} collective-permute-done((s32[2]{0:T(128)S(1)}, s32[2]{0:T(128)S(1)}, u32[]{:S(2)}, u32[]{:S(2)}) %collective-permute-start) | collective-permute-done | bytes 40 | tf_op jit(solution)/shard_map/ppermute | solution.py:329
  42.4 0.0 collective-permute-done.1.refs_1_
  42.4 0.0 collective-permute-done.2.refs_2_
  42.4 0.0 copy-start.2
  42.4 0.0 collective-permute-done.3.refs_3_
  42.4 0.5 copy-done.8
  42.9 0.3 copy-done
  43.2 0.2 copy-done.2
  43.3 0.8 copy-done.4
  44.1 2.6 %pack.3 = (bf16[16,2,72,128]{3,2,1,0:T(8,128)(2,1)}, s32[2]{0:T(128)}) custom-call(bf16[2,3,128,1152]{3,2,1,0:T(8,128)(2,1)} %x_ref.3, s32[2]{0:T(128)} %refs_5_.1, s32[2]{0:T(128)} %refs_6_.1, s32[2]{0:T(128)} %copy-done.8, bf16[6,32,1152]{2,1,0:T(8,128)(2,1)} %copy-done, bf16[6,32,1152]{2,1,0:T(8,128)(2,1)} %copy-done.2, bf16[6,32,1152]{2,1,0:T(8,128)(2,1)} %copy-done.4), custom_call_target="tpu_custom_call" | custom-call | tf_op jit(solution)/shard_map/pack/pallas_call | solution.py:62
  46.7 0.0 copy-start.1
  46.7 0.0 copy-start.3
  46.7 0.0 all-to-all-done.x_ref.q_ref
  46.7 7.1 %all-to-all-start.1 = ((bf16[16,2,72,128]{3,2,1,0:T(8,128)(2,1)}), bf16[16,2,72,128]{3,2,1,0:T(8,128)(2,1)S(1)}, u32[]{:S(2)}, u32[]{:S(2)}) async-start(bf16[16,2,72,128]{3,2,1,0:T(8,128)(2,1)} %get-tuple-element.23), calls=%async_computation.1 | async-start | bytes 1179648 | tf_op jit(solution)/shard_map/all_to_all | solution.py:333
  53.8 1.0 copy-done.5
  54.8 1.0 swap_half.1
  55.8 1.9 %collective-permute-start.5 = (bf16[4,6,16,1152]{3,2,1,0:T(8,128)(2,1)}, bf16[4,6,16,1152]{3,2,1,0:T(8,128)(2,1)S(1)}, u32[]{:S(2)}, u32[]{:S(2)}) collective-permute-start(bf16[4,6,16,1152]{3,2,1,0:T(8,128)(2,1)} %swap_half.1), channel_id=1, source_target_pairs={{0,16},{16,0},{1,17},{17,1},{2,18},{18,2},{3,19},{19,3},{4,20},{20... | collective-permute-start | bytes 2654216 | tf_op jit(solution)/shard_map/ppermute | solution.py:329
  57.7 6.7 %first_frame.1 = bf16[16,72,128]{2,1,0:T(8,128)(2,1)} custom-call(bf16[16,4,72,128]{3,2,1,0:T(8,128)(2,1)S(1)} %all-to-all-done.x_ref.q_ref), custom_call_target="tpu_custom_call" | custom-call | tf_op jit(solution)/shard_map/first_frame/pallas_call | solution.py:119
  64.4 2.4 %collective-permute-start.4 = (bf16[16,72,128]{2,1,0:T(8,128)(2,1)}, bf16[16,72,128]{2,1,0:T(8,128)(2,1)S(1)}, u32[]{:S(2)}, u32[]{:S(2)}) collective-permute-start(bf16[16,72,128]{2,1,0:T(8,128)(2,1)} %first_frame.1), channel_id=1, source_target_pairs={{0,496},{16,0},{32,16},{48,32},{64,48},{80,64},{96,80},{112,96},{1... | collective-permute-start | bytes 884744 | tf_op jit(solution)/shard_map/ppermute | solution.py:329
  66.8 0.0 collective-permute-done.5.refs_4_
  66.8 3.0 %temporal.1 = (bf16[16,16,1152]{2,1,0:T(8,128)(2,1)}, bf16[16,1152]{1,0:T(8,128)(2,1)}) custom-call(s32[1]{0:T(128)} %bitcast.core_ref, s32[1]{0:T(128)} %bitcast.1.x_ref, bf16[6,32,1152]{2,1,0:T(8,128)(2,1)S(1)} %copy-done.6, bf16[6,32,1152]{2,1,0:T(8,128)(2,1)S(1)} %copy-done.1, bf16[6,32,1152]{2,1,0:T(8,128)(2,1)S(1)} %copy-done.3, ...), custom_call_target="tpu_custom_call" | custom-call | tf_op jit(solution)/shard_map/temporal/pallas_call | solution.py:237
  69.8 9.7 %collective-permute-start.6 = (bf16[16,1152]{1,0:T(8,128)(2,1)}, bf16[16,1152]{1,0:T(8,128)(2,1)S(1)}, u32[]{:S(2)}, u32[]{:S(2)}) collective-permute-start(bf16[16,1152]{1,0:T(8,128)(2,1)} %get-tuple-element.26), channel_id=1, source_target_pairs={{0,384},{128,0},{256,128},{384,256},{1,385},{129,1},{257,129},{385... | collective-permute-start | bytes 110600 | tf_op jit(solution)/shard_map/ppermute | solution.py:329
  79.6 3.7 %collective-permute-done.6.passed_ref = bf16[16,1152]{1,0:T(8,128)(2,1)S(1)} collective-permute-done((bf16[16,1152]{1,0:T(8,128)(2,1)}, bf16[16,1152]{1,0:T(8,128)(2,1)S(1)}, u32[]{:S(2)}, u32[]{:S(2)}) %collective-permute-start.6) | collective-permute-done | bytes 36896 | tf_op jit(solution)/shard_map/ppermute | solution.py:329
  83.3 2.1 %to_send_back.1 = (bf16[4,16,1152]{2,1,0:T(8,128)(2,1)}, bf16[4,16,1152]{2,1,0:T(8,128)(2,1)}, bf16[4,16,1152]{2,1,0:T(8,128)(2,1)}, bf16[4,16,1152]{2,1,0:T(8,128)(2,1)}) custom-call(s32[1]{0:T(128)} %bitcast.1.x_ref, bf16[16,16,1152]{2,1,0:T(8,128)(2,1)} %get-tuple-element.25.timely_ref, bf16[16,1152]{1,0:T(8,128)(2,1)S(1)} %collective-permute-done.6.passed_ref), custom_call_target="tpu_custom_call" | custom-call | tf_op jit(solution)/shard_map/to_send_back/pallas_call | solution.py:262
  85.4 0.0 all-to-all-done.1.kv_ref
  85.4 0.0 collective-permute-done.4.far_ref
  85.5 6.8 %second_frame.1 = bf16[16,2,72,128]{3,2,1,0:T(8,128)(2,1)} custom-call(bf16[16,4,72,128]{3,2,1,0:T(8,128)(2,1)S(1)} %all-to-all-done.x_ref.q_ref, bf16[16,2,72,128]{3,2,1,0:T(8,128)(2,1)S(1)} %all-to-all-done.1.kv_ref, bf16[16,72,128]{2,1,0:T(8,128)(2,1)S(1)} %collective-permute-done.4.far_ref, bf16[4,16,1152]{2,1,0:T(8,128)(2,1)} %get-tuple-element.27.refs_0_), custom_call_target="tpu_custom_call" | custom-call | tf_op jit(solution)/shard_map/second_frame/pallas_call | solution.py:131
  92.2 7.4 %all-to-all-start.2 = ((bf16[16,2,72,128]{3,2,1,0:T(8,128)(2,1)}), bf16[16,2,72,128]{3,2,1,0:T(8,128)(2,1)S(1)}, u32[]{:S(2)}, u32[]{:S(2)}) async-start(bf16[16,2,72,128]{3,2,1,0:T(8,128)(2,1)} %second_frame.1), calls=%async_computation.2 | async-start | bytes 1179648 | tf_op jit(solution)/shard_map/all_to_all | solution.py:333
  99.6 10.8 %collective-permute-start.7 = (bf16[4,16,1152]{2,1,0:T(8,128)(2,1)S(1)}, bf16[4,16,1152]{2,1,0:T(8,128)(2,1)S(1)}, u32[]{:S(2)}, u32[]{:S(2)}) collective-permute-start(bf16[4,16,1152]{2,1,0:T(8,128)(2,1)S(1)} %copy-done.11), channel_id=1, source_target_pairs={{0,96},{32,0},{64,32},{96,64},{1,97},{33,1},{65,33},{97,65},{2,98}... | collective-permute-start | bytes 442376 | tf_op jit(solution)/shard_map/ppermute | solution.py:329
  110.4 1.9 %collective-permute-start.8 = (bf16[4,16,1152]{2,1,0:T(8,128)(2,1)S(1)}, bf16[4,16,1152]{2,1,0:T(8,128)(2,1)S(1)}, u32[]{:S(2)}, u32[]{:S(2)}) collective-permute-start(bf16[4,16,1152]{2,1,0:T(8,128)(2,1)S(1)} %copy-done.10), channel_id=1, source_target_pairs={{0,64},{32,96},{64,0},{96,32},{1,65},{33,97},{65,1},{97,33},{2,66}... | collective-permute-start | bytes 442376 | tf_op jit(solution)/shard_map/ppermute | solution.py:329
  112.4 2.5 %collective-permute-start.9 = (bf16[4,16,1152]{2,1,0:T(8,128)(2,1)S(1)}, bf16[4,16,1152]{2,1,0:T(8,128)(2,1)S(1)}, u32[]{:S(2)}, u32[]{:S(2)}) collective-permute-start(bf16[4,16,1152]{2,1,0:T(8,128)(2,1)S(1)} %copy-done.9), channel_id=1, source_target_pairs={{0,32},{32,64},{64,96},{96,0},{1,33},{33,65},{65,97},{97,1},{2,34}... | collective-permute-start | bytes 442376 | tf_op jit(solution)/shard_map/ppermute | solution.py:329
  114.9 0.0 collective-permute-done.7.refs_1_
  114.9 2.9 %collective-permute-done.8.refs_2_ = bf16[4,16,1152]{2,1,0:T(8,128)(2,1)S(1)} collective-permute-done((bf16[4,16,1152]{2,1,0:T(8,128)(2,1)S(1)}, bf16[4,16,1152]{2,1,0:T(8,128)(2,1)S(1)}, u32[]{:S(2)}, u32[]{:S(2)}) %collective-permute-start.8) | collective-permute-done | bytes 147488 | tf_op jit(solution)/shard_map/ppermute | solution.py:329
  117.8 3.5 %collective-permute-done.9.refs_3_ = bf16[4,16,1152]{2,1,0:T(8,128)(2,1)S(1)} collective-permute-done((bf16[4,16,1152]{2,1,0:T(8,128)(2,1)S(1)}, bf16[4,16,1152]{2,1,0:T(8,128)(2,1)S(1)}, u32[]{:S(2)}, u32[]{:S(2)}) %collective-permute-start.9) | collective-permute-done | bytes 147488 | tf_op jit(solution)/shard_map/ppermute | solution.py:329
  121.3 0.7 return_half.1
  122.0 4.0 %collective-permute-start.10 = (bf16[4,2,16,1152]{3,2,1,0:T(8,128)(2,1)}, bf16[4,2,16,1152]{3,2,1,0:T(8,128)(2,1)S(1)}, u32[]{:S(2)}, u32[]{:S(2)}) collective-permute-start(bf16[4,2,16,1152]{3,2,1,0:T(8,128)(2,1)} %return_half.1), channel_id=1, source_target_pairs={{0,16},{16,0},{1,17},{17,1},{2,18},{18,2},{3,19},{19,3},{4,20},{20... | collective-permute-start | bytes 884744 | tf_op jit(solution)/shard_map/ppermute | solution.py:329
  126.1 1.4 %collective-permute-done.10.refs_4_ = bf16[4,2,16,1152]{3,2,1,0:T(8,128)(2,1)S(1)} collective-permute-done((bf16[4,2,16,1152]{3,2,1,0:T(8,128)(2,1)}, bf16[4,2,16,1152]{3,2,1,0:T(8,128)(2,1)S(1)}, u32[]{:S(2)}, u32[]{:S(2)}) %collective-permute-start.10) | collective-permute-done | bytes 294944 | tf_op jit(solution)/shard_map/ppermute | solution.py:329
  127.5 0.0 all-to-all-done.2.space_ref
  127.5 2.2 %combine.1 = bf16[2,128,1152]{2,1,0:T(8,128)(2,1)} custom-call(s32[1]{0:T(128)} %bitcast.core_ref, s32[1]{0:T(128)} %bitcast.1.x_ref, bf16[16,2,72,128]{3,2,1,0:T(8,128)(2,1)S(1)} %all-to-all-done.2.space_ref, bf16[4,16,1152]{2,1,0:T(8,128)(2,1)S(1)} %copy-done.7, bf16[4,16,1152]{2,1,0:T(8,128)(2,1)S(1)} %collective-permute-done.7.refs_1_, ...), custom_call_target="tpu_custom_call" | custom-call | tf_op jit(solution)/shard_map/combine/pallas_call | solution.py:313
  (16 shorter events, 0.0 us)
Async XLA Ops:
  2.9 43.8 %all-to-all-start = ((bf16[16,4,72,128]{3,2,1,0:T(8,128)(2,1)}), bf16[16,4,72,128]{3,2,1,0:T(8,128)(2,1)S(1)}, u32[]{:S(2)}, u32[]{:S(2)}) async-start(bf16[16,4,72,128]{3,2,1,0:T(8,128)(2,1)} %get-tuple-element.18.after_ref), calls=%async_computation | async-start | bytes 2359296 | tf_op jit(solution)/shard_map/all_to_all | solution.py:333
  12.1 13.3 %copy-start.12 = (s32[2]{0:T(128)S(1)}, s32[2]{0:T(128)}, u32[]{:S(2)}) copy-start(s32[2]{0:T(128)} %get-tuple-element.19) | copy-start | bytes 28
  14.9 27.5 %collective-permute-start.1 = (bf16[6,32,1152]{2,1,0:T(8,128)(2,1)}, bf16[6,32,1152]{2,1,0:T(8,128)(2,1)S(1)}, u32[]{:S(2)}, u32[]{:S(2)}) collective-permute-start(bf16[6,32,1152]{2,1,0:T(8,128)(2,1)} %get-tuple-element.20), channel_id=1, source_target_pairs={{0,32},{32,64},{64,96},{96,0},{1,33},{33,65},{65,97},{97,1},{2,34}... | collective-permute-start | bytes 1327112 | tf_op jit(solution)/shard_map/ppermute | solution.py:329
  18.0 24.4 %collective-permute-start.2 = (bf16[6,32,1152]{2,1,0:T(8,128)(2,1)}, bf16[6,32,1152]{2,1,0:T(8,128)(2,1)S(1)}, u32[]{:S(2)}, u32[]{:S(2)}) collective-permute-start(bf16[6,32,1152]{2,1,0:T(8,128)(2,1)} %get-tuple-element.21), channel_id=1, source_target_pairs={{0,64},{32,96},{64,0},{96,32},{1,65},{33,97},{65,1},{97,33},{2,66}... | collective-permute-start | bytes 1327112 | tf_op jit(solution)/shard_map/ppermute | solution.py:329
  22.4 20.0 %collective-permute-start.3 = (bf16[6,32,1152]{2,1,0:T(8,128)(2,1)}, bf16[6,32,1152]{2,1,0:T(8,128)(2,1)S(1)}, u32[]{:S(2)}, u32[]{:S(2)}) collective-permute-start(bf16[6,32,1152]{2,1,0:T(8,128)(2,1)} %get-tuple-element.22), channel_id=1, source_target_pairs={{0,96},{32,0},{64,32},{96,64},{1,97},{33,1},{65,33},{97,65},{2,98}... | collective-permute-start | bytes 1327112 | tf_op jit(solution)/shard_map/ppermute | solution.py:329
  25.5 16.9 %collective-permute-start = (s32[2]{0:T(128)S(1)}, s32[2]{0:T(128)S(1)}, u32[]{:S(2)}, u32[]{:S(2)}) collective-permute-start(s32[2]{0:T(128)S(1)} %copy-done.12), channel_id=1, source_target_pairs={{0,496},{16,0},{32,16},{48,32},{64,48},{80,64},{96,80},{112,96},{1... | collective-permute-start | bytes 32 | tf_op jit(solution)/shard_map/ppermute | solution.py:329
  42.4 0.5 copy-start.8
  42.4 0.8 copy-start
  42.4 0.9 copy-start.2
  43.3 0.8 copy-start.4
  44.1 9.7 %copy-start.6 = (bf16[6,32,1152]{2,1,0:T(8,128)(2,1)S(1)}, bf16[6,32,1152]{2,1,0:T(8,128)(2,1)}, u32[]{:S(2)}) copy-start(bf16[6,32,1152]{2,1,0:T(8,128)(2,1)} %get-tuple-element.24.refs_0_) | copy-start | bytes 1327108
  46.7 7.1 %copy-start.1 = (bf16[6,32,1152]{2,1,0:T(8,128)(2,1)S(1)}, bf16[6,32,1152]{2,1,0:T(8,128)(2,1)}, u32[]{:S(2)}) copy-start(bf16[6,32,1152]{2,1,0:T(8,128)(2,1)} %copy-done) | copy-start | bytes 1327108
  46.7 7.1 %copy-start.3 = (bf16[6,32,1152]{2,1,0:T(8,128)(2,1)S(1)}, bf16[6,32,1152]{2,1,0:T(8,128)(2,1)}, u32[]{:S(2)}) copy-start(bf16[6,32,1152]{2,1,0:T(8,128)(2,1)} %copy-done.2) | copy-start | bytes 1327108
  46.7 38.7 %all-to-all-start.1 = ((bf16[16,2,72,128]{3,2,1,0:T(8,128)(2,1)}), bf16[16,2,72,128]{3,2,1,0:T(8,128)(2,1)S(1)}, u32[]{:S(2)}, u32[]{:S(2)}) async-start(bf16[16,2,72,128]{3,2,1,0:T(8,128)(2,1)} %get-tuple-element.23), calls=%async_computation.1 | async-start | bytes 1179648 | tf_op jit(solution)/shard_map/all_to_all | solution.py:333
  53.8 1.0 copy-start.5
  55.8 11.0 %collective-permute-start.5 = (bf16[4,6,16,1152]{3,2,1,0:T(8,128)(2,1)}, bf16[4,6,16,1152]{3,2,1,0:T(8,128)(2,1)S(1)}, u32[]{:S(2)}, u32[]{:S(2)}) collective-permute-start(bf16[4,6,16,1152]{3,2,1,0:T(8,128)(2,1)} %swap_half.1), channel_id=1, source_target_pairs={{0,16},{16,0},{1,17},{17,1},{2,18},{18,2},{3,19},{19,3},{4,20},{20... | collective-permute-start | bytes 2654216 | tf_op jit(solution)/shard_map/ppermute | solution.py:329
  64.4 21.0 %collective-permute-start.4 = (bf16[16,72,128]{2,1,0:T(8,128)(2,1)}, bf16[16,72,128]{2,1,0:T(8,128)(2,1)S(1)}, u32[]{:S(2)}, u32[]{:S(2)}) collective-permute-start(bf16[16,72,128]{2,1,0:T(8,128)(2,1)} %first_frame.1), channel_id=1, source_target_pairs={{0,496},{16,0},{32,16},{48,32},{64,48},{80,64},{96,80},{112,96},{1... | collective-permute-start | bytes 884744 | tf_op jit(solution)/shard_map/ppermute | solution.py:329
  69.8 13.5 %collective-permute-start.6 = (bf16[16,1152]{1,0:T(8,128)(2,1)}, bf16[16,1152]{1,0:T(8,128)(2,1)S(1)}, u32[]{:S(2)}, u32[]{:S(2)}) collective-permute-start(bf16[16,1152]{1,0:T(8,128)(2,1)} %get-tuple-element.26), channel_id=1, source_target_pairs={{0,384},{128,0},{256,128},{384,256},{1,385},{129,1},{257,129},{385... | collective-permute-start | bytes 110600 | tf_op jit(solution)/shard_map/ppermute | solution.py:329
  92.2 7.4 %copy-start.11 = (bf16[4,16,1152]{2,1,0:T(8,128)(2,1)S(1)}, bf16[4,16,1152]{2,1,0:T(8,128)(2,1)}, u32[]{:S(2)}) copy-start(bf16[4,16,1152]{2,1,0:T(8,128)(2,1)} %get-tuple-element.28) | copy-start | bytes 442372
  92.2 18.2 %copy-start.10 = (bf16[4,16,1152]{2,1,0:T(8,128)(2,1)S(1)}, bf16[4,16,1152]{2,1,0:T(8,128)(2,1)}, u32[]{:S(2)}) copy-start(bf16[4,16,1152]{2,1,0:T(8,128)(2,1)} %get-tuple-element.29) | copy-start | bytes 442372
  92.2 20.2 %copy-start.9 = (bf16[4,16,1152]{2,1,0:T(8,128)(2,1)S(1)}, bf16[4,16,1152]{2,1,0:T(8,128)(2,1)}, u32[]{:S(2)}) copy-start(bf16[4,16,1152]{2,1,0:T(8,128)(2,1)} %get-tuple-element.30) | copy-start | bytes 442372
  92.2 29.1 %copy-start.7 = (bf16[4,16,1152]{2,1,0:T(8,128)(2,1)S(1)}, bf16[4,16,1152]{2,1,0:T(8,128)(2,1)}, u32[]{:S(2)}) copy-start(bf16[4,16,1152]{2,1,0:T(8,128)(2,1)} %get-tuple-element.27.refs_0_) | copy-start | bytes 442372
  92.2 35.2 %all-to-all-start.2 = ((bf16[16,2,72,128]{3,2,1,0:T(8,128)(2,1)}), bf16[16,2,72,128]{3,2,1,0:T(8,128)(2,1)S(1)}, u32[]{:S(2)}, u32[]{:S(2)}) async-start(bf16[16,2,72,128]{3,2,1,0:T(8,128)(2,1)} %second_frame.1), calls=%async_computation.2 | async-start | bytes 1179648 | tf_op jit(solution)/shard_map/all_to_all | solution.py:333
  99.6 15.3 %collective-permute-start.7 = (bf16[4,16,1152]{2,1,0:T(8,128)(2,1)S(1)}, bf16[4,16,1152]{2,1,0:T(8,128)(2,1)S(1)}, u32[]{:S(2)}, u32[]{:S(2)}) collective-permute-start(bf16[4,16,1152]{2,1,0:T(8,128)(2,1)S(1)} %copy-done.11), channel_id=1, source_target_pairs={{0,96},{32,0},{64,32},{96,64},{1,97},{33,1},{65,33},{97,65},{2,98}... | collective-permute-start | bytes 442376 | tf_op jit(solution)/shard_map/ppermute | solution.py:329
  110.4 7.4 %collective-permute-start.8 = (bf16[4,16,1152]{2,1,0:T(8,128)(2,1)S(1)}, bf16[4,16,1152]{2,1,0:T(8,128)(2,1)S(1)}, u32[]{:S(2)}, u32[]{:S(2)}) collective-permute-start(bf16[4,16,1152]{2,1,0:T(8,128)(2,1)S(1)} %copy-done.10), channel_id=1, source_target_pairs={{0,64},{32,96},{64,0},{96,32},{1,65},{33,97},{65,1},{97,33},{2,66}... | collective-permute-start | bytes 442376 | tf_op jit(solution)/shard_map/ppermute | solution.py:329
  112.4 8.9 %collective-permute-start.9 = (bf16[4,16,1152]{2,1,0:T(8,128)(2,1)S(1)}, bf16[4,16,1152]{2,1,0:T(8,128)(2,1)S(1)}, u32[]{:S(2)}, u32[]{:S(2)}) collective-permute-start(bf16[4,16,1152]{2,1,0:T(8,128)(2,1)S(1)} %copy-done.9), channel_id=1, source_target_pairs={{0,32},{32,64},{64,96},{96,0},{1,33},{33,65},{65,97},{97,1},{2,34}... | collective-permute-start | bytes 442376 | tf_op jit(solution)/shard_map/ppermute | solution.py:329
  122.0 5.4 %collective-permute-start.10 = (bf16[4,2,16,1152]{3,2,1,0:T(8,128)(2,1)}, bf16[4,2,16,1152]{3,2,1,0:T(8,128)(2,1)S(1)}, u32[]{:S(2)}, u32[]{:S(2)}) collective-permute-start(bf16[4,2,16,1152]{3,2,1,0:T(8,128)(2,1)} %return_half.1), channel_id=1, source_target_pairs={{0,16},{16,0},{1,17},{17,1},{2,18},{18,2},{3,19},{19,3},{4,20},{20... | collective-permute-start | bytes 884744 | tf_op jit(solution)/shard_map/ppermute | solution.py:329

commit v3 on v2

--- a/solution.py
+++ b/solution.py
@@ -70,6 +70,22 @@
         compiler_params=PARAMS,
         name="pack",
     )(spatial_qkv, timestep, noise_level, *after)
+
+
+def gate_kernel(*refs):
+    del refs
+
+
+def once_there(block, after):
+    return pl.pallas_call(
+        gate_kernel,
+        in_specs=[ANY] * (1 + len(after)),
+        out_specs=ANY,
+        out_shape=jax.ShapeDtypeStruct(block.shape, block.dtype),
+        input_output_aliases={0: 0},
+        compiler_params=PARAMS,
+        name="once_there",
+    )(block, *after)
 
 
 def attend(find, query, value, write):
@@ -89,22 +105,23 @@
             write(block * (QBLOCK // TOK) + j, result[:, j * TOK : (j + 1) * TOK])
 
 
-def first_kernel(x_ref, o_ref, query, value):
+def first_kernel(x_ref, *refs):
+    o_ref, query, value = refs[-3:]
+
     def write(group, result):
         o_ref[group] = result
 
     attend(lambda group, part: x_ref[group, part], query, value, write)
 
 
-def second_kernel(q_ref, kv_ref, far_ref, *refs):
+def second_kernel(q_ref, kv_ref, *refs):
     o_ref, query, value = refs[-3:]
 
     def find(group, part):
         return kv_ref[group, part - 1] if part else q_ref[group, 3]
 
     def write(group, result):
-        o_ref[group, 0] = result
-        o_ref[group, 1] = far_ref[group]
+        o_ref[group] = result
 
     attend(find, query, value, write)
 
@@ -115,28 +132,46 @@
 ]
 
 
-def first_frame(packed):
+def first_frame(packed, after):
     return pl.pallas_call(
         first_kernel,
-        in_specs=[VMEM],
-        out_specs=VMEM,
-        out_shape=jax.ShapeDtypeStruct((GROUPS, HEAD_DIM, TOK), BF16),
+        in_specs=[VMEM] + [ANY] * len(after),
+        out_specs=VMEM,
+        out_shape=pltpu.VMEM((GROUPS, HEAD_DIM, TOK), BF16),
         scratch_shapes=SPATIAL_SCRATCH,
         compiler_params=PARAMS,
         name="first_frame",
-    )(resident(packed))
-
-
-def second_frame(queries, packed, far, after):
+    )(resident(packed), *after)
+
+
+def second_frame(queries, packed, after):
     return pl.pallas_call(
         second_kernel,
+        in_specs=[VMEM, VMEM] + [ANY] * len(after),
+        out_specs=VMEM,
+        out_shape=pltpu.VMEM((GROUPS, HEAD_DIM, TOK), BF16),
+        scratch_shapes=SPATIAL_SCRATCH,
+        compiler_params=PARAMS,
+        name="second_frame",
+    )(resident(queries), resident(packed), *after)
+
+
+def beside_kernel(near_ref, far_ref, crossed_ref, *refs):
+    o_ref = refs[-1]
+    for group in range(GROUPS):
+        o_ref[group, 0] = near_ref[group]
+        o_ref[group, 1] = far_ref[group] + crossed_ref[group]
+
+
+def beside(near, far, crossed, after):
+    return pl.pallas_call(
+        beside_kernel,
         in_specs=[VMEM, VMEM, VMEM] + [ANY] * len(after),
         out_specs=VMEM,
         out_shape=jax.ShapeDtypeStruct((GROUPS, 2, HEAD_DIM, TOK), BF16),
-        scratch_shapes=SPATIAL_SCRATCH,
-        compiler_params=PARAMS,
-        name="second_frame",
-    )(resident(queries), resident(packed), resident(far), *after)
+        compiler_params=PARAMS,
+        name="beside",
+    )(resident(near), resident(far), resident(crossed), *after)
 
 
 def spread_kernel(x_ref, q_ref, kv_ref, after_ref, *o_refs):
@@ -239,8 +274,8 @@
         in_specs=[SMEM, SMEM] + [VMEM] * (CHIPS + 1),
         out_specs=[VMEM, VMEM],
         out_shape=[
-            jax.ShapeDtypeStruct((PLEN, SHARE, D), BF16),
-            jax.ShapeDtypeStruct((SHARE, D), BF16),
+            pltpu.VMEM((PLEN, SHARE, D), BF16),
+            pltpu.VMEM((SHARE, D), BF16),
         ],
         scratch_shapes=[pltpu.VMEM((PLEN * SHARE, D), BF16)] * 3,
         compiler_params=PARAMS,
@@ -248,7 +283,8 @@
     )(core, x, *[resident(block) for block in blocks], resident(other))
 
 
-def back_kernel(x_ref, timely_ref, passed_ref, *o_refs):
+def back_kernel(x_ref, timely_ref, passed_ref, *refs):
+    o_refs = refs[-CHIPS:]
     slot = crossing_slot(x_ref[0])
     for step, o_ref in enumerate(o_refs):
         o_ref[...] = timely_ref[4 * step : 4 * step + 4]
@@ -258,15 +294,15 @@
             o_ref[3] = passed_ref[...]
 
 
-def to_send_back(x, timely, passed):
+def to_send_back(x, timely, passed, after):
     return pl.pallas_call(
         back_kernel,
-        in_specs=[SMEM, VMEM, VMEM],
+        in_specs=[SMEM, VMEM, VMEM] + [ANY] * len(after),
         out_specs=[VMEM] * CHIPS,
-        out_shape=[jax.ShapeDtypeStruct((4, SHARE, D), BF16)] * CHIPS,
+        out_shape=[pltpu.VMEM((4, SHARE, D), BF16)] * CHIPS,
         compiler_params=PARAMS,
         name="to_send_back",
-    )(x, timely, resident(passed))
+    )(x, resident(timely), resident(passed), *after)
 
 
 def return_kernel(core_ref, *refs):
@@ -329,6 +365,32 @@
     return lax.ppermute(block, axes, [(i, (i + distance) % size) for i in range(size)])
 
 
+def one_back(first, after):
+    parts, chips, cores, groups = (lax.axis_size(a) for a in QUEUE + ("sp",))
+
+    def number(part, x, core, group):
+        return (((part % parts) * chips + x) * cores + core) * groups + group
+
+    inside, aside, across = [], [], []
+    for part in range(parts):
+        for group in range(groups):
+            for member in range(1, chips * cores):
+                there = member - 1
+                inside.append(
+                    (
+                        number(part, member // cores, member % cores, group),
+                        number(part, there // cores, there % cores, group),
+                    )
+                )
+            column = group * chips // groups
+            between = number(part, column, 0, group)
+            aside.append((number(part, 0, 0, group), between))
+            across.append((between, number(part - 1, chips - 1, cores - 1, group)))
+    axes = QUEUE + ("sp",)
+    moved = once_there(resident(lax.ppermute(first, axes, aside)), after)
+    return lax.ppermute(first, axes, inside), lax.ppermute(moved, axes, across)
+
+
 def exchange(block, axes):
     return lax.all_to_all(block, axes, 0, 0)
 
@@ -351,17 +413,20 @@
     early = exchange(packed, "sp")
     indices = shift(indices, QUEUE, -1)
     blocks = spread(x_arg, temporal_query, temporal_kv, packed)
+    packed, _ = pack(
+        ((1, 1), (1, 2)), spatial_qkv, timestep, noise_level, blocks[:1]
+    )
     blocks = [blocks[0]] + [shift(blocks[k], "x", k) for k in range(1, CHIPS)]
-    packed, _ = pack(
-        ((1, 1), (1, 2)), spatial_qkv, timestep, noise_level, (indices, *blocks[1:])
-    )
-    late = exchange(packed, "sp")
-    other = shift(swap_half(core_arg, blocks), "core", 1)
+    half = swap_half(core_arg, blocks)
+    late = exchange(once_there(packed, (indices, half)), "sp")
+    other = shift(half, "core", 1)
     timely, passed = temporal_share(core_arg, x_arg, blocks, other)
     passed = shift(passed, "part", -1)
-    back = to_send_back(x_arg, timely, passed)
-    far = shift(first_frame(early), QUEUE, -1)
-    space = exchange(second_frame(early, late, far, (back[0],)), "sp")
+    first = first_frame(early, ())
+    far, crossed = one_back(first, (resident(timely),))
+    near = second_frame(early, late, (resident(timely),))
+    back = to_send_back(x_arg, timely, passed, (resident(near),))
+    space = exchange(beside(near, far, crossed, (resident(back[0]),)), "sp")
     back = [back[0]] + [shift(back[k], "x", -k) for k in range(1, CHIPS)]
     theirs = shift(return_half(core_arg, back), "core", 1)
     return combine(

time: 130 us -> 121 us (0.931)
  waiting for transfers between devices: 24.8 us -> 16.2 us
  Pallas kernels: 30.7 us -> 27.7 us
  starting transfers between devices: 71.2 us -> 72.9 us
    ppermute x11 -> x10, waiting for transfers between devices: 24.8 us -> 16.2 us  [shift(): lax.ppermute(block, axes, [(i, (i + distance) % size) for i in range(size)])]
    ppermute x11 -> x10, starting transfers between devices: 47.5 us -> 41.8 us  [shift(): lax.ppermute(block, axes, [(i, (i + distance) % size) for i in range(size)])]
    ppermute x0 -> x3, starting transfers between devices: none -> 3.97 us  [the longest x1 1.91 us: one_back(): lax.ppermute(first, axes, inside)]
    all_to_all x3, starting transfers between devices: 23.7 us -> 27.2 us  [exchange(): return lax.all_to_all(block, axes, 0, 0)]
    pallas_call x3 -> x6, Pallas kernels: 15.5 us -> 12.8 us  [the longest x1 5.92 us: first_frame(): pl.pallas_call(first_kernel, in_specs=[VMEM] + [ANY] * len(after), out_sp...]
    unnamed x26 -> x14, local copies, waits for them, and re-layouts: 2.7 us -> 2.63 us
  transfers between devices with their start and end apart: 14 -> 16, of which waited for: 5 -> 5; matrix products, arithmetic and copies ran while one was open for 0% -> 0% of each run, Pallas kernels for 15% -> 18%
where the time goes in v3:
time: 121 us; the launch traced here: 120 us
  starting transfers between devices  72.9 us (60%)
  Pallas kernels  27.7 us (23%)
  waiting for transfers between devices  16.2 us (13%)
  local copies, waits for them, and re-layouts  2.63 us (2%)
    ppermute x10, starting transfers between devices, shift(): lax.ppermute(block, axes, [(i, (i + distance) % size) for i in range(size)])  41.8 us
    all_to_all x3, starting transfers between devices, exchange(): return lax.all_to_all(block, axes, 0, 0)  27.2 us
    ppermute x10, waiting for transfers between devices, shift(): lax.ppermute(block, axes, [(i, (i + distance) % size) for i in range(size)])  16.2 us
    pallas_call x1, Pallas kernels, first_frame(): pl.pallas_call(first_kernel, in_specs=[VMEM] + [ANY] * len(after), out_sp...  5.92 us
    pallas_call x1, Pallas kernels, second_frame(): pl.pallas_call(second_kernel, in_specs=[VMEM, VMEM] + [ANY] * len(after),...  5.91 us
    pallas_call x2, Pallas kernels, pack(): pl.pallas_call(functools.partial(pack_kernel, parts), in_specs=[VMEM, SME...  5.4 us
    pallas_call x1, Pallas kernels, temporal_share(): pl.pallas_call(temporal_kernel, in_specs=[SMEM, SMEM] + [VMEM] * (CHIPS +...  2.81 us
    pallas_call x1, Pallas kernels, spread(): pl.pallas_call(spread_kernel, in_specs=[SMEM, VMEM, VMEM, ANY], out_specs...  2.77 us
  transfers between devices with their start and end apart: 16, of which 5 were waited for; matrix products, arithmetic and copies ran while one was open for 0% of the time, Pallas kernels for 18%

profile of v3, /device:TPU:1, one launch (start us, length us, event | category | flops | bytes accessed | tf_op | source)
XLA Modules:
  0.0 119.8 jit_solution(13746631572908646287)
XLA Ops:
  0.0 2.9 %pack.2 = (bf16[16,4,72,128]{3,2,1,0:T(8,128)(2,1)}, s32[2]{0:T(128)}) custom-call(bf16[2,3,128,1152]{3,2,1,0:T(8,128)(2,1)} %x_ref.3, s32[2]{0:T(128)} %refs_5_.1, s32[2]{0:T(128)} %refs_6_.1), custom_call_target="tpu_custom_call" | custom-call | tf_op jit(solution)/shard_map/pack/pallas_call | solution.py:62
  2.9 9.2 %all-to-all-start = ((bf16[16,4,72,128]{3,2,1,0:T(8,128)(2,1)}), bf16[16,4,72,128]{3,2,1,0:T(8,128)(2,1)S(1)}, u32[]{:S(2)}, u32[]{:S(2)}) async-start(bf16[16,4,72,128]{3,2,1,0:T(8,128)(2,1)} %get-tuple-element.18.after_ref), calls=%async_computation | async-start | bytes 2359296 | tf_op jit(solution)/shard_map/all_to_all | solution.py:395
  12.1 0.0 copy-start.6
  12.1 2.8 %spread.1 = (bf16[6,32,1152]{2,1,0:T(8,128)(2,1)}, bf16[6,32,1152]{2,1,0:T(8,128)(2,1)}, bf16[6,32,1152]{2,1,0:T(8,128)(2,1)}, bf16[6,32,1152]{2,1,0:T(8,128)(2,1)}) custom-call(s32[1]{0:T(128)} %bitcast.1.x_ref, bf16[2,128,1152]{2,1,0:T(8,128)(2,1)} %q_ref.1, bf16[2,2,128,1152]{3,2,1,0:T(8,128)(2,1)} %kv_ref.1, ...), custom_call_target="tpu_custom_call" | custom-call | tf_op jit(solution)/shard_map/spread/pallas_call | solution.py:189
  14.9 3.2 %collective-permute-start.1 = (bf16[6,32,1152]{2,1,0:T(8,128)(2,1)}, bf16[6,32,1152]{2,1,0:T(8,128)(2,1)S(1)}, u32[]{:S(2)}, u32[]{:S(2)}) collective-permute-start(bf16[6,32,1152]{2,1,0:T(8,128)(2,1)} %get-tuple-element.22), channel_id=1, source_target_pairs={{0,32},{32,64},{64,96},{96,0},{1,33},{33,65},{65,97},{97,1},{2,34}... | collective-permute-start | bytes 1327112 | tf_op jit(solution)/shard_map/ppermute | solution.py:365
  18.1 4.4 %collective-permute-start.2 = (bf16[6,32,1152]{2,1,0:T(8,128)(2,1)}, bf16[6,32,1152]{2,1,0:T(8,128)(2,1)S(1)}, u32[]{:S(2)}, u32[]{:S(2)}) collective-permute-start(bf16[6,32,1152]{2,1,0:T(8,128)(2,1)} %get-tuple-element.23), channel_id=1, source_target_pairs={{0,64},{32,96},{64,0},{96,32},{1,65},{33,97},{65,1},{97,33},{2,66}... | collective-permute-start | bytes 1327112 | tf_op jit(solution)/shard_map/ppermute | solution.py:365
  22.5 3.1 %collective-permute-start.3 = (bf16[6,32,1152]{2,1,0:T(8,128)(2,1)}, bf16[6,32,1152]{2,1,0:T(8,128)(2,1)S(1)}, u32[]{:S(2)}, u32[]{:S(2)}) collective-permute-start(bf16[6,32,1152]{2,1,0:T(8,128)(2,1)} %get-tuple-element.24), channel_id=1, source_target_pairs={{0,96},{32,0},{64,32},{96,64},{1,97},{33,1},{65,33},{97,65},{2,98}... | collective-permute-start | bytes 1327112 | tf_op jit(solution)/shard_map/ppermute | solution.py:365
  25.6 3.7 %collective-permute-start = (s32[2]{0:T(128)S(1)}, s32[2]{0:T(128)S(1)}, u32[]{:S(2)}, u32[]{:S(2)}) collective-permute-start(s32[2]{0:T(128)S(1)} %copy-done.6), channel_id=1, source_target_pairs={{0,496},{16,0},{32,16},{48,32},{64,48},{80,64},{96,80},{112,96},{1... | collective-permute-start | bytes 32 | tf_op jit(solution)/shard_map/ppermute | solution.py:365
  29.3 2.5 %pack.3 = (bf16[16,2,72,128]{3,2,1,0:T(8,128)(2,1)}, s32[2]{0:T(128)}) custom-call(bf16[2,3,128,1152]{3,2,1,0:T(8,128)(2,1)} %x_ref.3, s32[2]{0:T(128)} %refs_5_.1, s32[2]{0:T(128)} %refs_6_.1, bf16[6,32,1152]{2,1,0:T(8,128)(2,1)} %get-tuple-element.19.refs_0_), custom_call_target="tpu_custom_call" | custom-call | tf_op jit(solution)/shard_map/pack/pallas_call | solution.py:62
  31.8 0.0 collective-permute-done.1.refs_1_
  31.8 7.7 %collective-permute-done.2.refs_2_ = bf16[6,32,1152]{2,1,0:T(8,128)(2,1)S(1)} collective-permute-done((bf16[6,32,1152]{2,1,0:T(8,128)(2,1)}, bf16[6,32,1152]{2,1,0:T(8,128)(2,1)S(1)}, u32[]{:S(2)}, u32[]{:S(2)}) %collective-permute-start.2) | collective-permute-done | bytes 442400 | tf_op jit(solution)/shard_map/ppermute | solution.py:365
  39.5 2.0 %collective-permute-done.3.refs_3_ = bf16[6,32,1152]{2,1,0:T(8,128)(2,1)S(1)} collective-permute-done((bf16[6,32,1152]{2,1,0:T(8,128)(2,1)}, bf16[6,32,1152]{2,1,0:T(8,128)(2,1)S(1)}, u32[]{:S(2)}, u32[]{:S(2)}) %collective-permute-start.3) | collective-permute-done | bytes 442400 | tf_op jit(solution)/shard_map/ppermute | solution.py:365
  41.5 1.0 swap_half.1.refs_2_
  42.5 0.0 copy-done.3
  42.5 0.0 collective-permute-done.refs_1_.refs_7_
  42.5 0.6 copy-done.5
  43.1 0.0 all-to-all-done.q_ref.x_ref
  43.1 6.9 %all-to-all-start.1 = ((bf16[16,2,72,128]{3,2,1,0:T(8,128)(2,1)}), bf16[16,2,72,128]{3,2,1,0:T(8,128)(2,1)S(1)}, u32[]{:S(2)}, u32[]{:S(2)}) async-start(bf16[16,2,72,128]{3,2,1,0:T(8,128)(2,1)} %once_there.2), calls=%async_computation.1 | async-start | bytes 1179648 | tf_op jit(solution)/shard_map/all_to_all | solution.py:395
  50.1 3.6 %collective-permute-start.4 = (bf16[4,6,16,1152]{3,2,1,0:T(8,128)(2,1)}, bf16[4,6,16,1152]{3,2,1,0:T(8,128)(2,1)S(1)}, u32[]{:S(2)}, u32[]{:S(2)}) collective-permute-start(bf16[4,6,16,1152]{3,2,1,0:T(8,128)(2,1)} %swap_half.1.refs_2_), channel_id=1, source_target_pairs={{0,16},{16,0},{1,17},{17,1},{2,18},{18,2},{3,19},{19,3},{4,20},{20... | collective-permute-start | bytes 2654216 | tf_op jit(solution)/shard_map/ppermute | solution.py:365
  53.7 5.9 %first_frame.1 = bf16[16,72,128]{2,1,0:T(8,128)(2,1)S(1)} custom-call(bf16[16,4,72,128]{3,2,1,0:T(8,128)(2,1)S(1)} %all-to-all-done.q_ref.x_ref), custom_call_target="tpu_custom_call" | custom-call | tf_op jit(solution)/shard_map/first_frame/pallas_call | solution.py:136
  59.6 1.4 %collective-permute-start.6 = (bf16[16,72,128]{2,1,0:T(8,128)(2,1)S(1)}, bf16[16,72,128]{2,1,0:T(8,128)(2,1)}, u32[]{:S(2)}, u32[]{:S(2)}) collective-permute-start(bf16[16,72,128]{2,1,0:T(8,128)(2,1)S(1)} %first_frame.1), channel_id=1, source_target_pairs={{0,0},{1,1},{2,2},{3,3},{4,36},{5,37},{6,38},{7,39},{8,72},{9,73},... | collective-permute-start | bytes 884744 | tf_op jit(solution)/shard_map/ppermute | solution.py:390
  61.0 0.0 collective-permute-done.4.refs_4_
  61.0 1.0 copy-done.2
  62.0 1.0 copy-done.4
  63.1 2.8 %temporal.1 = (bf16[16,16,1152]{2,1,0:T(8,128)(2,1)S(1)}, bf16[16,1152]{1,0:T(8,128)(2,1)}) custom-call(s32[1]{0:T(128)} %bitcast.core_ref, s32[1]{0:T(128)} %bitcast.1.x_ref, bf16[6,32,1152]{2,1,0:T(8,128)(2,1)S(1)} %copy-done, bf16[6,32,1152]{2,1,0:T(8,128)(2,1)S(1)} %collective-permute-done.1.refs_1_, bf16[6,32,1152]{2,1,0:T(8,128)(2,1)S(1)} %copy-done.2, ...), custom_call_target="tpu_custom_call" | custom-call | tf_op jit(solution)/shard_map/temporal/pallas_call | solution.py:272
  65.9 1.9 %collective-permute-start.5 = (bf16[16,72,128]{2,1,0:T(8,128)(2,1)S(1)}, bf16[16,72,128]{2,1,0:T(8,128)(2,1)S(1)}, u32[]{:S(2)}, u32[]{:S(2)}) collective-permute-start(bf16[16,72,128]{2,1,0:T(8,128)(2,1)S(1)} %first_frame.1), channel_id=1, source_target_pairs={{16,0},{32,16},{48,32},{64,48},{80,64},{96,80},{112,96},{17,1},{33... | collective-permute-start | bytes 884744 | tf_op jit(solution)/shard_map/ppermute | solution.py:391
  67.8 0.0 collective-permute-done.6.refs_0_
  67.8 0.7 collective-permute-start.7
  68.5 9.9 %collective-permute-start.8 = (bf16[16,1152]{1,0:T(8,128)(2,1)}, bf16[16,1152]{1,0:T(8,128)(2,1)S(1)}, u32[]{:S(2)}, u32[]{:S(2)}) collective-permute-start(bf16[16,1152]{1,0:T(8,128)(2,1)} %get-tuple-element.26), channel_id=1, source_target_pairs={{0,384},{128,0},{256,128},{384,256},{1,385},{129,1},{257,129},{385... | collective-permute-start | bytes 110600 | tf_op jit(solution)/shard_map/ppermute | solution.py:365
  78.4 0.0 all-to-all-done.1.kv_ref
  78.5 5.9 %second_frame.1.refs_0_.near_ref = bf16[16,72,128]{2,1,0:T(8,128)(2,1)S(1)} custom-call(bf16[16,4,72,128]{3,2,1,0:T(8,128)(2,1)S(1)} %all-to-all-done.q_ref.x_ref, bf16[16,2,72,128]{3,2,1,0:T(8,128)(2,1)S(1)} %all-to-all-done.1.kv_ref, bf16[16,16,1152]{2,1,0:T(8,128)(2,1)S(1)} %get-tuple-element.25.refs_0_.refs_1_.timely_ref), custom_call_target="tpu_custom_call" | custom-call | tf_op jit(solution)/shard_map/second_frame/pallas_call | solution.py:148
  84.4 0.0 collective-permute-done.8.passed_ref
  84.4 0.1 to_send_back.1
  84.4 0.0 collective-permute-done.5.far_ref
  84.5 0.0 collective-permute-done.7.crossed_ref
  84.5 0.9 beside.1
  85.4 11.1 %all-to-all-start.2 = ((bf16[16,2,72,128]{3,2,1,0:T(8,128)(2,1)}), bf16[16,2,72,128]{3,2,1,0:T(8,128)(2,1)S(1)}, u32[]{:S(2)}, u32[]{:S(2)}) async-start(bf16[16,2,72,128]{3,2,1,0:T(8,128)(2,1)} %beside.1), calls=%async_computation.2 | async-start | bytes 1179648 | tf_op jit(solution)/shard_map/all_to_all | solution.py:395
  96.4 1.9 %collective-permute-start.9 = (bf16[4,16,1152]{2,1,0:T(8,128)(2,1)S(1)}, bf16[4,16,1152]{2,1,0:T(8,128)(2,1)S(1)}, u32[]{:S(2)}, u32[]{:S(2)}) collective-permute-start(bf16[4,16,1152]{2,1,0:T(8,128)(2,1)S(1)} %get-tuple-element.28), channel_id=1, source_target_pairs={{0,96},{32,0},{64,32},{96,64},{1,97},{33,1},{65,33},{97,65},{2,98}... | collective-permute-start | bytes 442376 | tf_op jit(solution)/shard_map/ppermute | solution.py:365
  98.4 1.9 %collective-permute-start.10 = (bf16[4,16,1152]{2,1,0:T(8,128)(2,1)S(1)}, bf16[4,16,1152]{2,1,0:T(8,128)(2,1)S(1)}, u32[]{:S(2)}, u32[]{:S(2)}) collective-permute-start(bf16[4,16,1152]{2,1,0:T(8,128)(2,1)S(1)} %get-tuple-element.29), channel_id=1, source_target_pairs={{0,64},{32,96},{64,0},{96,32},{1,65},{33,97},{65,1},{97,33},{2,66}... | collective-permute-start | bytes 442376 | tf_op jit(solution)/shard_map/ppermute | solution.py:365
  100.3 3.4 %collective-permute-start.11 = (bf16[4,16,1152]{2,1,0:T(8,128)(2,1)S(1)}, bf16[4,16,1152]{2,1,0:T(8,128)(2,1)S(1)}, u32[]{:S(2)}, u32[]{:S(2)}) collective-permute-start(bf16[4,16,1152]{2,1,0:T(8,128)(2,1)S(1)} %get-tuple-element.30), channel_id=1, source_target_pairs={{0,32},{32,64},{64,96},{96,0},{1,33},{33,65},{65,97},{97,1},{2,34}... | collective-permute-start | bytes 442376 | tf_op jit(solution)/shard_map/ppermute | solution.py:365
  103.7 0.0 collective-permute-done.9.refs_1_
  103.7 2.4 %collective-permute-done.10.refs_2_ = bf16[4,16,1152]{2,1,0:T(8,128)(2,1)S(1)} collective-permute-done((bf16[4,16,1152]{2,1,0:T(8,128)(2,1)S(1)}, bf16[4,16,1152]{2,1,0:T(8,128)(2,1)S(1)}, u32[]{:S(2)}, u32[]{:S(2)}) %collective-permute-start.10) | collective-permute-done | bytes 147488 | tf_op jit(solution)/shard_map/ppermute | solution.py:365
  106.1 2.8 %collective-permute-done.11.refs_3_ = bf16[4,16,1152]{2,1,0:T(8,128)(2,1)S(1)} collective-permute-done((bf16[4,16,1152]{2,1,0:T(8,128)(2,1)S(1)}, bf16[4,16,1152]{2,1,0:T(8,128)(2,1)S(1)}, u32[]{:S(2)}, u32[]{:S(2)}) %collective-permute-start.11) | collective-permute-done | bytes 147488 | tf_op jit(solution)/shard_map/ppermute | solution.py:365
  108.9 0.7 return_half.1
  109.6 6.6 %collective-permute-start.12 = (bf16[4,2,16,1152]{3,2,1,0:T(8,128)(2,1)}, bf16[4,2,16,1152]{3,2,1,0:T(8,128)(2,1)S(1)}, u32[]{:S(2)}, u32[]{:S(2)}) collective-permute-start(bf16[4,2,16,1152]{3,2,1,0:T(8,128)(2,1)} %return_half.1), channel_id=1, source_target_pairs={{0,16},{16,0},{1,17},{17,1},{2,18},{18,2},{3,19},{19,3},{4,20},{20... | collective-permute-start | bytes 884744 | tf_op jit(solution)/shard_map/ppermute | solution.py:365
  116.2 1.4 %collective-permute-done.12.refs_4_ = bf16[4,2,16,1152]{3,2,1,0:T(8,128)(2,1)S(1)} collective-permute-done((bf16[4,2,16,1152]{3,2,1,0:T(8,128)(2,1)}, bf16[4,2,16,1152]{3,2,1,0:T(8,128)(2,1)S(1)}, u32[]{:S(2)}, u32[]{:S(2)}) %collective-permute-start.12) | collective-permute-done | bytes 294944 | tf_op jit(solution)/shard_map/ppermute | solution.py:365
  117.6 0.0 all-to-all-done.2.space_ref
  117.6 2.2 %combine.1 = bf16[2,128,1152]{2,1,0:T(8,128)(2,1)} custom-call(s32[1]{0:T(128)} %bitcast.core_ref, s32[1]{0:T(128)} %bitcast.1.x_ref, bf16[16,2,72,128]{3,2,1,0:T(8,128)(2,1)S(1)} %all-to-all-done.2.space_ref, bf16[4,16,1152]{2,1,0:T(8,128)(2,1)S(1)} %get-tuple-element.27.refs_0_, bf16[4,16,1152]{2,1,0:T(8,128)(2,1)S(1)} %collective-permute-done.9.refs_1_, ...), custom_call_target="tpu_custom_call" | custom-call | tf_op jit(solution)/shard_map/combine/pallas_call | solution.py:349
  (11 shorter events, 0.0 us)
Async XLA Ops:
  2.9 40.2 %all-to-all-start = ((bf16[16,4,72,128]{3,2,1,0:T(8,128)(2,1)}), bf16[16,4,72,128]{3,2,1,0:T(8,128)(2,1)S(1)}, u32[]{:S(2)}, u32[]{:S(2)}) async-start(bf16[16,4,72,128]{3,2,1,0:T(8,128)(2,1)} %get-tuple-element.18.after_ref), calls=%async_computation | async-start | bytes 2359296 | tf_op jit(solution)/shard_map/all_to_all | solution.py:395
  12.1 13.5 %copy-start.6 = (s32[2]{0:T(128)S(1)}, s32[2]{0:T(128)}, u32[]{:S(2)}) copy-start(s32[2]{0:T(128)} %get-tuple-element.21) | copy-start | bytes 28
  14.9 26.6 %copy-start = (bf16[6,32,1152]{2,1,0:T(8,128)(2,1)S(1)}, bf16[6,32,1152]{2,1,0:T(8,128)(2,1)}, u32[]{:S(2)}) copy-start(bf16[6,32,1152]{2,1,0:T(8,128)(2,1)} %get-tuple-element.19.refs_0_) | copy-start | bytes 1327108
  14.9 16.9 %collective-permute-start.1 = (bf16[6,32,1152]{2,1,0:T(8,128)(2,1)}, bf16[6,32,1152]{2,1,0:T(8,128)(2,1)S(1)}, u32[]{:S(2)}, u32[]{:S(2)}) collective-permute-start(bf16[6,32,1152]{2,1,0:T(8,128)(2,1)} %get-tuple-element.22), channel_id=1, source_target_pairs={{0,32},{32,64},{64,96},{96,0},{1,33},{33,65},{65,97},{97,1},{2,34}... | collective-permute-start | bytes 1327112 | tf_op jit(solution)/shard_map/ppermute | solution.py:365
  18.1 21.4 %collective-permute-start.2 = (bf16[6,32,1152]{2,1,0:T(8,128)(2,1)}, bf16[6,32,1152]{2,1,0:T(8,128)(2,1)S(1)}, u32[]{:S(2)}, u32[]{:S(2)}) collective-permute-start(bf16[6,32,1152]{2,1,0:T(8,128)(2,1)} %get-tuple-element.23), channel_id=1, source_target_pairs={{0,64},{32,96},{64,0},{96,32},{1,65},{33,97},{65,1},{97,33},{2,66}... | collective-permute-start | bytes 1327112 | tf_op jit(solution)/shard_map/ppermute | solution.py:365
  22.5 19.0 %collective-permute-start.3 = (bf16[6,32,1152]{2,1,0:T(8,128)(2,1)}, bf16[6,32,1152]{2,1,0:T(8,128)(2,1)S(1)}, u32[]{:S(2)}, u32[]{:S(2)}) collective-permute-start(bf16[6,32,1152]{2,1,0:T(8,128)(2,1)} %get-tuple-element.24), channel_id=1, source_target_pairs={{0,96},{32,0},{64,32},{96,64},{1,97},{33,1},{65,33},{97,65},{2,98}... | collective-permute-start | bytes 1327112 | tf_op jit(solution)/shard_map/ppermute | solution.py:365
  25.6 17.0 %collective-permute-start = (s32[2]{0:T(128)S(1)}, s32[2]{0:T(128)S(1)}, u32[]{:S(2)}, u32[]{:S(2)}) collective-permute-start(s32[2]{0:T(128)S(1)} %copy-done.6), channel_id=1, source_target_pairs={{0,496},{16,0},{32,16},{48,32},{64,48},{80,64},{96,80},{112,96},{1... | collective-permute-start | bytes 32 | tf_op jit(solution)/shard_map/ppermute | solution.py:365
  39.5 3.0 %copy-start.1 = (bf16[6,32,1152]{2,1,0:T(8,128)(2,1)}, bf16[6,32,1152]{2,1,0:T(8,128)(2,1)S(1)}, u32[]{:S(2)}) copy-start(bf16[6,32,1152]{2,1,0:T(8,128)(2,1)S(1)} %collective-permute-done.2.refs_2_) | copy-start | bytes 1327108
  41.5 1.1 copy-start.3
  42.5 0.6 copy-start.5
  43.1 35.3 %all-to-all-start.1 = ((bf16[16,2,72,128]{3,2,1,0:T(8,128)(2,1)}), bf16[16,2,72,128]{3,2,1,0:T(8,128)(2,1)S(1)}, u32[]{:S(2)}, u32[]{:S(2)}) async-start(bf16[16,2,72,128]{3,2,1,0:T(8,128)(2,1)} %once_there.2), calls=%async_computation.1 | async-start | bytes 1179648 | tf_op jit(solution)/shard_map/all_to_all | solution.py:395
  50.1 11.0 %collective-permute-start.4 = (bf16[4,6,16,1152]{3,2,1,0:T(8,128)(2,1)}, bf16[4,6,16,1152]{3,2,1,0:T(8,128)(2,1)S(1)}, u32[]{:S(2)}, u32[]{:S(2)}) collective-permute-start(bf16[4,6,16,1152]{3,2,1,0:T(8,128)(2,1)} %swap_half.1.refs_2_), channel_id=1, source_target_pairs={{0,16},{16,0},{1,17},{17,1},{2,18},{18,2},{3,19},{19,3},{4,20},{20... | collective-permute-start | bytes 2654216 | tf_op jit(solution)/shard_map/ppermute | solution.py:365
  59.6 8.1 %collective-permute-start.6 = (bf16[16,72,128]{2,1,0:T(8,128)(2,1)S(1)}, bf16[16,72,128]{2,1,0:T(8,128)(2,1)}, u32[]{:S(2)}, u32[]{:S(2)}) collective-permute-start(bf16[16,72,128]{2,1,0:T(8,128)(2,1)S(1)} %first_frame.1), channel_id=1, source_target_pairs={{0,0},{1,1},{2,2},{3,3},{4,36},{5,37},{6,38},{7,39},{8,72},{9,73},... | collective-permute-start | bytes 884744 | tf_op jit(solution)/shard_map/ppermute | solution.py:390
  61.0 1.0 copy-start.2
  62.0 1.0 copy-start.4
  65.9 18.6 %collective-permute-start.5 = (bf16[16,72,128]{2,1,0:T(8,128)(2,1)S(1)}, bf16[16,72,128]{2,1,0:T(8,128)(2,1)S(1)}, u32[]{:S(2)}, u32[]{:S(2)}) collective-permute-start(bf16[16,72,128]{2,1,0:T(8,128)(2,1)S(1)} %first_frame.1), channel_id=1, source_target_pairs={{16,0},{32,16},{48,32},{64,48},{80,64},{96,80},{112,96},{17,1},{33... | collective-permute-start | bytes 884744 | tf_op jit(solution)/shard_map/ppermute | solution.py:391
  67.8 16.7 %collective-permute-start.7 = (bf16[16,72,128]{2,1,0:T(8,128)(2,1)}, bf16[16,72,128]{2,1,0:T(8,128)(2,1)S(1)}, u32[]{:S(2)}, u32[]{:S(2)}) collective-permute-start(bf16[16,72,128]{2,1,0:T(8,128)(2,1)} %once_there.3), channel_id=1, source_target_pairs={{0,496},{1,497},{2,498},{3,499},{36,500},{37,501},{38,502},{39,503... | collective-permute-start | bytes 884744 | tf_op jit(solution)/shard_map/ppermute | solution.py:391
  68.5 15.9 %collective-permute-start.8 = (bf16[16,1152]{1,0:T(8,128)(2,1)}, bf16[16,1152]{1,0:T(8,128)(2,1)S(1)}, u32[]{:S(2)}, u32[]{:S(2)}) collective-permute-start(bf16[16,1152]{1,0:T(8,128)(2,1)} %get-tuple-element.26), channel_id=1, source_target_pairs={{0,384},{128,0},{256,128},{384,256},{1,385},{129,1},{257,129},{385... | collective-permute-start | bytes 110600 | tf_op jit(solution)/shard_map/ppermute | solution.py:365
  85.4 32.3 %all-to-all-start.2 = ((bf16[16,2,72,128]{3,2,1,0:T(8,128)(2,1)}), bf16[16,2,72,128]{3,2,1,0:T(8,128)(2,1)S(1)}, u32[]{:S(2)}, u32[]{:S(2)}) async-start(bf16[16,2,72,128]{3,2,1,0:T(8,128)(2,1)} %beside.1), calls=%async_computation.2 | async-start | bytes 1179648 | tf_op jit(solution)/shard_map/all_to_all | solution.py:395
  96.4 7.2 %collective-permute-start.9 = (bf16[4,16,1152]{2,1,0:T(8,128)(2,1)S(1)}, bf16[4,16,1152]{2,1,0:T(8,128)(2,1)S(1)}, u32[]{:S(2)}, u32[]{:S(2)}) collective-permute-start(bf16[4,16,1152]{2,1,0:T(8,128)(2,1)S(1)} %get-tuple-element.28), channel_id=1, source_target_pairs={{0,96},{32,0},{64,32},{96,64},{1,97},{33,1},{65,33},{97,65},{2,98}... | collective-permute-start | bytes 442376 | tf_op jit(solution)/shard_map/ppermute | solution.py:365
  98.4 7.7 %collective-permute-start.10 = (bf16[4,16,1152]{2,1,0:T(8,128)(2,1)S(1)}, bf16[4,16,1152]{2,1,0:T(8,128)(2,1)S(1)}, u32[]{:S(2)}, u32[]{:S(2)}) collective-permute-start(bf16[4,16,1152]{2,1,0:T(8,128)(2,1)S(1)} %get-tuple-element.29), channel_id=1, source_target_pairs={{0,64},{32,96},{64,0},{96,32},{1,65},{33,97},{65,1},{97,33},{2,66}... | collective-permute-start | bytes 442376 | tf_op jit(solution)/shard_map/ppermute | solution.py:365
  100.3 8.6 %collective-permute-start.11 = (bf16[4,16,1152]{2,1,0:T(8,128)(2,1)S(1)}, bf16[4,16,1152]{2,1,0:T(8,128)(2,1)S(1)}, u32[]{:S(2)}, u32[]{:S(2)}) collective-permute-start(bf16[4,16,1152]{2,1,0:T(8,128)(2,1)S(1)} %get-tuple-element.30), channel_id=1, source_target_pairs={{0,32},{32,64},{64,96},{96,0},{1,33},{33,65},{65,97},{97,1},{2,34}... | collective-permute-start | bytes 442376 | tf_op jit(solution)/shard_map/ppermute | solution.py:365
  109.6 8.0 %collective-permute-start.12 = (bf16[4,2,16,1152]{3,2,1,0:T(8,128)(2,1)}, bf16[4,2,16,1152]{3,2,1,0:T(8,128)(2,1)S(1)}, u32[]{:S(2)}, u32[]{:S(2)}) collective-permute-start(bf16[4,2,16,1152]{3,2,1,0:T(8,128)(2,1)} %return_half.1), channel_id=1, source_target_pairs={{0,16},{16,0},{1,17},{17,1},{2,18},{18,2},{3,19},{19,3},{4,20},{20... | collective-permute-start | bytes 884744 | tf_op jit(solution)/shard_map/ppermute | solution.py:365

commit v4 on v3

--- a/solution.py
+++ b/solution.py
@@ -17,6 +17,7 @@
 TOK = 128
 QBLOCK = 256
 CHIPS = 4
+MEMBERS = 8
 WIDE = 32
 SHARE = 16
 SCALE = math.log2(math.e) / math.sqrt(HEAD_DIM)
@@ -27,13 +28,18 @@
 VMEM = pl.BlockSpec(memory_space=pltpu.VMEM)
 ANY = pl.BlockSpec(memory_space=pl.ANY)
 SMEM = pl.BlockSpec(memory_space=pltpu.SMEM)
-PARAMS = pltpu.CompilerParams(vmem_limit_bytes=56 << 20)
+PARAMS = pltpu.CompilerParams(vmem_limit_bytes=16 << 20)
+WIDE_PARAMS = pltpu.CompilerParams(vmem_limit_bytes=32 << 20)
 
 
 def matmul(a, b, a_dim, b_dim):
     return lax.dot_general(
         a, b, (((a_dim,), (b_dim,)), ((), ())), preferred_element_type=F32
     )
+
+
+def outside(array):
+    return pltpu.with_memory_space_constraint(array, pltpu.HBM)
 
 
 def resident(array):
@@ -46,30 +52,34 @@
         write(head, turned[head * HEAD_DIM : (head + 1) * HEAD_DIM])
 
 
-def pack_kernel(parts, x_ref, time_ref, level_ref, *refs):
+def pack_kernel(x_ref, time_ref, level_ref, *refs):
     o_ref, index_ref = refs[-2:]
     index_ref[0] = time_ref[0]
     index_ref[1] = level_ref[0]
-    for place, (frame, part) in enumerate(parts):
-
-        def write(head, rows, place=place):
-            o_ref[head, place] = rows
-
-        turn(x_ref[frame, part], write)
-
-
-def pack(parts, spatial_qkv, timestep, noise_level, after):
-    return pl.pallas_call(
-        functools.partial(pack_kernel, parts),
-        in_specs=[VMEM, SMEM, SMEM] + [ANY] * len(after),
-        out_specs=[VMEM, SMEM],
+
+    def write(head, rows):
+        o_ref[head, 0] = rows
+
+    turn(x_ref[0, 0], write)
+
+
+def pack(frame, spatial_qkv, timestep, noise_level, after):
+    return pl.pallas_call(
+        pack_kernel,
+        grid=(3,),
+        in_specs=[pl.BlockSpec((1, 1, TOK, D), lambda part: (frame, part, 0, 0)), SMEM, SMEM]
+        + [ANY] * len(after),
+        out_specs=[
+            pl.BlockSpec((HEADS, 1, HEAD_DIM, TOK), lambda part: (0, part, 0, 0)),
+            SMEM,
+        ],
         out_shape=[
-            jax.ShapeDtypeStruct((HEADS, len(parts), HEAD_DIM, TOK), BF16),
+            jax.ShapeDtypeStruct((HEADS, 3, HEAD_DIM, TOK), BF16),
             jax.ShapeDtypeStruct((2,), jnp.int32),
         ],
         compiler_params=PARAMS,
         name="pack",
-    )(spatial_qkv, timestep, noise_level, *after)
+    )(outside(spatial_qkv), timestep, noise_level, *after)
 
 
 def gate_kernel(*refs):
@@ -105,25 +115,13 @@
             write(block * (QBLOCK // TOK) + j, result[:, j * TOK : (j + 1) * TOK])
 
 
-def first_kernel(x_ref, *refs):
+def spatial_kernel(x_ref, *refs):
     o_ref, query, value = refs[-3:]
 
     def write(group, result):
         o_ref[group] = result
 
     attend(lambda group, part: x_ref[group, part], query, value, write)
-
-
-def second_kernel(q_ref, kv_ref, *refs):
-    o_ref, query, value = refs[-3:]
-
-    def find(group, part):
-        return kv_ref[group, part - 1] if part else q_ref[group, 3]
-
-    def write(group, result):
-        o_ref[group] = result
-
-    attend(find, query, value, write)
 
 
 SPATIAL_SCRATCH = [
@@ -132,28 +130,16 @@
 ]
 
 
-def first_frame(packed, after):
-    return pl.pallas_call(
-        first_kernel,
+def spatial_frame(packed, after):
+    return pl.pallas_call(
+        spatial_kernel,
         in_specs=[VMEM] + [ANY] * len(after),
         out_specs=VMEM,
         out_shape=pltpu.VMEM((GROUPS, HEAD_DIM, TOK), BF16),
         scratch_shapes=SPATIAL_SCRATCH,
-        compiler_params=PARAMS,
-        name="first_frame",
+        compiler_params=WIDE_PARAMS,
+        name="spatial",
     )(resident(packed), *after)
-
-
-def second_frame(queries, packed, after):
-    return pl.pallas_call(
-        second_kernel,
-        in_specs=[VMEM, VMEM] + [ANY] * len(after),
-        out_specs=VMEM,
-        out_shape=pltpu.VMEM((GROUPS, HEAD_DIM, TOK), BF16),
-        scratch_shapes=SPATIAL_SCRATCH,
-        compiler_params=PARAMS,
-        name="second_frame",
-    )(resident(queries), resident(packed), *after)
 
 
 def beside_kernel(near_ref, far_ref, crossed_ref, *refs):
@@ -193,31 +179,31 @@
         out_shape=[jax.ShapeDtypeStruct((6, WIDE, D), BF16)] * CHIPS,
         compiler_params=PARAMS,
         name="spread",
-    )(x, query, kv, after)
+    )(x, outside(query), outside(kv), after)
 
 
 def swap_kernel(core_ref, *refs):
-    blocks, o_ref = refs[:CHIPS], refs[CHIPS]
+    blocks, o_ref = refs[:CHIPS], refs[-1]
     half = pl.ds(pl.multiple_of((1 - core_ref[0]) * SHARE, SHARE), SHARE)
     for step in range(CHIPS):
         for row in range(6):
             o_ref[step, row] = blocks[step][row, half]
 
 
-def swap_half(core, blocks):
+def swap_half(core, blocks, after):
     return pl.pallas_call(
         swap_kernel,
-        in_specs=[SMEM] + [VMEM] * CHIPS,
+        in_specs=[SMEM] + [VMEM] * CHIPS + [ANY] * len(after),
         out_specs=VMEM,
         out_shape=jax.ShapeDtypeStruct((CHIPS, 6, SHARE, D), BF16),
         compiler_params=PARAMS,
         name="swap_half",
-    )(core, *[resident(block) for block in blocks])
-
-
-def temporal_kernel(core_ref, x_ref, *refs):
+    )(core, *[resident(block) for block in blocks], *after)
+
+
+def temporal_kernel(core_ref, *refs):
     blocks, other_ref = refs[:CHIPS], refs[CHIPS]
-    o_ref, crossing_ref, query, key, value = refs[CHIPS + 1 :]
+    mine_ref, send_ref, query, key, value = refs[CHIPS + 1 :]
     half = pl.ds(pl.multiple_of(core_ref[0] * SHARE, SHARE), SHARE)
     rows = PLEN * SHARE
     token_of_row = lax.broadcasted_iota(jnp.int32, (rows, rows), 0) % SHARE
@@ -247,93 +233,85 @@
         summed = matmul(weights.astype(BF16), v, 1, 0) / row_sum
         for tile in range(first, last + 1):
             tiles[tile] += summed[:, tile * 128 - low : tile * 128 - low + 128]
+    core = core_ref[0]
     for step in range(CHIPS):
-        for side in range(2):
-            core = core_ref[0] if side == 0 else 1 - core_ref[0]
-            ahead = (step + 1) % CHIPS
-            even = jnp.where(core == 1, 4 * step + 1, 4 * ahead + 3)
-            odd = 4 * step + 2 * core
-            for frame, slot in enumerate((even, odd)):
+        for side, (odd_ref, even_ref, ahead) in enumerate(
+            ((mine_ref, send_ref, 1 - core), (send_ref, mine_ref, core))
+        ):
+            back = lax.rem(step + ahead, CHIPS)
+            for frame, (ref, place) in enumerate(
+                ((even_ref, 2 * back + 1), (odd_ref, 2 * step))
+            ):
                 row = ((step * 2 + side) * 2 + frame) * SHARE
                 for tile in range(D // 128):
-                    o_ref[slot, :, tile * 128 : (tile + 1) * 128] = tiles[tile][
+                    ref[place, :, tile * 128 : (tile + 1) * 128] = tiles[tile][
                         row : row + SHARE
                     ].astype(BF16)
 
 
-    crossing_ref[...] = o_ref[crossing_slot(x_ref[0])]
-
-
-def crossing_slot(x):
-    return 4 * lax.rem(x + 1, CHIPS) + 3
-
-
-def temporal_share(core, x, blocks, other):
+def temporal_share(core, blocks, other):
     return pl.pallas_call(
         temporal_kernel,
-        in_specs=[SMEM, SMEM] + [VMEM] * (CHIPS + 1),
+        in_specs=[SMEM] + [VMEM] * (CHIPS + 1),
         out_specs=[VMEM, VMEM],
-        out_shape=[
-            pltpu.VMEM((PLEN, SHARE, D), BF16),
-            pltpu.VMEM((SHARE, D), BF16),
-        ],
+        out_shape=[pltpu.VMEM((2 * CHIPS, SHARE, D), BF16)] * 2,
         scratch_shapes=[pltpu.VMEM((PLEN * SHARE, D), BF16)] * 3,
         compiler_params=PARAMS,
         name="temporal",
-    )(core, x, *[resident(block) for block in blocks], resident(other))
-
-
-def back_kernel(x_ref, timely_ref, passed_ref, *refs):
-    o_refs = refs[-CHIPS:]
-    slot = crossing_slot(x_ref[0])
-    for step, o_ref in enumerate(o_refs):
-        o_ref[...] = timely_ref[4 * step : 4 * step + 4]
-
-        @pl.when(slot == 4 * step + 3)
-        def _():
-            o_ref[3] = passed_ref[...]
-
-
-def to_send_back(x, timely, passed, after):
+    )(core, *[resident(block) for block in blocks], resident(other))
+
+
+def edge_kernel(x_ref, mine_ref, theirs_ref, o_ref):
+    slot = 2 * lax.rem(x_ref[0] + 1, CHIPS) + 1
+    o_ref[0] = mine_ref[slot]
+    o_ref[1] = theirs_ref[slot]
+
+
+def edge(x, mine, theirs):
+    return pl.pallas_call(
+        edge_kernel,
+        in_specs=[SMEM, VMEM, VMEM],
+        out_specs=VMEM,
+        out_shape=pltpu.VMEM((2, SHARE, D), BF16),
+        compiler_params=PARAMS,
+        name="edge",
+    )(x, resident(mine), resident(theirs))
+
+
+def back_kernel(core_ref, x_ref, mine_ref, theirs_ref, passed_ref, *refs):
+    slot = 2 * lax.rem(x_ref[0] + 1, CHIPS) + 1
+    for step, o_ref in enumerate(refs[-CHIPS:]):
+        o_ref[0:2] = mine_ref[2 * step : 2 * step + 2]
+        o_ref[2:4] = theirs_ref[2 * step : 2 * step + 2]
+
+        @pl.when((slot == 2 * step + 1) & (core_ref[0] == 1))
+        def _(o_ref=o_ref):
+            o_ref[1] = passed_ref[0]
+            o_ref[3] = passed_ref[1]
+
+
+def to_send_back(core, x, mine, theirs, passed, after):
     return pl.pallas_call(
         back_kernel,
-        in_specs=[SMEM, VMEM, VMEM] + [ANY] * len(after),
+        in_specs=[SMEM, SMEM, VMEM, VMEM, VMEM] + [ANY] * len(after),
         out_specs=[VMEM] * CHIPS,
         out_shape=[pltpu.VMEM((4, SHARE, D), BF16)] * CHIPS,
         compiler_params=PARAMS,
         name="to_send_back",
-    )(x, resident(timely), resident(passed), *after)
-
-
-def return_kernel(core_ref, *refs):
-    start = 2 * (1 - core_ref[0])
-    for step in range(CHIPS):
-        for slot in range(2):
-            refs[CHIPS][step, slot] = refs[step][start + slot]
-
-
-def return_half(core, back):
-    return pl.pallas_call(
-        return_kernel,
-        in_specs=[SMEM] + [VMEM] * CHIPS,
-        out_specs=VMEM,
-        out_shape=jax.ShapeDtypeStruct((CHIPS, 2, SHARE, D), BF16),
-        compiler_params=PARAMS,
-        name="return_half",
-    )(core, *[resident(block) for block in back])
+    )(core, x, resident(mine), resident(theirs), resident(passed), *after)
 
 
 def combine_kernel(core_ref, x_ref, space_ref, *refs):
-    back, (theirs_ref, time_ref, level_ref, index_ref) = refs[:CHIPS], refs[CHIPS : CHIPS + 4]
-    gs_ref, gt_ref, table_ref, o_ref, times = refs[CHIPS + 4 :]
+    back, (time_ref, level_ref, index_ref) = refs[:CHIPS], refs[CHIPS : CHIPS + 3]
+    gs_ref, gt_ref, table_ref, o_ref, times = refs[CHIPS + 3 :]
     core = core_ref[0]
     for step in range(CHIPS):
         column = lax.rem(x_ref[0] + step, CHIPS) * WIDE
         here = pl.ds(pl.multiple_of(column + core * SHARE, SHARE), SHARE)
         there = pl.ds(pl.multiple_of(column + (1 - core) * SHARE, SHARE), SHARE)
         for slot in range(2):
-            times[slot, here] = back[step][2 * core + slot]
-            times[slot, there] = theirs_ref[step, slot]
+            times[slot, here] = back[step][slot]
+            times[slot, there] = back[step][2 + slot]
     rows = time_ref[1], index_ref[0]
     levels = level_ref[1], index_ref[1]
     for slot in range(2):
@@ -345,17 +323,17 @@
         o_ref[slot] = (size * (gate_space * space + gate_time * timely)).astype(BF16)
 
 
-def combine(core, x, space, back, theirs, timestep, noise_level, indices, spatial_gate, temporal_gate, step_table):
+def combine(core, x, space, back, timestep, noise_level, indices, spatial_gate, temporal_gate, step_table):
     return pl.pallas_call(
         combine_kernel,
-        in_specs=[SMEM, SMEM] + [VMEM] * (CHIPS + 2) + [SMEM] * 3 + [VMEM, VMEM, SMEM],
+        in_specs=[SMEM, SMEM] + [VMEM] * (CHIPS + 1) + [SMEM] * 3 + [VMEM, VMEM, SMEM],
         out_specs=VMEM,
         out_shape=jax.ShapeDtypeStruct((2, TOK, D), BF16),
         scratch_shapes=[pltpu.VMEM((2, TOK, D), BF16)],
         compiler_params=PARAMS,
         name="combine",
     )(
-        core, x, resident(space), *[resident(block) for block in back], resident(theirs),
+        core, x, resident(space), *[resident(block) for block in back],
         timestep, noise_level, indices, spatial_gate, temporal_gate, step_table,
     )
 
@@ -407,30 +385,32 @@
 ):
     x, core = lax.axis_index("x"), lax.axis_index("core")
     x_arg, core_arg = x[None].astype(jnp.int32), core[None].astype(jnp.int32)
-    packed, indices = pack(
-        ((0, 0), (0, 1), (0, 2), (1, 0)), spatial_qkv, timestep, noise_level, ()
-    )
+    packed, indices = pack(0, spatial_qkv, timestep, noise_level, ())
     early = exchange(packed, "sp")
     indices = shift(indices, QUEUE, -1)
     blocks = spread(x_arg, temporal_query, temporal_kv, packed)
-    packed, _ = pack(
-        ((1, 1), (1, 2)), spatial_qkv, timestep, noise_level, blocks[:1]
-    )
-    blocks = [blocks[0]] + [shift(blocks[k], "x", k) for k in range(1, CHIPS)]
-    half = swap_half(core_arg, blocks)
+    packed, _ = pack(1, spatial_qkv, timestep, noise_level, blocks[:1])
+    moved = {k: shift(blocks[k], "x", k) for k in (2, 3, 1)}
+    blocks = [blocks[0]] + [moved[k] for k in range(1, CHIPS)]
+    first = spatial_frame(early, ())
+    half = swap_half(core_arg, blocks, (resident(first),))
     late = exchange(once_there(packed, (indices, half)), "sp")
     other = shift(half, "core", 1)
-    timely, passed = temporal_share(core_arg, x_arg, blocks, other)
-    passed = shift(passed, "part", -1)
-    first = first_frame(early, ())
-    far, crossed = one_back(first, (resident(timely),))
-    near = second_frame(early, late, (resident(timely),))
-    back = to_send_back(x_arg, timely, passed, (resident(near),))
+    mine, send = temporal_share(core_arg, blocks, other)
+    theirs = shift(send, "core", 1)
+    size = lax.axis_size(QUEUE)
+    passed = lax.ppermute(
+        edge(x_arg, mine, theirs),
+        QUEUE,
+        [(i, (i - MEMBERS) % size) for i in range(1, size, 2)],
+    )
+    far, crossed = one_back(first, (resident(mine),))
+    near = spatial_frame(late, (resident(mine),))
+    back = to_send_back(core_arg, x_arg, mine, theirs, passed, (resident(near),))
     space = exchange(beside(near, far, crossed, (resident(back[0]),)), "sp")
     back = [back[0]] + [shift(back[k], "x", -k) for k in range(1, CHIPS)]
-    theirs = shift(return_half(core_arg, back), "core", 1)
     return combine(
-        core_arg, x_arg, space, back, theirs, timestep, noise_level, indices,
+        core_arg, x_arg, space, back, timestep, noise_level, indices,
         spatial_gate, temporal_gate, step_table,
     )
 

time: 121 us -> 110 us (0.909)
  waiting for transfers between devices: 16.2 us -> 10.2 us
  starting transfers between devices: 72.9 us -> 69 us
  Pallas kernels: 27.7 us -> 26.3 us
    ppermute x10 -> x9, starting transfers between devices: 41.8 us -> 32.6 us  [shift(): lax.ppermute(block, axes, [(i, (i + distance) % size) for i in range(size)])]
    ppermute x0 -> x1, starting transfers between devices: none -> 7.55 us  [per_device(): lax.ppermute(edge(x_arg, mine, theirs), QUEUE, [(i, (i - MEMBERS) % size)...]
    ppermute x10 -> x9, waiting for transfers between devices: 16.2 us -> 10.2 us  [shift(): lax.ppermute(block, axes, [(i, (i + distance) % size) for i in range(size)])]
    all_to_all x3, starting transfers between devices: 27.2 us -> 24.8 us  [exchange(): return lax.all_to_all(block, axes, 0, 0)]
    unnamed x14 -> x18, local copies, waits for them, and re-layouts: 2.63 us -> 2.36 us
  transfers between devices with their start and end apart: 16 -> 16, of which waited for: 5 -> 7; matrix products, arithmetic and copies ran while one was open for 0% -> 0% of each run, Pallas kernels for 18% -> 19%
where the time goes in v4:
time: 110 us; the launch traced here: 108 us
  starting transfers between devices  69 us (63%)
  Pallas kernels  26.3 us (24%)
  waiting for transfers between devices  10.2 us (9%)
  local copies, waits for them, and re-layouts  2.36 us (2%)
    ppermute x9, starting transfers between devices, shift(): lax.ppermute(block, axes, [(i, (i + distance) % size) for i in range(size)])  32.6 us
    all_to_all x3, starting transfers between devices, exchange(): return lax.all_to_all(block, axes, 0, 0)  24.8 us
    pallas_call x2, Pallas kernels, spatial_frame(): pl.pallas_call(spatial_kernel, in_specs=[VMEM] + [ANY] * len(after), out_...  12.6 us
    ppermute x9, waiting for transfers between devices, shift(): lax.ppermute(block, axes, [(i, (i + distance) % size) for i in range(size)])  10.2 us
    ppermute x1, starting transfers between devices, per_device(): lax.ppermute(edge(x_arg, mine, theirs), QUEUE, [(i, (i - MEMBERS) % size)...  7.55 us
    pallas_call x2, Pallas kernels, pack(): pl.pallas_call(pack_kernel, grid=(3,), in_specs=[pl.BlockSpec((1, 1, TOK,...  6.28 us
    pallas_call x1, Pallas kernels, spread(): pl.pallas_call(spread_kernel, in_specs=[SMEM, VMEM, VMEM, ANY], out_specs...  2.49 us
    unnamed x18, local copies, waits for them, and re-layouts  2.36 us
  transfers between devices with their start and end apart: 16, of which 7 were waited for; matrix products, arithmetic and copies ran while one was open for 0% of the time, Pallas kernels for 19%

profile of v4, /device:TPU:1, one launch (start us, length us, event | category | flops | bytes accessed | tf_op | source)
XLA Modules:
  0.0 108.1 jit_solution(3913742770371354424)
XLA Ops:
  0.0 0.7 copy-done.4
  0.7 0.7 copy-done.6
  1.3 3.1 %pack.2 = (bf16[16,3,72,128]{3,2,1,0:T(8,128)(2,1)}, s32[2]{0:T(128)S(1)}) custom-call(bf16[2,3,128,1152]{3,2,1,0:T(8,128)(2,1)} %x_ref.3, s32[2]{0:T(128)S(1)} %copy-done.4, s32[2]{0:T(128)S(1)} %copy-done.6), custom_call_target="tpu_custom_call" | custom-call | tf_op jit(solution)/shard_map/pack/pallas_call | solution.py:67
  4.4 9.2 %all-to-all-start = ((bf16[16,3,72,128]{3,2,1,0:T(8,128)(2,1)}), bf16[16,3,72,128]{3,2,1,0:T(8,128)(2,1)S(1)}, u32[]{:S(2)}, u32[]{:S(2)}) async-start(bf16[16,3,72,128]{3,2,1,0:T(8,128)(2,1)} %get-tuple-element.18.after_ref), calls=%async_computation | async-start | bytes 1769472 | tf_op jit(solution)/shard_map/all_to_all | solution.py:373
  13.6 0.0 copy-start.5
  13.6 0.0 copy-start.7
  13.7 2.5 %spread.1 = (bf16[6,32,1152]{2,1,0:T(8,128)(2,1)S(1)}, bf16[6,32,1152]{2,1,0:T(8,128)(2,1)}, bf16[6,32,1152]{2,1,0:T(8,128)(2,1)}, bf16[6,32,1152]{2,1,0:T(8,128)(2,1)S(1)}) custom-call(s32[1]{0:T(128)} %bitcast.1.x_ref, bf16[2,128,1152]{2,1,0:T(8,128)(2,1)} %q_ref.1, bf16[2,2,128,1152]{3,2,1,0:T(8,128)(2,1)} %kv_ref.1, ...), custom_call_target="tpu_custom_call" | custom-call | tf_op jit(solution)/shard_map/spread/pallas_call | solution.py:175
  16.1 3.1 %collective-permute-start.1 = (bf16[6,32,1152]{2,1,0:T(8,128)(2,1)}, bf16[6,32,1152]{2,1,0:T(8,128)(2,1)S(1)}, u32[]{:S(2)}, u32[]{:S(2)}) collective-permute-start(bf16[6,32,1152]{2,1,0:T(8,128)(2,1)} %get-tuple-element.22), channel_id=1, source_target_pairs={{0,32},{32,64},{64,96},{96,0},{1,33},{33,65},{65,97},{97,1},{2,34}... | collective-permute-start | bytes 1327112 | tf_op jit(solution)/shard_map/ppermute | solution.py:343
  19.3 4.4 %collective-permute-start.2 = (bf16[6,32,1152]{2,1,0:T(8,128)(2,1)}, bf16[6,32,1152]{2,1,0:T(8,128)(2,1)S(1)}, u32[]{:S(2)}, u32[]{:S(2)}) collective-permute-start(bf16[6,32,1152]{2,1,0:T(8,128)(2,1)} %get-tuple-element.23), channel_id=1, source_target_pairs={{0,64},{32,96},{64,0},{96,32},{1,65},{33,97},{65,1},{97,33},{2,66}... | collective-permute-start | bytes 1327112 | tf_op jit(solution)/shard_map/ppermute | solution.py:343
  23.6 3.1 %collective-permute-start.3 = (bf16[6,32,1152]{2,1,0:T(8,128)(2,1)S(1)}, bf16[6,32,1152]{2,1,0:T(8,128)(2,1)S(1)}, u32[]{:S(2)}, u32[]{:S(2)}) collective-permute-start(bf16[6,32,1152]{2,1,0:T(8,128)(2,1)S(1)} %get-tuple-element.24), channel_id=1, source_target_pairs={{0,96},{32,0},{64,32},{96,64},{1,97},{33,1},{65,33},{97,65},{2,98}... | collective-permute-start | bytes 1327112 | tf_op jit(solution)/shard_map/ppermute | solution.py:343
  26.7 3.7 %collective-permute-start = (s32[2]{0:T(128)S(1)}, s32[2]{0:T(128)S(1)}, u32[]{:S(2)}, u32[]{:S(2)}) collective-permute-start(s32[2]{0:T(128)S(1)} %get-tuple-element.21), channel_id=1, source_target_pairs={{0,496},{16,0},{32,16},{48,32},{64,48},{80,64},{96,80},{112,96},{1... | collective-permute-start | bytes 32 | tf_op jit(solution)/shard_map/ppermute | solution.py:343
  30.4 3.2 %pack.3 = (bf16[16,3,72,128]{3,2,1,0:T(8,128)(2,1)}, s32[2]{0:T(128)}) custom-call(bf16[2,3,128,1152]{3,2,1,0:T(8,128)(2,1)} %x_ref.3, s32[2]{0:T(128)S(1)} %copy-done.5, s32[2]{0:T(128)S(1)} %copy-done.7, bf16[6,32,1152]{2,1,0:T(8,128)(2,1)S(1)} %get-tuple-element.19.refs_0_), custom_call_target="tpu_custom_call" | custom-call | tf_op jit(solution)/shard_map/pack/pallas_call | solution.py:67
  33.6 0.0 all-to-all-done.x_ref
  33.6 6.7 %spatial.2.refs_4_ = bf16[16,72,128]{2,1,0:T(8,128)(2,1)} custom-call(bf16[16,3,72,128]{3,2,1,0:T(8,128)(2,1)S(1)} %all-to-all-done.x_ref), custom_call_target="tpu_custom_call" | custom-call | tf_op jit(solution)/shard_map/spatial/pallas_call | solution.py:134
  40.2 0.0 collective-permute-done.1.refs_1_
  40.3 0.4 collective-permute-done.2.refs_2_
  40.6 1.9 %collective-permute-done.3.refs_3_ = bf16[6,32,1152]{2,1,0:T(8,128)(2,1)S(1)} collective-permute-done((bf16[6,32,1152]{2,1,0:T(8,128)(2,1)S(1)}, bf16[6,32,1152]{2,1,0:T(8,128)(2,1)S(1)}, u32[]{:S(2)}, u32[]{:S(2)}) %collective-permute-start.3) | collective-permute-done | bytes 442400 | tf_op jit(solution)/shard_map/ppermute | solution.py:343
  42.5 0.1 swap_half.1.refs_2_
  42.6 1.1 collective-permute-done.refs_1_.refs_6_
  43.6 7.0 %all-to-all-start.1 = ((bf16[16,3,72,128]{3,2,1,0:T(8,128)(2,1)}), bf16[16,3,72,128]{3,2,1,0:T(8,128)(2,1)S(1)}, u32[]{:S(2)}, u32[]{:S(2)}) async-start(bf16[16,3,72,128]{3,2,1,0:T(8,128)(2,1)} %once_there.2), calls=%async_computation.1 | async-start | bytes 1769472 | tf_op jit(solution)/shard_map/all_to_all | solution.py:373
  50.6 5.8 %collective-permute-start.4 = (bf16[4,6,16,1152]{3,2,1,0:T(8,128)(2,1)S(1)}, bf16[4,6,16,1152]{3,2,1,0:T(8,128)(2,1)S(1)}, u32[]{:S(2)}, u32[]{:S(2)}) collective-permute-start(bf16[4,6,16,1152]{3,2,1,0:T(8,128)(2,1)S(1)} %swap_half.1.refs_2_), channel_id=1, source_target_pairs={{0,16},{16,0},{1,17},{17,1},{2,18},{18,2},{3,19},{19,3},{4,20},{20... | collective-permute-start | bytes 2654216 | tf_op jit(solution)/shard_map/ppermute | solution.py:343
  56.4 1.4 %collective-permute-start.6 = (bf16[16,72,128]{2,1,0:T(8,128)(2,1)}, bf16[16,72,128]{2,1,0:T(8,128)(2,1)}, u32[]{:S(2)}, u32[]{:S(2)}) collective-permute-start(bf16[16,72,128]{2,1,0:T(8,128)(2,1)} %spatial.2.refs_4_), channel_id=1, source_target_pairs={{0,0},{1,1},{2,2},{3,3},{4,36},{5,37},{6,38},{7,39},{8,72},{9,73},... | collective-permute-start | bytes 884744 | tf_op jit(solution)/shard_map/ppermute | solution.py:368
  57.7 0.6 collective-permute-done.4.refs_4_
  58.4 1.0 copy-done.1
  59.4 2.2 %temporal.1 = (bf16[8,16,1152]{2,1,0:T(8,128)(2,1)S(1)}, bf16[8,16,1152]{2,1,0:T(8,128)(2,1)S(1)}) custom-call(s32[1]{0:T(128)} %bitcast.core_ref, bf16[6,32,1152]{2,1,0:T(8,128)(2,1)S(1)} %get-tuple-element.19.refs_0_, bf16[6,32,1152]{2,1,0:T(8,128)(2,1)S(1)} %collective-permute-done.1.refs_1_, bf16[6,32,1152]{2,1,0:T(8,128)(2,1)S(1)} %collective-permute-done.2.refs_2_, ...), custom_call_target="tpu_custom_call" | custom-call | tf_op jit(solution)/shard_map/temporal/pallas_call | solution.py:253
  61.6 3.6 %collective-permute-start.8 = (bf16[8,16,1152]{2,1,0:T(8,128)(2,1)S(1)}, bf16[8,16,1152]{2,1,0:T(8,128)(2,1)S(1)}, u32[]{:S(2)}, u32[]{:S(2)}) collective-permute-start(bf16[8,16,1152]{2,1,0:T(8,128)(2,1)S(1)} %get-tuple-element.26), channel_id=1, source_target_pairs={{0,16},{16,0},{1,17},{17,1},{2,18},{18,2},{3,19},{19,3},{4,20},{20... | collective-permute-start | bytes 884744 | tf_op jit(solution)/shard_map/ppermute | solution.py:343
  65.2 1.9 %collective-permute-start.5 = (bf16[16,72,128]{2,1,0:T(8,128)(2,1)}, bf16[16,72,128]{2,1,0:T(8,128)(2,1)S(1)}, u32[]{:S(2)}, u32[]{:S(2)}) collective-permute-start(bf16[16,72,128]{2,1,0:T(8,128)(2,1)} %spatial.2.refs_4_), channel_id=1, source_target_pairs={{16,0},{32,16},{48,32},{64,48},{80,64},{96,80},{112,96},{17,1},{33... | collective-permute-start | bytes 884744 | tf_op jit(solution)/shard_map/ppermute | solution.py:369
  67.2 0.0 collective-permute-done.6.refs_0_
  67.2 0.7 collective-permute-start.7
  67.9 0.0 collective-permute-done.8.theirs_ref
  67.9 7.5 %collective-permute-start.9 = (bf16[2,16,1152]{2,1,0:T(8,128)(2,1)S(1)}, bf16[2,16,1152]{2,1,0:T(8,128)(2,1)S(1)}, u32[]{:S(2)}, u32[]{:S(2)}) collective-permute-start(bf16[2,16,1152]{2,1,0:T(8,128)(2,1)S(1)} %edge.1), channel_id=1, source_target_pairs={{16,400},{48,432},{80,464},{112,496},{144,16},{176,48},{208,80},{2... | collective-permute-start | bytes 221192 | tf_op jit(solution)/shard_map/ppermute | solution.py:402
  75.5 0.0 all-to-all-done.1.x_ref
  75.5 5.9 %spatial.3.refs_0_.near_ref = bf16[16,72,128]{2,1,0:T(8,128)(2,1)S(1)} custom-call(bf16[16,3,72,128]{3,2,1,0:T(8,128)(2,1)S(1)} %all-to-all-done.1.x_ref, bf16[8,16,1152]{2,1,0:T(8,128)(2,1)S(1)} %get-tuple-element.25.refs_0_.refs_1_.mine_ref), custom_call_target="tpu_custom_call" | custom-call | tf_op jit(solution)/shard_map/spatial/pallas_call | solution.py:134
  81.4 0.0 copy-start.2
  81.4 0.0 copy-start.3
  81.4 0.0 copy-start.8
  81.5 0.1 to_send_back.1
  81.5 0.0 collective-permute-done.5.far_ref
  81.5 0.9 beside.1
  82.4 8.7 %all-to-all-start.2 = ((bf16[16,2,72,128]{3,2,1,0:T(8,128)(2,1)}), bf16[16,2,72,128]{3,2,1,0:T(8,128)(2,1)S(1)}, u32[]{:S(2)}, u32[]{:S(2)}) async-start(bf16[16,2,72,128]{3,2,1,0:T(8,128)(2,1)} %beside.1), calls=%async_computation.2 | async-start | bytes 1179648 | tf_op jit(solution)/shard_map/all_to_all | solution.py:373
  91.2 4.6 %collective-permute-start.10 = (bf16[4,16,1152]{2,1,0:T(8,128)(2,1)S(1)}, bf16[4,16,1152]{2,1,0:T(8,128)(2,1)S(1)}, u32[]{:S(2)}, u32[]{:S(2)}) collective-permute-start(bf16[4,16,1152]{2,1,0:T(8,128)(2,1)S(1)} %get-tuple-element.28), channel_id=1, source_target_pairs={{0,96},{32,0},{64,32},{96,64},{1,97},{33,1},{65,33},{97,65},{2,98}... | collective-permute-start | bytes 442376 | tf_op jit(solution)/shard_map/ppermute | solution.py:343
  95.7 1.9 %collective-permute-start.11 = (bf16[4,16,1152]{2,1,0:T(8,128)(2,1)S(1)}, bf16[4,16,1152]{2,1,0:T(8,128)(2,1)S(1)}, u32[]{:S(2)}, u32[]{:S(2)}) collective-permute-start(bf16[4,16,1152]{2,1,0:T(8,128)(2,1)S(1)} %get-tuple-element.29), channel_id=1, source_target_pairs={{0,64},{32,96},{64,0},{96,32},{1,65},{33,97},{65,1},{97,33},{2,66}... | collective-permute-start | bytes 442376 | tf_op jit(solution)/shard_map/ppermute | solution.py:343
  97.7 2.5 %collective-permute-start.12 = (bf16[4,16,1152]{2,1,0:T(8,128)(2,1)S(1)}, bf16[4,16,1152]{2,1,0:T(8,128)(2,1)S(1)}, u32[]{:S(2)}, u32[]{:S(2)}) collective-permute-start(bf16[4,16,1152]{2,1,0:T(8,128)(2,1)S(1)} %get-tuple-element.30), channel_id=1, source_target_pairs={{0,32},{32,64},{64,96},{96,0},{1,33},{33,65},{65,97},{97,1},{2,34}... | collective-permute-start | bytes 442376 | tf_op jit(solution)/shard_map/ppermute | solution.py:343
  100.1 0.8 collective-permute-done.10.refs_1_
  100.9 3.4 %collective-permute-done.11.refs_2_ = bf16[4,16,1152]{2,1,0:T(8,128)(2,1)S(1)} collective-permute-done((bf16[4,16,1152]{2,1,0:T(8,128)(2,1)S(1)}, bf16[4,16,1152]{2,1,0:T(8,128)(2,1)S(1)}, u32[]{:S(2)}, u32[]{:S(2)}) %collective-permute-start.11) | collective-permute-done | bytes 147488 | tf_op jit(solution)/shard_map/ppermute | solution.py:343
  104.4 2.0 %collective-permute-done.12.refs_3_ = bf16[4,16,1152]{2,1,0:T(8,128)(2,1)S(1)} collective-permute-done((bf16[4,16,1152]{2,1,0:T(8,128)(2,1)S(1)}, bf16[4,16,1152]{2,1,0:T(8,128)(2,1)S(1)}, u32[]{:S(2)}, u32[]{:S(2)}) %collective-permute-start.12) | collective-permute-done | bytes 147488 | tf_op jit(solution)/shard_map/ppermute | solution.py:343
  106.4 0.0 all-to-all-done.2.space_ref
  106.4 1.7 %combine.1 = bf16[2,128,1152]{2,1,0:T(8,128)(2,1)} custom-call(s32[1]{0:T(128)} %bitcast.core_ref, s32[1]{0:T(128)} %bitcast.1.x_ref, bf16[16,2,72,128]{3,2,1,0:T(8,128)(2,1)S(1)} %all-to-all-done.2.space_ref, bf16[4,16,1152]{2,1,0:T(8,128)(2,1)S(1)} %get-tuple-element.27.refs_0_, bf16[4,16,1152]{2,1,0:T(8,128)(2,1)S(1)} %collective-permute-done.10.refs_1_, ...), custom_call_target="tpu_custom_call" | custom-call | tf_op jit(solution)/shard_map/combine/pallas_call | solution.py:327
  (15 shorter events, 0.0 us)
Async XLA Ops:
  0.0 0.7 copy-start.4
  0.7 0.7 copy-start.6
  4.4 29.2 %all-to-all-start = ((bf16[16,3,72,128]{3,2,1,0:T(8,128)(2,1)}), bf16[16,3,72,128]{3,2,1,0:T(8,128)(2,1)S(1)}, u32[]{:S(2)}, u32[]{:S(2)}) async-start(bf16[16,3,72,128]{3,2,1,0:T(8,128)(2,1)} %get-tuple-element.18.after_ref), calls=%async_computation | async-start | bytes 1769472 | tf_op jit(solution)/shard_map/all_to_all | solution.py:373
  13.6 16.8 %copy-start.5 = (s32[2]{0:T(128)S(1)}, s32[2]{0:T(128)}, u32[]{:S(2)}) copy-start(s32[2]{0:T(128)} %refs_4_.1) | copy-start | bytes 28
  13.6 16.8 %copy-start.7 = (s32[2]{0:T(128)S(1)}, s32[2]{0:T(128)}, u32[]{:S(2)}) copy-start(s32[2]{0:T(128)} %refs_5_.1) | copy-start | bytes 28
  16.1 24.1 %collective-permute-start.1 = (bf16[6,32,1152]{2,1,0:T(8,128)(2,1)}, bf16[6,32,1152]{2,1,0:T(8,128)(2,1)S(1)}, u32[]{:S(2)}, u32[]{:S(2)}) collective-permute-start(bf16[6,32,1152]{2,1,0:T(8,128)(2,1)} %get-tuple-element.22), channel_id=1, source_target_pairs={{0,32},{32,64},{64,96},{96,0},{1,33},{33,65},{65,97},{97,1},{2,34}... | collective-permute-start | bytes 1327112 | tf_op jit(solution)/shard_map/ppermute | solution.py:343
  19.3 21.4 %collective-permute-start.2 = (bf16[6,32,1152]{2,1,0:T(8,128)(2,1)}, bf16[6,32,1152]{2,1,0:T(8,128)(2,1)S(1)}, u32[]{:S(2)}, u32[]{:S(2)}) collective-permute-start(bf16[6,32,1152]{2,1,0:T(8,128)(2,1)} %get-tuple-element.23), channel_id=1, source_target_pairs={{0,64},{32,96},{64,0},{96,32},{1,65},{33,97},{65,1},{97,33},{2,66}... | collective-permute-start | bytes 1327112 | tf_op jit(solution)/shard_map/ppermute | solution.py:343
  23.6 18.9 %collective-permute-start.3 = (bf16[6,32,1152]{2,1,0:T(8,128)(2,1)S(1)}, bf16[6,32,1152]{2,1,0:T(8,128)(2,1)S(1)}, u32[]{:S(2)}, u32[]{:S(2)}) collective-permute-start(bf16[6,32,1152]{2,1,0:T(8,128)(2,1)S(1)} %get-tuple-element.24), channel_id=1, source_target_pairs={{0,96},{32,0},{64,32},{96,64},{1,97},{33,1},{65,33},{97,65},{2,98}... | collective-permute-start | bytes 1327112 | tf_op jit(solution)/shard_map/ppermute | solution.py:343
  26.7 16.9 %collective-permute-start = (s32[2]{0:T(128)S(1)}, s32[2]{0:T(128)S(1)}, u32[]{:S(2)}, u32[]{:S(2)}) collective-permute-start(s32[2]{0:T(128)S(1)} %get-tuple-element.21), channel_id=1, source_target_pairs={{0,496},{16,0},{32,16},{48,32},{64,48},{80,64},{96,80},{112,96},{1... | collective-permute-start | bytes 32 | tf_op jit(solution)/shard_map/ppermute | solution.py:343
  42.5 1.1 %copy-start = (bf16[6,32,1152]{2,1,0:T(8,128)(2,1)}, bf16[6,32,1152]{2,1,0:T(8,128)(2,1)S(1)}, u32[]{:S(2)}) copy-start(bf16[6,32,1152]{2,1,0:T(8,128)(2,1)S(1)} %collective-permute-done.3.refs_3_) | copy-start | bytes 1327108
  43.6 31.8 %all-to-all-start.1 = ((bf16[16,3,72,128]{3,2,1,0:T(8,128)(2,1)}), bf16[16,3,72,128]{3,2,1,0:T(8,128)(2,1)S(1)}, u32[]{:S(2)}, u32[]{:S(2)}) async-start(bf16[16,3,72,128]{3,2,1,0:T(8,128)(2,1)} %once_there.2), calls=%async_computation.1 | async-start | bytes 1769472 | tf_op jit(solution)/shard_map/all_to_all | solution.py:373
  50.6 7.8 %collective-permute-start.4 = (bf16[4,6,16,1152]{3,2,1,0:T(8,128)(2,1)S(1)}, bf16[4,6,16,1152]{3,2,1,0:T(8,128)(2,1)S(1)}, u32[]{:S(2)}, u32[]{:S(2)}) collective-permute-start(bf16[4,6,16,1152]{3,2,1,0:T(8,128)(2,1)S(1)} %swap_half.1.refs_2_), channel_id=1, source_target_pairs={{0,16},{16,0},{1,17},{17,1},{2,18},{18,2},{3,19},{19,3},{4,20},{20... | collective-permute-start | bytes 2654216 | tf_op jit(solution)/shard_map/ppermute | solution.py:343
  56.4 10.8 %collective-permute-start.6 = (bf16[16,72,128]{2,1,0:T(8,128)(2,1)}, bf16[16,72,128]{2,1,0:T(8,128)(2,1)}, u32[]{:S(2)}, u32[]{:S(2)}) collective-permute-start(bf16[16,72,128]{2,1,0:T(8,128)(2,1)} %spatial.2.refs_4_), channel_id=1, source_target_pairs={{0,0},{1,1},{2,2},{3,3},{4,36},{5,37},{6,38},{7,39},{8,72},{9,73},... | collective-permute-start | bytes 884744 | tf_op jit(solution)/shard_map/ppermute | solution.py:368
  58.4 1.0 copy-start.1
  61.6 6.3 %collective-permute-start.8 = (bf16[8,16,1152]{2,1,0:T(8,128)(2,1)S(1)}, bf16[8,16,1152]{2,1,0:T(8,128)(2,1)S(1)}, u32[]{:S(2)}, u32[]{:S(2)}) collective-permute-start(bf16[8,16,1152]{2,1,0:T(8,128)(2,1)S(1)} %get-tuple-element.26), channel_id=1, source_target_pairs={{0,16},{16,0},{1,17},{17,1},{2,18},{18,2},{3,19},{19,3},{4,20},{20... | collective-permute-start | bytes 884744 | tf_op jit(solution)/shard_map/ppermute | solution.py:343
  65.2 16.3 %collective-permute-start.5 = (bf16[16,72,128]{2,1,0:T(8,128)(2,1)}, bf16[16,72,128]{2,1,0:T(8,128)(2,1)S(1)}, u32[]{:S(2)}, u32[]{:S(2)}) collective-permute-start(bf16[16,72,128]{2,1,0:T(8,128)(2,1)} %spatial.2.refs_4_), channel_id=1, source_target_pairs={{16,0},{32,16},{48,32},{64,48},{80,64},{96,80},{112,96},{17,1},{33... | collective-permute-start | bytes 884744 | tf_op jit(solution)/shard_map/ppermute | solution.py:369
  67.2 14.3 %collective-permute-start.7 = (bf16[16,72,128]{2,1,0:T(8,128)(2,1)}, bf16[16,72,128]{2,1,0:T(8,128)(2,1)S(1)}, u32[]{:S(2)}, u32[]{:S(2)}) collective-permute-start(bf16[16,72,128]{2,1,0:T(8,128)(2,1)} %once_there.3), channel_id=1, source_target_pairs={{0,496},{1,497},{2,498},{3,499},{36,500},{37,501},{38,502},{39,503... | collective-permute-start | bytes 884744 | tf_op jit(solution)/shard_map/ppermute | solution.py:369
  67.9 13.5 %collective-permute-start.9 = (bf16[2,16,1152]{2,1,0:T(8,128)(2,1)S(1)}, bf16[2,16,1152]{2,1,0:T(8,128)(2,1)S(1)}, u32[]{:S(2)}, u32[]{:S(2)}) collective-permute-start(bf16[2,16,1152]{2,1,0:T(8,128)(2,1)S(1)} %edge.1), channel_id=1, source_target_pairs={{16,400},{48,432},{80,464},{112,496},{144,16},{176,48},{208,80},{2... | collective-permute-start | bytes 221192 | tf_op jit(solution)/shard_map/ppermute | solution.py:402
  81.4 25.0 %copy-start.2 = (f32[30,1152]{1,0:T(8,128)S(1)}, f32[30,1152]{1,0:T(8,128)}, u32[]{:S(2)}) copy-start(f32[30,1152]{1,0:T(8,128)} %refs_7_.1) | copy-start | bytes 414724
  81.4 25.0 %copy-start.3 = (f32[30,1152]{1,0:T(8,128)S(1)}, f32[30,1152]{1,0:T(8,128)}, u32[]{:S(2)}) copy-start(f32[30,1152]{1,0:T(8,128)} %refs_8_.1) | copy-start | bytes 414724
  81.4 25.0 %copy-start.8 = (f32[64]{0:T(128)S(1)}, f32[64]{0:T(128)}, u32[]{:S(2)}) copy-start(f32[64]{0:T(128)} %refs_9_.1) | copy-start | bytes 772
  82.4 24.0 %all-to-all-start.2 = ((bf16[16,2,72,128]{3,2,1,0:T(8,128)(2,1)}), bf16[16,2,72,128]{3,2,1,0:T(8,128)(2,1)S(1)}, u32[]{:S(2)}, u32[]{:S(2)}) async-start(bf16[16,2,72,128]{3,2,1,0:T(8,128)(2,1)} %beside.1), calls=%async_computation.2 | async-start | bytes 1179648 | tf_op jit(solution)/shard_map/all_to_all | solution.py:373
  91.2 9.8 %collective-permute-start.10 = (bf16[4,16,1152]{2,1,0:T(8,128)(2,1)S(1)}, bf16[4,16,1152]{2,1,0:T(8,128)(2,1)S(1)}, u32[]{:S(2)}, u32[]{:S(2)}) collective-permute-start(bf16[4,16,1152]{2,1,0:T(8,128)(2,1)S(1)} %get-tuple-element.28), channel_id=1, source_target_pairs={{0,96},{32,0},{64,32},{96,64},{1,97},{33,1},{65,33},{97,65},{2,98}... | collective-permute-start | bytes 442376 | tf_op jit(solution)/shard_map/ppermute | solution.py:343
  95.7 8.6 %collective-permute-start.11 = (bf16[4,16,1152]{2,1,0:T(8,128)(2,1)S(1)}, bf16[4,16,1152]{2,1,0:T(8,128)(2,1)S(1)}, u32[]{:S(2)}, u32[]{:S(2)}) collective-permute-start(bf16[4,16,1152]{2,1,0:T(8,128)(2,1)S(1)} %get-tuple-element.29), channel_id=1, source_target_pairs={{0,64},{32,96},{64,0},{96,32},{1,65},{33,97},{65,1},{97,33},{2,66}... | collective-permute-start | bytes 442376 | tf_op jit(solution)/shard_map/ppermute | solution.py:343
  97.7 8.7 %collective-permute-start.12 = (bf16[4,16,1152]{2,1,0:T(8,128)(2,1)S(1)}, bf16[4,16,1152]{2,1,0:T(8,128)(2,1)S(1)}, u32[]{:S(2)}, u32[]{:S(2)}) collective-permute-start(bf16[4,16,1152]{2,1,0:T(8,128)(2,1)S(1)} %get-tuple-element.30), channel_id=1, source_target_pairs={{0,32},{32,64},{64,96},{96,0},{1,33},{33,65},{65,97},{97,1},{2,34}... | collective-permute-start | bytes 442376 | tf_op jit(solution)/shard_map/ppermute | solution.py:343

commit v5 on v4

--- a/solution.py
+++ b/solution.py
@@ -160,40 +160,54 @@
     )(resident(near), resident(far), resident(crossed), *after)
 
 
+def piece(refs, step, row):
+    if step == 2:
+        return refs[2 + row // 3], row % 3
+    return refs[step + (step > 2)], row
+
+
+def put(refs, step, row, tokens):
+    ref, place = piece(refs, step, row)
+    ref[place] = tokens
+
+
 def spread_kernel(x_ref, q_ref, kv_ref, after_ref, *o_refs):
     del after_ref
-    for step, o_ref in enumerate(o_refs):
+    for step in range(CHIPS):
         column = lax.rem(x_ref[0] + step, CHIPS) * WIDE
         rows = pl.ds(pl.multiple_of(column, WIDE), WIDE)
         for frame in range(2):
-            o_ref[frame] = q_ref[frame, rows]
+            put(o_refs, step, frame, q_ref[frame, rows])
             for part in range(2):
-                o_ref[2 + 2 * frame + part] = kv_ref[frame, part, rows]
+                put(o_refs, step, 2 + 2 * frame + part, kv_ref[frame, part, rows])
 
 
 def spread(x, query, kv, after):
     return pl.pallas_call(
         spread_kernel,
         in_specs=[SMEM, VMEM, VMEM, ANY],
-        out_specs=[VMEM] * CHIPS,
-        out_shape=[jax.ShapeDtypeStruct((6, WIDE, D), BF16)] * CHIPS,
+        out_specs=[VMEM] * (CHIPS + 1),
+        out_shape=[
+            jax.ShapeDtypeStruct((rows, WIDE, D), BF16) for rows in (6, 6, 3, 3, 6)
+        ],
         compiler_params=PARAMS,
         name="spread",
     )(x, outside(query), outside(kv), after)
 
 
 def swap_kernel(core_ref, *refs):
-    blocks, o_ref = refs[:CHIPS], refs[-1]
+    blocks, o_ref = refs[: CHIPS + 1], refs[-1]
     half = pl.ds(pl.multiple_of((1 - core_ref[0]) * SHARE, SHARE), SHARE)
     for step in range(CHIPS):
         for row in range(6):
-            o_ref[step, row] = blocks[step][row, half]
+            ref, place = piece(blocks, step, row)
+            o_ref[step, row] = ref[place, half]
 
 
 def swap_half(core, blocks, after):
     return pl.pallas_call(
         swap_kernel,
-        in_specs=[SMEM] + [VMEM] * CHIPS + [ANY] * len(after),
+        in_specs=[SMEM] + [VMEM] * (CHIPS + 1) + [ANY] * len(after),
         out_specs=VMEM,
         out_shape=jax.ShapeDtypeStruct((CHIPS, 6, SHARE, D), BF16),
         compiler_params=PARAMS,
@@ -202,8 +216,8 @@
 
 
 def temporal_kernel(core_ref, *refs):
-    blocks, other_ref = refs[:CHIPS], refs[CHIPS]
-    mine_ref, send_ref, query, key, value = refs[CHIPS + 1 :]
+    blocks, other_ref = refs[: CHIPS + 1], refs[CHIPS + 1]
+    mine_ref, send_ref, query, key, value = refs[CHIPS + 2 :]
     half = pl.ds(pl.multiple_of(core_ref[0] * SHARE, SHARE), SHARE)
     rows = PLEN * SHARE
     token_of_row = lax.broadcasted_iota(jnp.int32, (rows, rows), 0) % SHARE
@@ -216,7 +230,8 @@
                 start = ((step * 2 + side) * 2 + frame) * SHARE
                 place = slice(start, start + SHARE)
                 for to, row in ((query, frame), (key, 2 + 2 * frame), (value, 3 + 2 * frame)):
-                    to[place] = other_ref[step, row] if side else blocks[step][row, half]
+                    ref, found = piece(blocks, step, row)
+                    to[place] = other_ref[step, row] if side else ref[found, half]
 
     tiles = [jnp.zeros((rows, 128), F32) for _ in range(D // 128)]
     for head in range(HEADS):
@@ -252,7 +267,7 @@
 def temporal_share(core, blocks, other):
     return pl.pallas_call(
         temporal_kernel,
-        in_specs=[SMEM] + [VMEM] * (CHIPS + 1),
+        in_specs=[SMEM] + [VMEM] * (CHIPS + 2),
         out_specs=[VMEM, VMEM],
         out_shape=[pltpu.VMEM((2 * CHIPS, SHARE, D), BF16)] * 2,
         scratch_shapes=[pltpu.VMEM((PLEN * SHARE, D), BF16)] * 3,
@@ -390,8 +405,11 @@
     indices = shift(indices, QUEUE, -1)
     blocks = spread(x_arg, temporal_query, temporal_kv, packed)
     packed, _ = pack(1, spatial_qkv, timestep, noise_level, blocks[:1])
-    moved = {k: shift(blocks[k], "x", k) for k in (2, 3, 1)}
-    blocks = [blocks[0]] + [moved[k] for k in range(1, CHIPS)]
+    between = shift(blocks[3], "x", -1)
+    ahead = shift(blocks[2], "x", 2)
+    behind = shift(blocks[4], "x", -1)
+    beyond = shift(between, "x", -1)
+    blocks = [blocks[0], shift(blocks[1], "x", 1), ahead, beyond, behind]
     first = spatial_frame(early, ())
     half = swap_half(core_arg, blocks, (resident(first),))
     late = exchange(once_there(packed, (indices, half)), "sp")

time: 110 us -> 114 us (1.036)
  starting transfers between devices: 69 us -> 73.9 us
  waiting for transfers between devices: 10.2 us -> 8.54 us
  local copies, waits for them, and re-layouts: 2.36 us -> 3.85 us
    ppermute x9 -> x11, starting transfers between devices: 32.6 us -> 40.6 us  [shift(): lax.ppermute(block, axes, [(i, (i + distance) % size) for i in range(size)])]
    ppermute x1, starting transfers between devices: 7.55 us -> 5.36 us  [per_device(): lax.ppermute(edge(x_arg, mine, theirs), QUEUE, [(i, (i - MEMBERS) % size)...]
    ppermute x9 -> x11, waiting for transfers between devices: 10.2 us -> 8.04 us  [shift(): lax.ppermute(block, axes, [(i, (i + distance) % size) for i in range(size)])]
    unnamed x18 -> x22, local copies, waits for them, and re-layouts: 2.36 us -> 3.85 us
  transfers between devices with their start and end apart: 16 -> 18, of which waited for: 7 -> 4; matrix products, arithmetic and copies ran while one was open for 0% -> 0% of each run, Pallas kernels for 19% -> 18%
where the time goes in v5:
time: 114 us; the launch traced here: 113 us
  starting transfers between devices  73.9 us (65%)
  Pallas kernels  26.1 us (23%)
  waiting for transfers between devices  8.54 us (7%)
  local copies, waits for them, and re-layouts  3.85 us (3%)
    ppermute x11, starting transfers between devices, shift(): lax.ppermute(block, axes, [(i, (i + distance) % size) for i in range(size)])  40.6 us
    all_to_all x3, starting transfers between devices, exchange(): return lax.all_to_all(block, axes, 0, 0)  24 us
    pallas_call x2, Pallas kernels, spatial_frame(): pl.pallas_call(spatial_kernel, in_specs=[VMEM] + [ANY] * len(after), out_...  12.6 us
    ppermute x11, waiting for transfers between devices, shift(): lax.ppermute(block, axes, [(i, (i + distance) % size) for i in range(size)])  8.04 us
    pallas_call x2, Pallas kernels, pack(): pl.pallas_call(pack_kernel, grid=(3,), in_specs=[pl.BlockSpec((1, 1, TOK,...  6.26 us
    ppermute x1, starting transfers between devices, per_device(): lax.ppermute(edge(x_arg, mine, theirs), QUEUE, [(i, (i - MEMBERS) % size)...  5.36 us
    unnamed x22, local copies, waits for them, and re-layouts  3.85 us
    pallas_call x1, Pallas kernels, spread(): pl.pallas_call(spread_kernel, in_specs=[SMEM, VMEM, VMEM, ANY], out_specs...  2.35 us
  transfers between devices with their start and end apart: 18, of which 4 were waited for; matrix products, arithmetic and copies ran while one was open for 0% of the time, Pallas kernels for 18%

profile of v5, /device:TPU:1, one launch (start us, length us, event | category | flops | bytes accessed | tf_op | source)
XLA Modules:
  0.0 112.8 jit_solution(18033840958743213493)
XLA Ops:
  0.0 0.7 copy-done.6
  0.7 0.7 copy-done.8
  1.3 3.1 %pack.2 = (bf16[16,3,72,128]{3,2,1,0:T(8,128)(2,1)}, s32[2]{0:T(128)S(1)}) custom-call(bf16[2,3,128,1152]{3,2,1,0:T(8,128)(2,1)} %x_ref.3, s32[2]{0:T(128)S(1)} %copy-done.6, s32[2]{0:T(128)S(1)} %copy-done.8), custom_call_target="tpu_custom_call" | custom-call | tf_op jit(solution)/shard_map/pack/pallas_call | solution.py:67
  4.4 9.2 %all-to-all-start = ((bf16[16,3,72,128]{3,2,1,0:T(8,128)(2,1)}), bf16[16,3,72,128]{3,2,1,0:T(8,128)(2,1)S(1)}, u32[]{:S(2)}, u32[]{:S(2)}) async-start(bf16[16,3,72,128]{3,2,1,0:T(8,128)(2,1)} %get-tuple-element.19.after_ref), calls=%async_computation | async-start | bytes 1769472 | tf_op jit(solution)/shard_map/all_to_all | solution.py:388
  13.6 0.0 copy-start.7
  13.6 0.0 copy-start.9
  13.7 2.3 %spread.1 = (bf16[6,32,1152]{2,1,0:T(8,128)(2,1)S(1)}, bf16[6,32,1152]{2,1,0:T(8,128)(2,1)}, bf16[3,32,1152]{2,1,0:T(8,128)(2,1)S(1)}, bf16[3,32,1152]{2,1,0:T(8,128)(2,1)S(1)}, bf16[6,32,1152]{2,1,0:T(8,128)(2,1)S(1)}) custom-call(s32[1]{0:T(128)} %bitcast.1.x_ref, bf16[2,128,1152]{2,1,0:T(8,128)(2,1)} %q_ref.1, bf16[2,2,128,1152]{3,2,1,0:T(8,128)(2,1)} %kv_ref.1, ...), custom_call_target="tpu_custom_call" | custom-call | tf_op jit(solution)/shard_map/spread/pallas_call | solution.py:186
  16.0 4.4 %collective-permute-start.3 = (bf16[3,32,1152]{2,1,0:T(8,128)(2,1)S(1)}, bf16[3,32,1152]{2,1,0:T(8,128)(2,1)}, u32[]{:S(2)}, u32[]{:S(2)}) collective-permute-start(bf16[3,32,1152]{2,1,0:T(8,128)(2,1)S(1)} %get-tuple-element.25), channel_id=1, source_target_pairs={{0,96},{32,0},{64,32},{96,64},{1,97},{33,1},{65,33},{97,65},{2,98}... | collective-permute-start | bytes 663560 | tf_op jit(solution)/shard_map/ppermute | solution.py:358
  20.4 1.9 %collective-permute-start.1 = (bf16[6,32,1152]{2,1,0:T(8,128)(2,1)}, bf16[6,32,1152]{2,1,0:T(8,128)(2,1)S(1)}, u32[]{:S(2)}, u32[]{:S(2)}) collective-permute-start(bf16[6,32,1152]{2,1,0:T(8,128)(2,1)} %get-tuple-element.23), channel_id=1, source_target_pairs={{0,32},{32,64},{64,96},{96,0},{1,33},{33,65},{65,97},{97,1},{2,34}... | collective-permute-start | bytes 1327112 | tf_op jit(solution)/shard_map/ppermute | solution.py:358
  22.3 4.6 %collective-permute-start.5 = (bf16[6,32,1152]{2,1,0:T(8,128)(2,1)S(1)}, bf16[6,32,1152]{2,1,0:T(8,128)(2,1)S(1)}, u32[]{:S(2)}, u32[]{:S(2)}) collective-permute-start(bf16[6,32,1152]{2,1,0:T(8,128)(2,1)S(1)} %get-tuple-element.26), channel_id=1, source_target_pairs={{0,96},{32,0},{64,32},{96,64},{1,97},{33,1},{65,33},{97,65},{2,98}... | collective-permute-start | bytes 1327112 | tf_op jit(solution)/shard_map/ppermute | solution.py:358
  26.9 1.9 %collective-permute-start.2 = (bf16[3,32,1152]{2,1,0:T(8,128)(2,1)S(1)}, bf16[3,32,1152]{2,1,0:T(8,128)(2,1)S(1)}, u32[]{:S(2)}, u32[]{:S(2)}) collective-permute-start(bf16[3,32,1152]{2,1,0:T(8,128)(2,1)S(1)} %get-tuple-element.24), channel_id=1, source_target_pairs={{0,64},{32,96},{64,0},{96,32},{1,65},{33,97},{65,1},{97,33},{2,66}... | collective-permute-start | bytes 663560 | tf_op jit(solution)/shard_map/ppermute | solution.py:358
  28.8 3.1 %collective-permute-start.4 = (bf16[3,32,1152]{2,1,0:T(8,128)(2,1)}, bf16[3,32,1152]{2,1,0:T(8,128)(2,1)S(1)}, u32[]{:S(2)}, u32[]{:S(2)}) collective-permute-start(bf16[3,32,1152]{2,1,0:T(8,128)(2,1)} %collective-permute-done.3), channel_id=1, source_target_pairs={{0,96},{32,0},{64,32},{96,64},{1,97},{33,1},{65,33},{97,65},{2,98}... | collective-permute-start | bytes 663560 | tf_op jit(solution)/shard_map/ppermute | solution.py:358
  31.9 4.0 %collective-permute-start = (s32[2]{0:T(128)S(1)}, s32[2]{0:T(128)S(1)}, u32[]{:S(2)}, u32[]{:S(2)}) collective-permute-start(s32[2]{0:T(128)S(1)} %get-tuple-element.22), channel_id=1, source_target_pairs={{0,496},{16,0},{32,16},{48,32},{64,48},{80,64},{96,80},{112,96},{1... | collective-permute-start | bytes 32 | tf_op jit(solution)/shard_map/ppermute | solution.py:358
  36.0 3.1 %pack.3 = (bf16[16,3,72,128]{3,2,1,0:T(8,128)(2,1)}, s32[2]{0:T(128)}) custom-call(bf16[2,3,128,1152]{3,2,1,0:T(8,128)(2,1)} %x_ref.3, s32[2]{0:T(128)S(1)} %copy-done.7, s32[2]{0:T(128)S(1)} %copy-done.9, bf16[6,32,1152]{2,1,0:T(8,128)(2,1)S(1)} %get-tuple-element.20.refs_0_), custom_call_target="tpu_custom_call" | custom-call | tf_op jit(solution)/shard_map/pack/pallas_call | solution.py:67
  39.1 0.0 all-to-all-done.x_ref
  39.1 6.7 %spatial.2.refs_5_ = bf16[16,72,128]{2,1,0:T(8,128)(2,1)} custom-call(bf16[16,3,72,128]{3,2,1,0:T(8,128)(2,1)S(1)} %all-to-all-done.x_ref), custom_call_target="tpu_custom_call" | custom-call | tf_op jit(solution)/shard_map/spatial/pallas_call | solution.py:134
  45.8 0.0 collective-permute-done.4.refs_3_
  45.8 0.0 collective-permute-done.1.refs_1_
  45.8 0.1 swap_half.1.refs_2_
  45.9 0.0 collective-permute-done.refs_1_.refs_6_
  45.9 0.6 copy-done
  46.5 0.1 copy-done.2
  46.5 7.2 %all-to-all-start.1 = ((bf16[16,3,72,128]{3,2,1,0:T(8,128)(2,1)}), bf16[16,3,72,128]{3,2,1,0:T(8,128)(2,1)S(1)}, u32[]{:S(2)}, u32[]{:S(2)}) async-start(bf16[16,3,72,128]{3,2,1,0:T(8,128)(2,1)} %once_there.2), calls=%async_computation.1 | async-start | bytes 1769472 | tf_op jit(solution)/shard_map/all_to_all | solution.py:388
  53.8 9.9 %collective-permute-start.6 = (bf16[4,6,16,1152]{3,2,1,0:T(8,128)(2,1)S(1)}, bf16[4,6,16,1152]{3,2,1,0:T(8,128)(2,1)S(1)}, u32[]{:S(2)}, u32[]{:S(2)}) collective-permute-start(bf16[4,6,16,1152]{3,2,1,0:T(8,128)(2,1)S(1)} %swap_half.1.refs_2_), channel_id=1, source_target_pairs={{0,16},{16,0},{1,17},{17,1},{2,18},{18,2},{3,19},{19,3},{4,20},{20... | collective-permute-start | bytes 2654216 | tf_op jit(solution)/shard_map/ppermute | solution.py:358
  63.6 1.4 %collective-permute-start.8 = (bf16[16,72,128]{2,1,0:T(8,128)(2,1)}, bf16[16,72,128]{2,1,0:T(8,128)(2,1)}, u32[]{:S(2)}, u32[]{:S(2)}) collective-permute-start(bf16[16,72,128]{2,1,0:T(8,128)(2,1)} %spatial.2.refs_5_), channel_id=1, source_target_pairs={{0,0},{1,1},{2,2},{3,3},{4,36},{5,37},{6,38},{7,39},{8,72},{9,73},... | collective-permute-start | bytes 884744 | tf_op jit(solution)/shard_map/ppermute | solution.py:383
  65.0 0.6 collective-permute-done.6.refs_5_
  65.7 0.9 copy-done.1
  66.6 0.9 copy-done.3
  67.5 2.2 %temporal.1 = (bf16[8,16,1152]{2,1,0:T(8,128)(2,1)S(1)}, bf16[8,16,1152]{2,1,0:T(8,128)(2,1)S(1)}) custom-call(s32[1]{0:T(128)} %bitcast.core_ref, bf16[6,32,1152]{2,1,0:T(8,128)(2,1)S(1)} %get-tuple-element.20.refs_0_, bf16[6,32,1152]{2,1,0:T(8,128)(2,1)S(1)} %collective-permute-done.1.refs_1_, bf16[3,32,1152]{2,1,0:T(8,128)(2,1)S(1)} %copy-done.1, ...), custom_call_target="tpu_custom_call" | custom-call | tf_op jit(solution)/shard_map/temporal/pallas_call | solution.py:268
  69.7 3.6 %collective-permute-start.10 = (bf16[8,16,1152]{2,1,0:T(8,128)(2,1)S(1)}, bf16[8,16,1152]{2,1,0:T(8,128)(2,1)S(1)}, u32[]{:S(2)}, u32[]{:S(2)}) collective-permute-start(bf16[8,16,1152]{2,1,0:T(8,128)(2,1)S(1)} %get-tuple-element.28), channel_id=1, source_target_pairs={{0,16},{16,0},{1,17},{17,1},{2,18},{18,2},{3,19},{19,3},{4,20},{20... | collective-permute-start | bytes 884744 | tf_op jit(solution)/shard_map/ppermute | solution.py:358
  73.4 1.9 %collective-permute-start.7 = (bf16[16,72,128]{2,1,0:T(8,128)(2,1)}, bf16[16,72,128]{2,1,0:T(8,128)(2,1)S(1)}, u32[]{:S(2)}, u32[]{:S(2)}) collective-permute-start(bf16[16,72,128]{2,1,0:T(8,128)(2,1)} %spatial.2.refs_5_), channel_id=1, source_target_pairs={{16,0},{32,16},{48,32},{64,48},{80,64},{96,80},{112,96},{17,1},{33... | collective-permute-start | bytes 884744 | tf_op jit(solution)/shard_map/ppermute | solution.py:384
  75.3 0.0 collective-permute-done.8.refs_0_
  75.3 0.7 collective-permute-start.9
  76.0 5.4 %collective-permute-start.11 = (bf16[2,16,1152]{2,1,0:T(8,128)(2,1)S(1)}, bf16[2,16,1152]{2,1,0:T(8,128)(2,1)S(1)}, u32[]{:S(2)}, u32[]{:S(2)}) collective-permute-start(bf16[2,16,1152]{2,1,0:T(8,128)(2,1)S(1)} %edge.1), channel_id=1, source_target_pairs={{16,400},{48,432},{80,464},{112,496},{144,16},{176,48},{208,80},{2... | collective-permute-start | bytes 221192 | tf_op jit(solution)/shard_map/ppermute | solution.py:420
  81.4 5.9 %spatial.3.refs_0_.near_ref = bf16[16,72,128]{2,1,0:T(8,128)(2,1)S(1)} custom-call(bf16[16,3,72,128]{3,2,1,0:T(8,128)(2,1)S(1)} %all-to-all-done.1.x_ref, bf16[8,16,1152]{2,1,0:T(8,128)(2,1)S(1)} %get-tuple-element.27.refs_0_.refs_1_.mine_ref), custom_call_target="tpu_custom_call" | custom-call | tf_op jit(solution)/shard_map/spatial/pallas_call | solution.py:134
  87.4 0.0 copy-start.4
  87.4 0.0 copy-start.5
  87.4 0.0 copy-start.10
  87.4 0.1 to_send_back.1
  87.5 0.9 beside.1
  88.4 7.6 %all-to-all-start.2 = ((bf16[16,2,72,128]{3,2,1,0:T(8,128)(2,1)}), bf16[16,2,72,128]{3,2,1,0:T(8,128)(2,1)S(1)}, u32[]{:S(2)}, u32[]{:S(2)}) async-start(bf16[16,2,72,128]{3,2,1,0:T(8,128)(2,1)} %beside.1), calls=%async_computation.2 | async-start | bytes 1179648 | tf_op jit(solution)/shard_map/all_to_all | solution.py:388
  96.0 2.2 %collective-permute-start.12 = (bf16[4,16,1152]{2,1,0:T(8,128)(2,1)S(1)}, bf16[4,16,1152]{2,1,0:T(8,128)(2,1)S(1)}, u32[]{:S(2)}, u32[]{:S(2)}) collective-permute-start(bf16[4,16,1152]{2,1,0:T(8,128)(2,1)S(1)} %get-tuple-element.30), channel_id=1, source_target_pairs={{0,96},{32,0},{64,32},{96,64},{1,97},{33,1},{65,33},{97,65},{2,98}... | collective-permute-start | bytes 442376 | tf_op jit(solution)/shard_map/ppermute | solution.py:358
  98.2 1.9 %collective-permute-start.13 = (bf16[4,16,1152]{2,1,0:T(8,128)(2,1)S(1)}, bf16[4,16,1152]{2,1,0:T(8,128)(2,1)S(1)}, u32[]{:S(2)}, u32[]{:S(2)}) collective-permute-start(bf16[4,16,1152]{2,1,0:T(8,128)(2,1)S(1)} %get-tuple-element.31), channel_id=1, source_target_pairs={{0,64},{32,96},{64,0},{96,32},{1,65},{33,97},{65,1},{97,33},{2,66}... | collective-permute-start | bytes 442376 | tf_op jit(solution)/shard_map/ppermute | solution.py:358
  100.1 3.1 %collective-permute-start.14 = (bf16[4,16,1152]{2,1,0:T(8,128)(2,1)S(1)}, bf16[4,16,1152]{2,1,0:T(8,128)(2,1)S(1)}, u32[]{:S(2)}, u32[]{:S(2)}) collective-permute-start(bf16[4,16,1152]{2,1,0:T(8,128)(2,1)S(1)} %get-tuple-element.32), channel_id=1, source_target_pairs={{0,32},{32,64},{64,96},{96,0},{1,33},{33,65},{65,97},{97,1},{2,34}... | collective-permute-start | bytes 442376 | tf_op jit(solution)/shard_map/ppermute | solution.py:358
  103.2 3.8 %collective-permute-done.13.refs_2_ = bf16[4,16,1152]{2,1,0:T(8,128)(2,1)S(1)} collective-permute-done((bf16[4,16,1152]{2,1,0:T(8,128)(2,1)S(1)}, bf16[4,16,1152]{2,1,0:T(8,128)(2,1)S(1)}, u32[]{:S(2)}, u32[]{:S(2)}) %collective-permute-start.13) | collective-permute-done | bytes 147488 | tf_op jit(solution)/shard_map/ppermute | solution.py:358
  107.0 3.6 %collective-permute-done.14.refs_3_ = bf16[4,16,1152]{2,1,0:T(8,128)(2,1)S(1)} collective-permute-done((bf16[4,16,1152]{2,1,0:T(8,128)(2,1)S(1)}, bf16[4,16,1152]{2,1,0:T(8,128)(2,1)S(1)}, u32[]{:S(2)}, u32[]{:S(2)}) %collective-permute-start.14) | collective-permute-done | bytes 147488 | tf_op jit(solution)/shard_map/ppermute | solution.py:358
  110.6 0.5 all-to-all-done.2.space_ref
  111.1 1.7 %combine.1 = bf16[2,128,1152]{2,1,0:T(8,128)(2,1)} custom-call(s32[1]{0:T(128)} %bitcast.core_ref, s32[1]{0:T(128)} %bitcast.1.x_ref, bf16[16,2,72,128]{3,2,1,0:T(8,128)(2,1)S(1)} %all-to-all-done.2.space_ref, bf16[4,16,1152]{2,1,0:T(8,128)(2,1)S(1)} %get-tuple-element.29.refs_0_, bf16[4,16,1152]{2,1,0:T(8,128)(2,1)S(1)} %collective-permute-done.12.refs_1_, ...), custom_call_target="tpu_custom_call" | custom-call | tf_op jit(solution)/shard_map/combine/pallas_call | solution.py:342
  (23 shorter events, 0.1 us)
Async XLA Ops:
  0.0 0.7 copy-start.6
  0.7 0.7 copy-start.8
  4.4 34.7 %all-to-all-start = ((bf16[16,3,72,128]{3,2,1,0:T(8,128)(2,1)}), bf16[16,3,72,128]{3,2,1,0:T(8,128)(2,1)S(1)}, u32[]{:S(2)}, u32[]{:S(2)}) async-start(bf16[16,3,72,128]{3,2,1,0:T(8,128)(2,1)} %get-tuple-element.19.after_ref), calls=%async_computation | async-start | bytes 1769472 | tf_op jit(solution)/shard_map/all_to_all | solution.py:388
  13.6 22.3 %copy-start.7 = (s32[2]{0:T(128)S(1)}, s32[2]{0:T(128)}, u32[]{:S(2)}) copy-start(s32[2]{0:T(128)} %refs_4_.1) | copy-start | bytes 28
  13.6 22.3 %copy-start.9 = (s32[2]{0:T(128)S(1)}, s32[2]{0:T(128)}, u32[]{:S(2)}) copy-start(s32[2]{0:T(128)} %refs_5_.1) | copy-start | bytes 28
  16.0 12.8 %collective-permute-start.3 = (bf16[3,32,1152]{2,1,0:T(8,128)(2,1)S(1)}, bf16[3,32,1152]{2,1,0:T(8,128)(2,1)}, u32[]{:S(2)}, u32[]{:S(2)}) collective-permute-start(bf16[3,32,1152]{2,1,0:T(8,128)(2,1)S(1)} %get-tuple-element.25), channel_id=1, source_target_pairs={{0,96},{32,0},{64,32},{96,64},{1,97},{33,1},{65,33},{97,65},{2,98}... | collective-permute-start | bytes 663560 | tf_op jit(solution)/shard_map/ppermute | solution.py:358
  20.4 25.4 %collective-permute-start.1 = (bf16[6,32,1152]{2,1,0:T(8,128)(2,1)}, bf16[6,32,1152]{2,1,0:T(8,128)(2,1)S(1)}, u32[]{:S(2)}, u32[]{:S(2)}) collective-permute-start(bf16[6,32,1152]{2,1,0:T(8,128)(2,1)} %get-tuple-element.23), channel_id=1, source_target_pairs={{0,32},{32,64},{64,96},{96,0},{1,33},{33,65},{65,97},{97,1},{2,34}... | collective-permute-start | bytes 1327112 | tf_op jit(solution)/shard_map/ppermute | solution.py:358
  22.3 23.5 %collective-permute-start.5 = (bf16[6,32,1152]{2,1,0:T(8,128)(2,1)S(1)}, bf16[6,32,1152]{2,1,0:T(8,128)(2,1)S(1)}, u32[]{:S(2)}, u32[]{:S(2)}) collective-permute-start(bf16[6,32,1152]{2,1,0:T(8,128)(2,1)S(1)} %get-tuple-element.26), channel_id=1, source_target_pairs={{0,96},{32,0},{64,32},{96,64},{1,97},{33,1},{65,33},{97,65},{2,98}... | collective-permute-start | bytes 1327112 | tf_op jit(solution)/shard_map/ppermute | solution.py:358
  26.9 18.9 %collective-permute-start.2 = (bf16[3,32,1152]{2,1,0:T(8,128)(2,1)S(1)}, bf16[3,32,1152]{2,1,0:T(8,128)(2,1)S(1)}, u32[]{:S(2)}, u32[]{:S(2)}) collective-permute-start(bf16[3,32,1152]{2,1,0:T(8,128)(2,1)S(1)} %get-tuple-element.24), channel_id=1, source_target_pairs={{0,64},{32,96},{64,0},{96,32},{1,65},{33,97},{65,1},{97,33},{2,66}... | collective-permute-start | bytes 663560 | tf_op jit(solution)/shard_map/ppermute | solution.py:358
  28.8 16.9 %collective-permute-start.4 = (bf16[3,32,1152]{2,1,0:T(8,128)(2,1)}, bf16[3,32,1152]{2,1,0:T(8,128)(2,1)S(1)}, u32[]{:S(2)}, u32[]{:S(2)}) collective-permute-start(bf16[3,32,1152]{2,1,0:T(8,128)(2,1)} %collective-permute-done.3), channel_id=1, source_target_pairs={{0,96},{32,0},{64,32},{96,64},{1,97},{33,1},{65,33},{97,65},{2,98}... | collective-permute-start | bytes 663560 | tf_op jit(solution)/shard_map/ppermute | solution.py:358
  31.9 14.0 %collective-permute-start = (s32[2]{0:T(128)S(1)}, s32[2]{0:T(128)S(1)}, u32[]{:S(2)}, u32[]{:S(2)}) collective-permute-start(s32[2]{0:T(128)S(1)} %get-tuple-element.22), channel_id=1, source_target_pairs={{0,496},{16,0},{32,16},{48,32},{64,48},{80,64},{96,80},{112,96},{1... | collective-permute-start | bytes 32 | tf_op jit(solution)/shard_map/ppermute | solution.py:358
  45.8 0.7 copy-start
  45.8 0.8 copy-start.2
  46.5 34.9 %all-to-all-start.1 = ((bf16[16,3,72,128]{3,2,1,0:T(8,128)(2,1)}), bf16[16,3,72,128]{3,2,1,0:T(8,128)(2,1)S(1)}, u32[]{:S(2)}, u32[]{:S(2)}) async-start(bf16[16,3,72,128]{3,2,1,0:T(8,128)(2,1)} %once_there.2), calls=%async_computation.1 | async-start | bytes 1769472 | tf_op jit(solution)/shard_map/all_to_all | solution.py:388
  53.8 11.9 %collective-permute-start.6 = (bf16[4,6,16,1152]{3,2,1,0:T(8,128)(2,1)S(1)}, bf16[4,6,16,1152]{3,2,1,0:T(8,128)(2,1)S(1)}, u32[]{:S(2)}, u32[]{:S(2)}) collective-permute-start(bf16[4,6,16,1152]{3,2,1,0:T(8,128)(2,1)S(1)} %swap_half.1.refs_2_), channel_id=1, source_target_pairs={{0,16},{16,0},{1,17},{17,1},{2,18},{18,2},{3,19},{19,3},{4,20},{20... | collective-permute-start | bytes 2654216 | tf_op jit(solution)/shard_map/ppermute | solution.py:358
  63.6 11.7 %collective-permute-start.8 = (bf16[16,72,128]{2,1,0:T(8,128)(2,1)}, bf16[16,72,128]{2,1,0:T(8,128)(2,1)}, u32[]{:S(2)}, u32[]{:S(2)}) collective-permute-start(bf16[16,72,128]{2,1,0:T(8,128)(2,1)} %spatial.2.refs_5_), channel_id=1, source_target_pairs={{0,0},{1,1},{2,2},{3,3},{4,36},{5,37},{6,38},{7,39},{8,72},{9,73},... | collective-permute-start | bytes 884744 | tf_op jit(solution)/shard_map/ppermute | solution.py:383
  65.7 0.9 copy-start.1
  66.6 0.9 copy-start.3
  69.7 6.3 %collective-permute-start.10 = (bf16[8,16,1152]{2,1,0:T(8,128)(2,1)S(1)}, bf16[8,16,1152]{2,1,0:T(8,128)(2,1)S(1)}, u32[]{:S(2)}, u32[]{:S(2)}) collective-permute-start(bf16[8,16,1152]{2,1,0:T(8,128)(2,1)S(1)} %get-tuple-element.28), channel_id=1, source_target_pairs={{0,16},{16,0},{1,17},{17,1},{2,18},{18,2},{3,19},{19,3},{4,20},{20... | collective-permute-start | bytes 884744 | tf_op jit(solution)/shard_map/ppermute | solution.py:358
  73.4 14.1 %collective-permute-start.7 = (bf16[16,72,128]{2,1,0:T(8,128)(2,1)}, bf16[16,72,128]{2,1,0:T(8,128)(2,1)S(1)}, u32[]{:S(2)}, u32[]{:S(2)}) collective-permute-start(bf16[16,72,128]{2,1,0:T(8,128)(2,1)} %spatial.2.refs_5_), channel_id=1, source_target_pairs={{16,0},{32,16},{48,32},{64,48},{80,64},{96,80},{112,96},{17,1},{33... | collective-permute-start | bytes 884744 | tf_op jit(solution)/shard_map/ppermute | solution.py:384
  75.3 12.2 %collective-permute-start.9 = (bf16[16,72,128]{2,1,0:T(8,128)(2,1)}, bf16[16,72,128]{2,1,0:T(8,128)(2,1)S(1)}, u32[]{:S(2)}, u32[]{:S(2)}) collective-permute-start(bf16[16,72,128]{2,1,0:T(8,128)(2,1)} %once_there.3), channel_id=1, source_target_pairs={{0,496},{1,497},{2,498},{3,499},{36,500},{37,501},{38,502},{39,503... | collective-permute-start | bytes 884744 | tf_op jit(solution)/shard_map/ppermute | solution.py:384
  76.0 11.3 %collective-permute-start.11 = (bf16[2,16,1152]{2,1,0:T(8,128)(2,1)S(1)}, bf16[2,16,1152]{2,1,0:T(8,128)(2,1)S(1)}, u32[]{:S(2)}, u32[]{:S(2)}) collective-permute-start(bf16[2,16,1152]{2,1,0:T(8,128)(2,1)S(1)} %edge.1), channel_id=1, source_target_pairs={{16,400},{48,432},{80,464},{112,496},{144,16},{176,48},{208,80},{2... | collective-permute-start | bytes 221192 | tf_op jit(solution)/shard_map/ppermute | solution.py:420
  87.4 23.7 %copy-start.4 = (f32[30,1152]{1,0:T(8,128)S(1)}, f32[30,1152]{1,0:T(8,128)}, u32[]{:S(2)}) copy-start(f32[30,1152]{1,0:T(8,128)} %refs_7_.1) | copy-start | bytes 414724
  87.4 23.7 %copy-start.5 = (f32[30,1152]{1,0:T(8,128)S(1)}, f32[30,1152]{1,0:T(8,128)}, u32[]{:S(2)}) copy-start(f32[30,1152]{1,0:T(8,128)} %refs_8_.1) | copy-start | bytes 414724
  87.4 23.7 %copy-start.10 = (f32[64]{0:T(128)S(1)}, f32[64]{0:T(128)}, u32[]{:S(2)}) copy-start(f32[64]{0:T(128)} %refs_9_.1) | copy-start | bytes 772
  88.4 22.7 %all-to-all-start.2 = ((bf16[16,2,72,128]{3,2,1,0:T(8,128)(2,1)}), bf16[16,2,72,128]{3,2,1,0:T(8,128)(2,1)S(1)}, u32[]{:S(2)}, u32[]{:S(2)}) async-start(bf16[16,2,72,128]{3,2,1,0:T(8,128)(2,1)} %beside.1), calls=%async_computation.2 | async-start | bytes 1179648 | tf_op jit(solution)/shard_map/all_to_all | solution.py:388
  96.0 7.2 %collective-permute-start.12 = (bf16[4,16,1152]{2,1,0:T(8,128)(2,1)S(1)}, bf16[4,16,1152]{2,1,0:T(8,128)(2,1)S(1)}, u32[]{:S(2)}, u32[]{:S(2)}) collective-permute-start(bf16[4,16,1152]{2,1,0:T(8,128)(2,1)S(1)} %get-tuple-element.30), channel_id=1, source_target_pairs={{0,96},{32,0},{64,32},{96,64},{1,97},{33,1},{65,33},{97,65},{2,98}... | collective-permute-start | bytes 442376 | tf_op jit(solution)/shard_map/ppermute | solution.py:358
  98.2 8.8 %collective-permute-start.13 = (bf16[4,16,1152]{2,1,0:T(8,128)(2,1)S(1)}, bf16[4,16,1152]{2,1,0:T(8,128)(2,1)S(1)}, u32[]{:S(2)}, u32[]{:S(2)}) collective-permute-start(bf16[4,16,1152]{2,1,0:T(8,128)(2,1)S(1)} %get-tuple-element.31), channel_id=1, source_target_pairs={{0,64},{32,96},{64,0},{96,32},{1,65},{33,97},{65,1},{97,33},{2,66}... | collective-permute-start | bytes 442376 | tf_op jit(solution)/shard_map/ppermute | solution.py:358
  100.1 10.5 %collective-permute-start.14 = (bf16[4,16,1152]{2,1,0:T(8,128)(2,1)S(1)}, bf16[4,16,1152]{2,1,0:T(8,128)(2,1)S(1)}, u32[]{:S(2)}, u32[]{:S(2)}) collective-permute-start(bf16[4,16,1152]{2,1,0:T(8,128)(2,1)S(1)} %get-tuple-element.32), channel_id=1, source_target_pairs={{0,32},{32,64},{64,96},{96,0},{1,33},{33,65},{65,97},{97,1},{2,34}... | collective-permute-start | bytes 442376 | tf_op jit(solution)/shard_map/ppermute | solution.py:358
